TPU v7x, 32 devices: a whole 2x2x4 slice. The times are simulated.
32 devices in a mesh: dp: 8 (over y, x, core), ctx: 4 (over z).
Axes of the slice: x: 2, y: 2, z: 4, core: 2. Of those that a mesh axis runs over, the one named last changes fastest.
Arguments:
- hidden_states: bfloat16 [768, 8192], P('ctx', 'dp'), may hold values from -160 to 160
- out_grads: bfloat16 [768, 8192], P('ctx', 'dp'), may hold values from -6 to 6
- norm_gain: bfloat16 [1, 8192], P(None, 'dp'), may hold values from 0.25 to 1.75
Outputs:
- a_factor: float32 [8192, 8192], P('ctx', 'dp')
- g_factor: float32 [8192, 8192], P('ctx', 'dp')
All inputs are finite; a program needn't handle non-finite values.
Results may differ from a plain program's by a relative error of at most 0.0028.
Values may be sent and summed in bfloat16 or wider, within the bound.
No kernel may reach another device: no remote copies, remote signals or barrier semaphores. Data moves between devices by JAX's collectives and lax.ppermute only.
A program may use at most 64 MiB of HBM per device.

v0:
```python
import jax
import jax.numpy as jnp
from jax import lax
from jax.sharding import PartitionSpec as P

D = 8192


EPS = 1e-05


def spread(block, axis, source):
    block = jnp.where(lax.axis_index(axis) == source, block, jnp.zeros_like(block))
    return lax.psum(block, axis)


def gram(left, right):
    return lax.dot_general(
        left, right, (((0,), (0,)), ((), ())), preferred_element_type=jnp.float32
    )


def body(hidden_states, out_grads, norm_gain):
    tokens_all = hidden_states.shape[0] * lax.axis_size("ctx")
    local = hidden_states.astype(jnp.float32)
    sums = lax.psum(jnp.sum(local * local, axis=1, keepdims=True), "dp")
    inv_rms = lax.rsqrt(sums / D + EPS)
    normed = (local * inv_rms * norm_gain.astype(jnp.float32)).astype(jnp.bfloat16)
    column_x, column_g = (
        lax.all_gather(normed, "ctx", axis=0, tiled=True),
        lax.all_gather(out_grads, "ctx", axis=0, tiled=True),
    )
    blocks_per_stripe = lax.axis_size("dp") // lax.axis_size("ctx")
    first_root = lax.axis_index("ctx") * blocks_per_stripe
    pieces_x = []
    pieces_g = []
    for offset in range(blocks_per_stripe):
        got_x, got_g = (
            spread(column_x, "dp", first_root + offset),
            spread(column_g, "dp", first_root + offset),
        )
        pieces_x.append(got_x)
        pieces_g.append(got_g)
    stripe_x = jnp.concatenate(pieces_x, axis=1)
    stripe_g = jnp.concatenate(pieces_g, axis=1)
    a_part = gram(stripe_x, column_x)
    g_part = gram(stripe_g, column_g)
    return (a_part / tokens_all, g_part / tokens_all)


def solution(mesh):
    return jax.shard_map(
        body,
        mesh=mesh,
        in_specs=(P("ctx", "dp"), P("ctx", "dp"), P(None, "dp")),
        out_specs=(P("ctx", "dp"), P("ctx", "dp")),
        check_vma=False,
    )
```

profile of v0, /device:TPU:0, one launch (start us, length us, event | category | flops | bytes accessed | tf_op | source)
XLA Modules:
  0.0 228.4 jit_solution(15920734401576343883)
XLA Ops:
  7.2 0.0 all-gather.3.cloned.1.call-start
  7.2 1.2 fusion.6
  8.4 15.1 %psum.35 = f32[192,1]{0,1:T(1,128)S(1)} all-reduce(f32[192,1]{0,1:T(1,128)S(1)} %bitcast.7), channel_id=1, replica_groups=mesh['dp'=8,'ctx'=4] {'dp'}, use_global_device_ids=true, to_apply=%region_1.0 | all-reduce | flops 192 | bytes 1536 | tf_op jit(solution)/shard_map/psum | solution.py:26
  23.5 0.7 mul.38
  24.2 1.9 fusion.8
  26.1 0.0 all-gather.3.cloned.1.call-update
  26.1 0.0 all-gather.5.cloned.1.call-start
  26.2 0.7 all-gather.5.cloned.1.call-update
  26.9 0.0 all-reduce.3.cloned.1.call-start
  26.9 35.8 %all-gather.3.cloned.1.call-done = bf16[768,1024]{1,0:T(8,128)(2,1)} async-done(((bf16[192,1024]{1,0:T(8,128)(2,1)}), bf16[768,1024]{1,0:T(8,128)(2,1)}) %all-gather.3.cloned.1.call-update) | async-done | bytes 1572880 | tf_op jit(solution)/shard_map/all_gather | solution.py:30
  62.7 3.3 %broadcast_select_fusion.3 = (bf16[768,1024]{1,0:T(8,128)(2,1)}, bf16[768,1024]{1,0:T(8,128)(2,1)}) fusion(bf16[768,1024]{1,0:T(8,128)(2,1)} %all-gather.3.cloned.1.call-done, pred[]{:T(512)S(6)} %eq.8, pred[]{:T(512)S(6)} %eq.9), kind=kLoop, calls=%fused_computation.11 | loop fusion | flops 1572864 | bytes 4718594 | tf_op jit(solution)/shard_map/jit(_where)/select_n | solution.py:13
  66.0 34.3 %all-gather.5.cloned.1.call-done = bf16[768,1024]{1,0:T(8,128)(2,1)} async-done(((bf16[192,1024]{1,0:T(8,128)(2,1)}), bf16[768,1024]{1,0:T(8,128)(2,1)}) %all-gather.5.cloned.1.call-update) | async-done | bytes 1572880 | tf_op jit(solution)/shard_map/all_gather | solution.py:31
  100.3 3.3 %broadcast_select_fusion.2 = (bf16[768,1024]{1,0:T(8,128)(2,1)}, bf16[768,1024]{1,0:T(8,128)(2,1)}) fusion(bf16[768,1024]{1,0:T(8,128)(2,1)} %all-gather.5.cloned.1.call-done, pred[]{:T(512)S(6)} %eq.8, pred[]{:T(512)S(6)} %eq.9), kind=kLoop, calls=%fused_computation.10 | loop fusion | flops 1572864 | bytes 4718594 | tf_op jit(solution)/shard_map/jit(_where)/select_n | solution.py:13
  103.5 0.0 copy-start
  103.5 0.0 all-reduce.3.cloned.1.call-update
  103.6 104.4 %all-reduce.3.cloned.1.call-done = (bf16[768,1024]{1,0:T(8,128)(2,1)}, bf16[768,1024]{1,0:T(8,128)(2,1)}, bf16[768,1024]{1,0:T(8,128)(2,1)}, bf16[768,1024]{1,0:T(8,128)(2,1)}) async-done(((bf16[768,1024]{1,0:T(8,128)(2,1)}, bf16[768,1024]{1,0:T(8,128)(2,1)}, bf16[768,1024]{1,0:T(8,128)(2,1)}, bf16[768,1024]{1,0:T(8,128)(2,1)}), (bf16[768,1024]{1,0:T(8,128)(2,1)}, bf16[768,1024]{1,0:T(8,128)(2,1)}, ...) | async-done | bytes 6291472 | tf_op jit(solution)/shard_map/psum | solution.py:14
  208.0 0.0 copy-done
  208.0 0.0 copy-start.1
  208.0 0.0 copy-start.2
  208.0 0.0 copy-start.3
  208.0 7.8 %convolution_multiply_fusion.1 = f32[2048,1024]{1,0:T(8,128)} fusion(bf16[768,1024]{1,0:T(8,128)(2,1)S(1)} %copy-done, bf16[768,1024]{1,0:T(8,128)(2,1)} %get-tuple-element.2, bf16[768,1024]{1,0:T(8,128)(2,1)} %get-tuple-element.3), kind=kOutput, calls=%fused_computation.1 | convolution fusion | flops 3229614080 | bytes 13107200 | tf_op jit(solution)/shard_map/dot_general | solution.py:18
  215.8 0.0 copy-done.1
  215.8 0.0 copy-done.2
  215.8 0.0 copy-done.3
  215.8 6.0 %convolution_multiply_fusion = f32[2048,1024]{1,0:T(8,128)} fusion(bf16[768,1024]{1,0:T(8,128)(2,1)S(1)} %copy-done.1, bf16[768,1024]{1,0:T(8,128)(2,1)S(1)} %copy-done.2, bf16[768,1024]{1,0:T(8,128)(2,1)S(1)} %copy-done.3), kind=kOutput, calls=%fused_computation | convolution fusion | flops 3229614080 | bytes 13107200 | tf_op jit(solution)/shard_map/dot_general | solution.py:18
  (1 shorter events, 0.0 us)
Async XLA Ops:
  7.2 55.6 %all-gather.3.cloned.1.call-start = ((), (), s32[]{:S(2)}) async-start(), calls=%async_computation | async-start | bytes 1966080 | tf_op jit(solution)/shard_map/all_gather | solution.py:30
  26.1 74.2 %all-gather.5.cloned.1.call-start = ((), (), s32[]{:S(2)}) async-start(), calls=%async_computation.1 | async-start | bytes 1966080 | tf_op jit(solution)/shard_map/all_gather | solution.py:31
  26.9 181.1 %all-reduce.3.cloned.1.call-start = ((), (), s32[]{:S(2)}) async-start(), calls=%async_computation.2 | async-start | bytes 12582912 | tf_op jit(solution)/shard_map/psum | solution.py:14
  103.5 104.5 %copy-start = (bf16[768,1024]{1,0:T(8,128)(2,1)S(1)}, bf16[768,1024]{1,0:T(8,128)(2,1)}, u32[]{:S(2)}) copy-start(bf16[768,1024]{1,0:T(8,128)(2,1)} %all-gather.3.cloned.1.call-done) | copy-start | bytes 4718596
  208.0 7.8 %copy-start.1 = (bf16[768,1024]{1,0:T(8,128)(2,1)S(1)}, bf16[768,1024]{1,0:T(8,128)(2,1)}, u32[]{:S(2)}) copy-start(bf16[768,1024]{1,0:T(8,128)(2,1)} %all-gather.5.cloned.1.call-done) | copy-start | bytes 4718596
  208.0 7.8 %copy-start.2 = (bf16[768,1024]{1,0:T(8,128)(2,1)S(1)}, bf16[768,1024]{1,0:T(8,128)(2,1)}, u32[]{:S(2)}) copy-start(bf16[768,1024]{1,0:T(8,128)(2,1)} %get-tuple-element.4) | copy-start | bytes 4718596
  208.0 7.8 %copy-start.3 = (bf16[768,1024]{1,0:T(8,128)(2,1)S(1)}, bf16[768,1024]{1,0:T(8,128)(2,1)}, u32[]{:S(2)}) copy-start(bf16[768,1024]{1,0:T(8,128)(2,1)} %get-tuple-element.5) | copy-start | bytes 4718596
Sparse Core Ops, SparseCore 0:
  26.2 36.4 all-gather.2
  64.3 35.9 all-gather.4
  104.4 103.5 all-reduce.2
where the time goes:
time: 229 us; the launch traced here: 228 us
  waiting for transfers between devices  175 us (76%)
  blocking collectives  15.1 us (7%)
  matrix products  13.8 us (6%)
  between operations  13.8 us (6%)
  other arithmetic  10.3 us (4%)
    psum x1, waiting for transfers between devices, spread(): return lax.psum(block, axis)  104 us
    all_gather x1, waiting for transfers between devices, body(): lax.all_gather(normed, 'ctx', axis=0, tiled=True)  35.8 us
    all_gather x1, waiting for transfers between devices, body(): lax.all_gather(out_grads, 'ctx', axis=0, tiled=True)  34.3 us
    psum x1, blocking collectives, body(): sums = lax.psum(jnp.sum(local * local, axis=1, keepdims=True), 'dp')  15.1 us
    dot_general x2, matrix products, gram(): lax.dot_general(left, right, (((0,), (0,)), ((), ())), preferred_element_...  13.8 us
    select_n x2, other arithmetic, spread(): jnp.where(lax.axis_index(axis) == source, block, jnp.zeros_like(block))  6.53 us
  transfers between devices with their start and end apart: 3, of which 3 were waited for; matrix products, arithmetic and copies ran while one was open for 1% of the time, Pallas kernels for 0%

commit v1 on v0

v1 whole, which is shorter than its diff:
```python
import jax
import jax.numpy as jnp
from jax import lax
from jax.sharding import PartitionSpec as P

EPS = 1e-05
AXES = ("dp", "ctx")


def spread(block, axis, source):
    block = jnp.where(lax.axis_index(axis) == source, block, jnp.zeros_like(block))
    return lax.psum(block, axis)


def gram(left, right):
    return lax.dot_general(
        left, right, (((0,), (0,)), ((), ())), preferred_element_type=jnp.float32
    )


def normalize(hidden_states, sums, norm_gain, features):
    inv_rms = lax.rsqrt(sums / features + EPS)
    return (
        hidden_states.astype(jnp.float32) * inv_rms * norm_gain.astype(jnp.float32)
    ).astype(jnp.bfloat16)


def squares(hidden_states):
    local = hidden_states.astype(jnp.float32)
    return jnp.sum(local * local, axis=1, keepdims=True)


def general(hidden_states, out_grads, norm_gain):
    tokens_all = hidden_states.shape[0] * lax.axis_size("ctx")
    features = hidden_states.shape[1] * lax.axis_size("dp")
    sums = lax.psum(squares(hidden_states), "dp")
    normed = normalize(hidden_states, sums, norm_gain, features)
    blocks_per_stripe = lax.axis_size("dp") // lax.axis_size("ctx")
    first_root = lax.axis_index("ctx") * blocks_per_stripe
    out = []
    for own in (normed, out_grads):
        column = lax.all_gather(own, "ctx", axis=0, tiled=True)
        stripe = jnp.concatenate(
            [spread(column, "dp", first_root + i) for i in range(blocks_per_stripe)],
            axis=1,
        )
        out.append(gram(stripe, column) / tokens_all)
    return tuple(out)


def swap(x, n_dp, n_ctx, partner):
    pairs = []
    for d in range(n_dp):
        for c in range(n_ctx):
            other = partner(d, c)
            if other is not None:
                pairs.append((d * n_ctx + c, other[0] * n_ctx + other[1]))
    return lax.ppermute(x, AXES, pairs)


def square_plane(hidden_states, out_grads, norm_gain):
    n_dp, n_ctx = lax.axis_size("dp"), lax.axis_size("ctx")
    tokens, width = hidden_states.shape
    dp, z = lax.axis_index("dp"), lax.axis_index("ctx")
    role = lax.bitwise_xor(dp // 2, z)
    parity = dp % 2

    def go(x, partner):
        return swap(x, n_dp, n_ctx, partner)

    def core(x):
        return go(x, lambda d, c: (d ^ 1, c))

    def along_x(x):
        return go(x, lambda d, c: (d ^ 2, c))

    def along_y(x):
        return go(x, lambda d, c: (d ^ 4, c))

    def across(x):
        return go(x, lambda d, c: (d ^ 6, c))

    def z1(x):
        return go(x, lambda d, c: (d, c ^ 1))

    def z2(x):
        return go(x, lambda d, c: (d, c ^ 2))

    def z_middle(x):
        return go(x, lambda d, c: (d, 3 - c) if c in (1, 2) else None)

    def gather_z(own):
        b = z2(own)
        a = z1(own)
        middle = z_middle(own)
        ends = z1(b)
        last = jnp.where((z == 1) | (z == 2), middle, ends)
        return [own, a, b, last]

    sums = squares(hidden_states)
    sums = sums + core(sums)
    sums = (sums + along_x(sums)) + (along_y(sums) + across(sums))
    normed = normalize(hidden_states, sums, norm_gain, width * n_dp)

    g = gather_z(out_grads)
    x = gather_z(normed)
    order = [g[0], x[0], g[1], g[2], g[3], x[1], x[2], x[3]]
    half = tokens // 2
    n = len(order)
    rx, ry = [], []
    for r in range(n + 1):
        source = order[min(r, n - 1)]
        low, high = source[:half], source[half:]
        if r == n:
            low, high = high, low
        px = low if r == 0 else jnp.where(role == 0, low, ry[r - 1])
        py = high if r == 0 else jnp.where(role == 0, high, rx[r - 1])
        rx.append(along_x(px))
        ry.append(along_y(py))
    stripes = []
    for c in range(n):
        low, high = order[c][:half], order[c][half:]
        if c < n - 1:
            got_low = lax.select_n(role, low, rx[c], rx[c + 2], ry[c + 1])
            got_high = lax.select_n(role, high, ry[c + 2], ry[c], rx[c + 1])
        else:
            got_low = lax.select_n(role, low, rx[c], ry[c + 1], ry[c + 1])
            got_high = lax.select_n(role, high, rx[c + 1], ry[c], rx[c + 1])
        stripes += [got_low, got_high]

    def factor(picks, chunks):
        mine = jnp.concatenate([s for p in picks for s in stripes[2 * p : 2 * p + 2]], axis=0)
        other = core(mine)
        first = jnp.where(parity == 0, mine, other)
        second = jnp.where(parity == 0, other, mine)
        stripe = jnp.concatenate([first, second], axis=1)
        return gram(stripe, jnp.concatenate(chunks, axis=0)) / (tokens * n_ctx)

    g_factor = factor([0, 2, 3, 4], g)
    a_factor = factor([1, 5, 6, 7], x)
    return a_factor, g_factor


def solution(mesh):
    square = mesh.shape["dp"] == 8 and mesh.shape["ctx"] == 4
    return jax.shard_map(
        square_plane if square else general,
        mesh=mesh,
        in_specs=(P("ctx", "dp"), P("ctx", "dp"), P(None, "dp")),
        out_specs=(P("ctx", "dp"), P("ctx", "dp")),
        check_vma=False,
    )
```

time: 229 us -> 131 us (0.57)
  waiting for transfers between devices: 175 us -> 68.2 us
  starting transfers between devices: 0.12 us -> 32.6 us
  blocking collectives: 15.1 us -> 0 us
  between operations: 13.8 us -> 0.9 us
  other arithmetic: 10.3 us -> 16.1 us
    psum x1 -> x0, waiting for transfers between devices: 104 us -> none  [spread(): return lax.psum(block, axis)]
    all_gather x2 -> x0, waiting for transfers between devices: 70.1 us -> none  [the longest x1 35.8 us: body(): lax.all_gather(normed, 'ctx', axis=0, tiled=True)]
    ppermute x0 -> x32, waiting for transfers between devices: none -> 68.2 us  [swap(): return lax.ppermute(x, AXES, pairs)]
    ppermute x0 -> x32, starting transfers between devices: none -> 32.6 us  [swap(): return lax.ppermute(x, AXES, pairs)]
    psum x1 -> x0, blocking collectives: 15.1 us -> none  [body(): sums = lax.psum(jnp.sum(local * local, axis=1, keepdims=True), 'dp')]
    unnamed x0 -> x6, other arithmetic: none -> 2.87 us
    select_n x2 -> x15, other arithmetic: 6.53 us -> 9.14 us  [the longest x5 4.01 us: square_plane(): py = high if r == 0 else jnp.where(role == 0, high, rx[r - 1])]
  transfers between devices with their start and end apart: 3 -> 32, of which waited for: 3 -> 18; matrix products, arithmetic and copies ran while one was open for 1% -> 14% of each run, Pallas kernels for 0% -> 0%
where the time goes in v1:
time: 131 us; the launch traced here: 130 us
  waiting for transfers between devices  68.2 us (52%)
  starting transfers between devices  32.6 us (25%)
  other arithmetic  16.1 us (12%)
  matrix products  11.7 us (9%)
    ppermute x32, waiting for transfers between devices, swap(): return lax.ppermute(x, AXES, pairs)  68.2 us
    ppermute x32, starting transfers between devices, swap(): return lax.ppermute(x, AXES, pairs)  32.6 us
    dot_general x2, matrix products, gram(): lax.dot_general(left, right, (((0,), (0,)), ((), ())), preferred_element_...  11.7 us
    select_n x5, other arithmetic, square_plane(): py = high if r == 0 else jnp.where(role == 0, high, rx[r - 1])  4.01 us
    select_n x2, other arithmetic, factor(): first = jnp.where(parity == 0, mine, other)  3.84 us
    unnamed x6, other arithmetic  2.87 us
  transfers between devices with their start and end apart: 32, of which 18 were waited for; matrix products, arithmetic and copies ran while one was open for 14% of the time, Pallas kernels for 0%

profile of v1, /device:TPU:0, one launch (start us, length us, event | category | flops | bytes accessed | tf_op | source)
XLA Modules:
  0.0 130.4 jit_solution(1105236325503282948)
XLA Ops:
  2.4 2.6 %collective-permute-start.7 = (bf16[192,1024]{1,0:T(8,128)(2,1)}, bf16[192,1024]{1,0:T(8,128)(2,1)S(1)}, u32[]{:S(2)}, u32[]{:S(2)}) collective-permute-start(bf16[192,1024]{1,0:T(8,128)(2,1)} %param.4), channel_id=1, source_target_pairs={{0,1},{1,0},{2,3},{3,2},{4,5},{5,4},{6,7},{7,6},{8,9},{9,8},{10,11... | collective-permute-start | bytes 1179656 | tf_op jit(solution)/shard_map/ppermute | solution.py:58
  6.0 1.6 %collective-permute-start.10 = (bf16[96,1024]{1,0:T(8,128)(2,1)S(1)}, bf16[96,1024]{1,0:T(8,128)(2,1)S(1)}, u32[]{:S(2)}, u32[]{:S(2)}) collective-permute-start(bf16[96,1024]{1,0:T(8,128)(2,1)S(1)} %slice.73), channel_id=1, source_target_pairs={{0,8},{1,9},{2,10},{3,11},{4,12},{5,13},{6,14},{7,15},{8,0},{9,1},... | collective-permute-start | bytes 589832 | tf_op jit(solution)/shard_map/ppermute | solution.py:58
  7.5 1.5 %collective-permute-start.3 = (f32[192,1]{0,1:T(1,128)S(1)}, f32[192,1]{0,1:T(1,128)S(1)}, u32[]{:S(2)}, u32[]{:S(2)}) collective-permute-start(f32[192,1]{0,1:T(1,128)S(1)} %add.24), channel_id=1, source_target_pairs={{0,24},{1,25},{2,26},{3,27},{4,28},{5,29},{6,30},{7,31},{8,16},{9,... | collective-permute-start | bytes 2312 | tf_op jit(solution)/shard_map/ppermute | solution.py:58
  9.5 1.5 %collective-permute-start.1 = (f32[192,1]{0,1:T(1,128)S(1)}, f32[192,1]{0,1:T(1,128)S(1)}, u32[]{:S(2)}, u32[]{:S(2)}) collective-permute-start(f32[192,1]{0,1:T(1,128)S(1)} %add.24), channel_id=1, source_target_pairs={{0,8},{1,9},{2,10},{3,11},{4,12},{5,13},{6,14},{7,15},{8,0},{9,1},... | collective-permute-start | bytes 2312 | tf_op jit(solution)/shard_map/ppermute | solution.py:58
  11.7 2.3 %collective-permute-done.3 = f32[192,1]{0,1:T(1,128)S(1)} collective-permute-done((f32[192,1]{0,1:T(1,128)S(1)}, f32[192,1]{0,1:T(1,128)S(1)}, u32[]{:S(2)}, u32[]{:S(2)}) %collective-permute-start.3) | collective-permute-done | bytes 800 | tf_op jit(solution)/shard_map/ppermute | solution.py:58
  15.9 5.2 %collective-permute-done.11 = bf16[96,1024]{1,0:T(8,128)(2,1)S(1)} collective-permute-done((bf16[96,1024]{1,0:T(8,128)(2,1)S(1)}, bf16[96,1024]{1,0:T(8,128)(2,1)S(1)}, u32[]{:S(2)}, u32[]{:S(2)}) %collective-permute-start.11) | collective-permute-done | bytes 196640 | tf_op jit(solution)/shard_map/ppermute | solution.py:58
  21.2 1.6 %collective-permute-start.12 = (bf16[96,1024]{1,0:T(8,128)(2,1)S(1)}, bf16[96,1024]{1,0:T(8,128)(2,1)S(1)}, u32[]{:S(2)}, u32[]{:S(2)}) collective-permute-start(bf16[96,1024]{1,0:T(8,128)(2,1)S(1)} %broadcast_select_fusion.17), channel_id=1, source_target_pairs={{0,8},{1,9},{2,10},{3,11},{4,12},{5,13},{6,14},{7,15},{8,0},{9,1},... | collective-permute-start | bytes 589832 | tf_op jit(solution)/shard_map/ppermute | solution.py:58
  22.7 4.2 %collective-permute-done.12 = bf16[96,1024]{1,0:T(8,128)(2,1)S(1)} collective-permute-done((bf16[96,1024]{1,0:T(8,128)(2,1)S(1)}, bf16[96,1024]{1,0:T(8,128)(2,1)S(1)}, u32[]{:S(2)}, u32[]{:S(2)}) %collective-permute-start.12) | collective-permute-done | bytes 196640 | tf_op jit(solution)/shard_map/ppermute | solution.py:58
  28.6 4.8 %collective-permute-done.4 = bf16[96,1024]{1,0:T(8,128)(2,1)S(1)} collective-permute-done((bf16[96,1024]{1,0:T(8,128)(2,1)S(1)}, bf16[96,1024]{1,0:T(8,128)(2,1)S(1)}, u32[]{:S(2)}, u32[]{:S(2)}) %collective-permute-start.4) | collective-permute-done | bytes 196640 | tf_op jit(solution)/shard_map/ppermute | solution.py:58
  33.4 1.6 %collective-permute-start.5 = (bf16[96,1024]{1,0:T(8,128)(2,1)S(1)}, bf16[96,1024]{1,0:T(8,128)(2,1)S(1)}, u32[]{:S(2)}, u32[]{:S(2)}) collective-permute-start(bf16[96,1024]{1,0:T(8,128)(2,1)S(1)} %broadcast_select_fusion.21), channel_id=1, source_target_pairs={{0,8},{1,9},{2,10},{3,11},{4,12},{5,13},{6,14},{7,15},{8,0},{9,1},... | collective-permute-start | bytes 589832 | tf_op jit(solution)/shard_map/ppermute | solution.py:58
  35.0 2.6 %collective-permute-start.6 = (bf16[192,1024]{1,0:T(8,128)(2,1)S(1)}, bf16[192,1024]{1,0:T(8,128)(2,1)S(1)}, u32[]{:S(2)}, u32[]{:S(2)}) collective-permute-start(bf16[192,1024]{1,0:T(8,128)(2,1)S(1)} %copy-done), channel_id=1, source_target_pairs={{0,2},{1,3},{2,0},{3,1},{4,6},{5,7},{6,4},{7,5},{8,10},{9,11},{10,... | collective-permute-start | bytes 1179656 | tf_op jit(solution)/shard_map/ppermute | solution.py:58
  37.6 1.6 %collective-permute-done.5 = bf16[96,1024]{1,0:T(8,128)(2,1)S(1)} collective-permute-done((bf16[96,1024]{1,0:T(8,128)(2,1)S(1)}, bf16[96,1024]{1,0:T(8,128)(2,1)S(1)}, u32[]{:S(2)}, u32[]{:S(2)}) %collective-permute-start.5) | collective-permute-done | bytes 196640 | tf_op jit(solution)/shard_map/ppermute | solution.py:58
  40.8 11.3 %collective-permute-done.6 = bf16[192,1024]{1,0:T(8,128)(2,1)S(1)} collective-permute-done((bf16[192,1024]{1,0:T(8,128)(2,1)S(1)}, bf16[192,1024]{1,0:T(8,128)(2,1)S(1)}, u32[]{:S(2)}, u32[]{:S(2)}) %collective-permute-start.6) | collective-permute-done | bytes 393248 | tf_op jit(solution)/shard_map/ppermute | solution.py:58
  54.5 6.5 %collective-permute-done.16 = bf16[192,1024]{1,0:T(8,128)(2,1)S(1)} collective-permute-done((bf16[192,1024]{1,0:T(8,128)(2,1)S(1)}, bf16[192,1024]{1,0:T(8,128)(2,1)S(1)}, u32[]{:S(2)}, u32[]{:S(2)}) %collective-permute-start.16) | collective-permute-done | bytes 393248 | tf_op jit(solution)/shard_map/ppermute | solution.py:58
  61.2 1.4 %collective-permute-start.14 = (bf16[192,1024]{1,0:T(8,128)(2,1)S(1)}, bf16[192,1024]{1,0:T(8,128)(2,1)S(1)}, u32[]{:S(2)}, u32[]{:S(2)}) collective-permute-start(bf16[192,1024]{1,0:T(8,128)(2,1)S(1)} %fusion.22), channel_id=1, source_target_pairs={{0,1},{1,0},{2,3},{3,2},{4,5},{5,4},{6,7},{7,6},{8,9},{9,8},{10,11... | collective-permute-start | bytes 1179656 | tf_op jit(solution)/shard_map/ppermute | solution.py:58
  62.6 1.8 %collective-permute-start.20 = (bf16[192,1024]{1,0:T(8,128)(2,1)S(1)}, bf16[192,1024]{1,0:T(8,128)(2,1)S(1)}, u32[]{:S(2)}, u32[]{:S(2)}) collective-permute-start(bf16[192,1024]{1,0:T(8,128)(2,1)S(1)} %fusion.22), channel_id=1, source_target_pairs={{0,2},{1,3},{2,0},{3,1},{4,6},{5,7},{6,4},{7,5},{8,10},{9,11},{10,... | collective-permute-start | bytes 1179656 | tf_op jit(solution)/shard_map/ppermute | solution.py:58
  67.6 9.7 %collective-permute-done.14 = bf16[192,1024]{1,0:T(8,128)(2,1)S(1)} collective-permute-done((bf16[192,1024]{1,0:T(8,128)(2,1)S(1)}, bf16[192,1024]{1,0:T(8,128)(2,1)S(1)}, u32[]{:S(2)}, u32[]{:S(2)}) %collective-permute-start.14) | collective-permute-done | bytes 393248 | tf_op jit(solution)/shard_map/ppermute | solution.py:58
  77.3 2.1 %broadcast_select_fusion.10 = (bf16[96,1024]{1,0:T(8,128)(2,1)S(1)}, bf16[96,1024]{1,0:T(8,128)(2,1)S(1)}, bf16[768,1024]{1,0:T(8,128)(2,1)S(1)}, bf16[768,1024]{1,0:T(8,128)(2,1)}) fusion(bf16[96,1024]{1,0:T(8,128)(2,1)S(1)} %collective-permute-done.24, pred[]{:T(512)S(6)} %eq.11, bf16[192,1024]{1,0:T(8,128)(2,1)S(1)} %collective-permute-done.14, ...), kind=kLoop, calls=%fused_computation.53 | loop fusion | flops 786431 | bytes 2555908 | tf_op jit(solution)/shard_map/jit(_where)/select_n | solution.py:117
  79.4 1.3 collective-permute-start.25
  80.7 1.4 %collective-permute-start.18 = (bf16[96,1024]{1,0:T(8,128)(2,1)S(1)}, bf16[96,1024]{1,0:T(8,128)(2,1)S(1)}, u32[]{:S(2)}, u32[]{:S(2)}) collective-permute-start(bf16[96,1024]{1,0:T(8,128)(2,1)S(1)} %get-tuple-element.17), channel_id=1, source_target_pairs={{0,8},{1,9},{2,10},{3,11},{4,12},{5,13},{6,14},{7,15},{8,0},{9,1},... | collective-permute-start | bytes 589832 | tf_op jit(solution)/shard_map/ppermute | solution.py:58
  85.1 1.3 collective-permute-done.18
  88.1 3.6 %collective-permute-done.21 = bf16[192,1024]{1,0:T(8,128)(2,1)S(1)} collective-permute-done((bf16[192,1024]{1,0:T(8,128)(2,1)S(1)}, bf16[192,1024]{1,0:T(8,128)(2,1)S(1)}, u32[]{:S(2)}, u32[]{:S(2)}) %collective-permute-start.21) | collective-permute-done | bytes 393248 | tf_op jit(solution)/shard_map/ppermute | solution.py:58
  93.0 1.5 %collective-permute-start.23 = (bf16[96,1024]{1,0:T(8,128)(2,1)S(1)}, bf16[96,1024]{1,0:T(8,128)(2,1)S(1)}, u32[]{:S(2)}, u32[]{:S(2)}) collective-permute-start(bf16[96,1024]{1,0:T(8,128)(2,1)S(1)} %broadcast_select_fusion.12), channel_id=1, source_target_pairs={{0,8},{1,9},{2,10},{3,11},{4,12},{5,13},{6,14},{7,15},{8,0},{9,1},... | collective-permute-start | bytes 589832 | tf_op jit(solution)/shard_map/ppermute | solution.py:58
  95.4 2.0 %collective-permute-done.26 = bf16[96,1024]{1,0:T(8,128)(2,1)S(1)} collective-permute-done((bf16[96,1024]{1,0:T(8,128)(2,1)S(1)}, bf16[96,1024]{1,0:T(8,128)(2,1)S(1)}, u32[]{:S(2)}, u32[]{:S(2)}) %collective-permute-start.26) | collective-permute-done | bytes 196640 | tf_op jit(solution)/shard_map/ppermute | solution.py:58
  97.5 2.1 %collective-permute-done.23 = bf16[96,1024]{1,0:T(8,128)(2,1)S(1)} collective-permute-done((bf16[96,1024]{1,0:T(8,128)(2,1)S(1)}, bf16[96,1024]{1,0:T(8,128)(2,1)S(1)}, u32[]{:S(2)}, u32[]{:S(2)}) %collective-permute-start.23) | collective-permute-done | bytes 196640 | tf_op jit(solution)/shard_map/ppermute | solution.py:58
  101.8 4.4 %collective-permute-done.27 = bf16[96,1024]{1,0:T(8,128)(2,1)S(1)} collective-permute-done((bf16[96,1024]{1,0:T(8,128)(2,1)S(1)}, bf16[96,1024]{1,0:T(8,128)(2,1)S(1)}, u32[]{:S(2)}, u32[]{:S(2)}) %collective-permute-start.27) | collective-permute-done | bytes 196640 | tf_op jit(solution)/shard_map/ppermute | solution.py:58
  107.9 4.1 %collective-permute-done.28 = bf16[96,1024]{1,0:T(8,128)(2,1)S(1)} collective-permute-done((bf16[96,1024]{1,0:T(8,128)(2,1)S(1)}, bf16[96,1024]{1,0:T(8,128)(2,1)S(1)}, u32[]{:S(2)}, u32[]{:S(2)}) %collective-permute-start.28) | collective-permute-done | bytes 196640 | tf_op jit(solution)/shard_map/ppermute | solution.py:58
  112.2 2.2 %collective-permute-done.29 = bf16[96,1024]{1,0:T(8,128)(2,1)S(1)} collective-permute-done((bf16[96,1024]{1,0:T(8,128)(2,1)S(1)}, bf16[96,1024]{1,0:T(8,128)(2,1)S(1)}, u32[]{:S(2)}, u32[]{:S(2)}) %collective-permute-start.29) | collective-permute-done | bytes 196640 | tf_op jit(solution)/shard_map/ppermute | solution.py:58
  114.9 2.2 %broadcast_select_fusion.1 = (bf16[768,1024]{1,0:T(8,128)(2,1)S(1)}, bf16[768,1024]{1,0:T(8,128)(2,1)S(1)}) fusion(bf16[768,1024]{1,0:T(8,128)(2,1)} %get-tuple-element.6, bf16[768,1024]{1,0:T(8,128)(2,1)} %collective-permute-done.31, pred[]{:T(512)S(6)} %eq.10), kind=kLoop, calls=%fused_computation.23 | loop fusion | flops 1572864 | bytes 6291457 | tf_op jit(solution)/shard_map/jit(_where)/select_n | solution.py:134
  117.0 5.8 %convolution_multiply_fusion = f32[2048,1024]{1,0:T(8,128)} fusion(bf16[768,1024]{1,0:T(8,128)(2,1)S(1)} %get-tuple-element.3, bf16[768,1024]{1,0:T(8,128)(2,1)S(1)} %get-tuple-element.2, bf16[192,1024]{1,0:T(8,128)(2,1)S(1)} %broadcast_select_fusion.5, bf16[192,1024]{1,0:T(8,128)(2,1)S(1)} %copy-done.3, bf16[192,1024]{1,0:T(8,128)(2,1)S(1)} %copy-done.5, ...), kind=kOutput, calls=%fused_computation | convolution fusion | flops 3235905536 | bytes 13107200 | tf_op jit(solution)/shard_map/dot_general | solution.py:16
  122.9 1.7 %broadcast_select_fusion.3 = (bf16[768,1024]{1,0:T(8,128)(2,1)S(1)}, bf16[768,1024]{1,0:T(8,128)(2,1)S(1)}) fusion(bf16[768,1024]{1,0:T(8,128)(2,1)S(1)} %select_dynamic-update-slice_fusion.8, bf16[768,1024]{1,0:T(8,128)(2,1)} %collective-permute-done.30, pred[]{:T(512)S(6)} %eq.10), kind=kLoop, calls=%fused_computation.25 | loop fusion | flops 1572864 | bytes 6291457 | tf_op jit(solution)/shard_map/jit(_where)/select_n | solution.py:134
  124.6 5.8 %convolution_multiply_fusion.1 = f32[2048,1024]{1,0:T(8,128)} fusion(bf16[768,1024]{1,0:T(8,128)(2,1)S(1)} %get-tuple-element.5, bf16[768,1024]{1,0:T(8,128)(2,1)S(1)} %get-tuple-element.4, bf16[192,1024]{1,0:T(8,128)(2,1)S(1)} %broadcast_select_fusion.4, bf16[192,1024]{1,0:T(8,128)(2,1)S(1)} %copy-done.7, bf16[192,1024]{1,0:T(8,128)(2,1)S(1)} %copy-done.9, ...), kind=kOutput, calls=%fused_computation.1 | convolution fusion | flops 3235905536 | bytes 13107200 | tf_op jit(solution)/shard_map/dot_general | solution.py:16
  (83 shorter events, 26.3 us)
Async XLA Ops:
  1.8 5.7 %collective-permute-start = (f32[192,1]{0,1:T(1,128)S(1)}, f32[192,1]{0,1:T(1,128)S(1)}, u32[]{:S(2)}, u32[]{:S(2)}) collective-permute-start(f32[192,1]{0,1:T(1,128)S(1)} %bitcast.4), channel_id=1, source_target_pairs={{0,4},{1,5},{2,6},{3,7},{4,0},{5,1},{6,2},{7,3},{8,12},{9,13},{10,... | collective-permute-start | bytes 2312 | tf_op jit(solution)/shard_map/ppermute | solution.py:58
  2.4 18.8 %collective-permute-start.7 = (bf16[192,1024]{1,0:T(8,128)(2,1)}, bf16[192,1024]{1,0:T(8,128)(2,1)S(1)}, u32[]{:S(2)}, u32[]{:S(2)}) collective-permute-start(bf16[192,1024]{1,0:T(8,128)(2,1)} %param.4), channel_id=1, source_target_pairs={{0,1},{1,0},{2,3},{3,2},{4,5},{5,4},{6,7},{7,6},{8,9},{9,8},{10,11... | collective-permute-start | bytes 1179656 | tf_op jit(solution)/shard_map/ppermute | solution.py:58
  6.0 9.2 %collective-permute-start.10 = (bf16[96,1024]{1,0:T(8,128)(2,1)S(1)}, bf16[96,1024]{1,0:T(8,128)(2,1)S(1)}, u32[]{:S(2)}, u32[]{:S(2)}) collective-permute-start(bf16[96,1024]{1,0:T(8,128)(2,1)S(1)} %slice.73), channel_id=1, source_target_pairs={{0,8},{1,9},{2,10},{3,11},{4,12},{5,13},{6,14},{7,15},{8,0},{9,1},... | collective-permute-start | bytes 589832 | tf_op jit(solution)/shard_map/ppermute | solution.py:58
  7.5 6.5 %collective-permute-start.3 = (f32[192,1]{0,1:T(1,128)S(1)}, f32[192,1]{0,1:T(1,128)S(1)}, u32[]{:S(2)}, u32[]{:S(2)}) collective-permute-start(f32[192,1]{0,1:T(1,128)S(1)} %add.24), channel_id=1, source_target_pairs={{0,24},{1,25},{2,26},{3,27},{4,28},{5,29},{6,30},{7,31},{8,16},{9,... | collective-permute-start | bytes 2312 | tf_op jit(solution)/shard_map/ppermute | solution.py:58
  9.0 5.0 %collective-permute-start.2 = (f32[192,1]{0,1:T(1,128)S(1)}, f32[192,1]{0,1:T(1,128)S(1)}, u32[]{:S(2)}, u32[]{:S(2)}) collective-permute-start(f32[192,1]{0,1:T(1,128)S(1)} %add.24), channel_id=1, source_target_pairs={{0,16},{1,17},{2,18},{3,19},{4,20},{5,21},{6,22},{7,23},{8,24},{9,... | collective-permute-start | bytes 2312 | tf_op jit(solution)/shard_map/ppermute | solution.py:58
  9.5 4.5 %collective-permute-start.1 = (f32[192,1]{0,1:T(1,128)S(1)}, f32[192,1]{0,1:T(1,128)S(1)}, u32[]{:S(2)}, u32[]{:S(2)}) collective-permute-start(f32[192,1]{0,1:T(1,128)S(1)} %add.24), channel_id=1, source_target_pairs={{0,8},{1,9},{2,10},{3,11},{4,12},{5,13},{6,14},{7,15},{8,0},{9,1},... | collective-permute-start | bytes 2312 | tf_op jit(solution)/shard_map/ppermute | solution.py:58
  15.2 5.9 %collective-permute-start.11 = (bf16[96,1024]{1,0:T(8,128)(2,1)S(1)}, bf16[96,1024]{1,0:T(8,128)(2,1)S(1)}, u32[]{:S(2)}, u32[]{:S(2)}) collective-permute-start(bf16[96,1024]{1,0:T(8,128)(2,1)S(1)} %broadcast_select_fusion.18), channel_id=1, source_target_pairs={{0,16},{1,17},{2,18},{3,19},{4,20},{5,21},{6,22},{7,23},{8,24},{9,... | collective-permute-start | bytes 589832 | tf_op jit(solution)/shard_map/ppermute | solution.py:58
  21.2 5.7 %collective-permute-start.12 = (bf16[96,1024]{1,0:T(8,128)(2,1)S(1)}, bf16[96,1024]{1,0:T(8,128)(2,1)S(1)}, u32[]{:S(2)}, u32[]{:S(2)}) collective-permute-start(bf16[96,1024]{1,0:T(8,128)(2,1)S(1)} %broadcast_select_fusion.17), channel_id=1, source_target_pairs={{0,8},{1,9},{2,10},{3,11},{4,12},{5,13},{6,14},{7,15},{8,0},{9,1},... | collective-permute-start | bytes 589832 | tf_op jit(solution)/shard_map/ppermute | solution.py:58
  27.7 5.7 %collective-permute-start.4 = (bf16[96,1024]{1,0:T(8,128)(2,1)S(1)}, bf16[96,1024]{1,0:T(8,128)(2,1)S(1)}, u32[]{:S(2)}, u32[]{:S(2)}) collective-permute-start(bf16[96,1024]{1,0:T(8,128)(2,1)S(1)} %get-tuple-element.11), channel_id=1, source_target_pairs={{0,16},{1,17},{2,18},{3,19},{4,20},{5,21},{6,22},{7,23},{8,24},{9,... | collective-permute-start | bytes 589832 | tf_op jit(solution)/shard_map/ppermute | solution.py:58
  33.4 5.7 %collective-permute-start.5 = (bf16[96,1024]{1,0:T(8,128)(2,1)S(1)}, bf16[96,1024]{1,0:T(8,128)(2,1)S(1)}, u32[]{:S(2)}, u32[]{:S(2)}) collective-permute-start(bf16[96,1024]{1,0:T(8,128)(2,1)S(1)} %broadcast_select_fusion.21), channel_id=1, source_target_pairs={{0,8},{1,9},{2,10},{3,11},{4,12},{5,13},{6,14},{7,15},{8,0},{9,1},... | collective-permute-start | bytes 589832 | tf_op jit(solution)/shard_map/ppermute | solution.py:58
  35.0 17.1 %collective-permute-start.6 = (bf16[192,1024]{1,0:T(8,128)(2,1)S(1)}, bf16[192,1024]{1,0:T(8,128)(2,1)S(1)}, u32[]{:S(2)}, u32[]{:S(2)}) collective-permute-start(bf16[192,1024]{1,0:T(8,128)(2,1)S(1)} %copy-done), channel_id=1, source_target_pairs={{0,2},{1,3},{2,0},{3,1},{4,6},{5,7},{6,4},{7,5},{8,10},{9,11},{10,... | collective-permute-start | bytes 1179656 | tf_op jit(solution)/shard_map/ppermute | solution.py:58
  39.2 13.0 %collective-permute-start.8 = (bf16[96,1024]{1,0:T(8,128)(2,1)S(1)}, bf16[96,1024]{1,0:T(8,128)(2,1)S(1)}, u32[]{:S(2)}, u32[]{:S(2)}) collective-permute-start(bf16[96,1024]{1,0:T(8,128)(2,1)S(1)} %broadcast_select_fusion.20), channel_id=1, source_target_pairs={{0,16},{1,17},{2,18},{3,19},{4,20},{5,21},{6,22},{7,23},{8,24},{9,... | collective-permute-start | bytes 589832 | tf_op jit(solution)/shard_map/ppermute | solution.py:58
  40.1 14.4 %collective-permute-start.15 = (bf16[192,1024]{1,0:T(8,128)(2,1)S(1)}, bf16[192,1024]{1,0:T(8,128)(2,1)S(1)}, u32[]{:S(2)}, u32[]{:S(2)}) collective-permute-start(bf16[192,1024]{1,0:T(8,128)(2,1)S(1)} %copy-done), channel_id=1, source_target_pairs={{1,2},{2,1},{5,6},{6,5},{9,10},{10,9},{13,14},{14,13},{17,18},{18,... | collective-permute-start | bytes 1179656 | tf_op jit(solution)/shard_map/ppermute | solution.py:58
  52.1 8.8 %collective-permute-start.16 = (bf16[192,1024]{1,0:T(8,128)(2,1)S(1)}, bf16[192,1024]{1,0:T(8,128)(2,1)S(1)}, u32[]{:S(2)}, u32[]{:S(2)}) collective-permute-start(bf16[192,1024]{1,0:T(8,128)(2,1)S(1)} %collective-permute-done.6), channel_id=1, source_target_pairs={{0,1},{1,0},{2,3},{3,2},{4,5},{5,4},{6,7},{7,6},{8,9},{9,8},{10,11... | collective-permute-start | bytes 1179656 | tf_op jit(solution)/shard_map/ppermute | solution.py:58
  53.1 7.9 %collective-permute-start.13 = (bf16[96,1024]{1,0:T(8,128)(2,1)S(1)}, bf16[96,1024]{1,0:T(8,128)(2,1)S(1)}, u32[]{:S(2)}, u32[]{:S(2)}) collective-permute-start(bf16[96,1024]{1,0:T(8,128)(2,1)S(1)} %get-tuple-element.20), channel_id=1, source_target_pairs={{0,16},{1,17},{2,18},{3,19},{4,20},{5,21},{6,22},{7,23},{8,24},{9,... | collective-permute-start | bytes 589832 | tf_op jit(solution)/shard_map/ppermute | solution.py:58
  54.0 7.1 %collective-permute-start.9 = (bf16[96,1024]{1,0:T(8,128)(2,1)S(1)}, bf16[96,1024]{1,0:T(8,128)(2,1)S(1)}, u32[]{:S(2)}, u32[]{:S(2)}) collective-permute-start(bf16[96,1024]{1,0:T(8,128)(2,1)S(1)} %get-tuple-element.21), channel_id=1, source_target_pairs={{0,8},{1,9},{2,10},{3,11},{4,12},{5,13},{6,14},{7,15},{8,0},{9,1},... | collective-permute-start | bytes 589832 | tf_op jit(solution)/shard_map/ppermute | solution.py:58
  61.1 5.7 %collective-permute-start.24 = (bf16[96,1024]{1,0:T(8,128)(2,1)S(1)}, bf16[96,1024]{1,0:T(8,128)(2,1)S(1)}, u32[]{:S(2)}, u32[]{:S(2)}) collective-permute-start(bf16[96,1024]{1,0:T(8,128)(2,1)S(1)} %get-tuple-element.18), channel_id=1, source_target_pairs={{0,8},{1,9},{2,10},{3,11},{4,12},{5,13},{6,14},{7,15},{8,0},{9,1},... | collective-permute-start | bytes 589832 | tf_op jit(solution)/shard_map/ppermute | solution.py:58
  61.2 16.1 %collective-permute-start.14 = (bf16[192,1024]{1,0:T(8,128)(2,1)S(1)}, bf16[192,1024]{1,0:T(8,128)(2,1)S(1)}, u32[]{:S(2)}, u32[]{:S(2)}) collective-permute-start(bf16[192,1024]{1,0:T(8,128)(2,1)S(1)} %fusion.22), channel_id=1, source_target_pairs={{0,1},{1,0},{2,3},{3,2},{4,5},{5,4},{6,7},{7,6},{8,9},{9,8},{10,11... | collective-permute-start | bytes 1179656 | tf_op jit(solution)/shard_map/ppermute | solution.py:58
  62.6 20.2 %collective-permute-start.20 = (bf16[192,1024]{1,0:T(8,128)(2,1)S(1)}, bf16[192,1024]{1,0:T(8,128)(2,1)S(1)}, u32[]{:S(2)}, u32[]{:S(2)}) collective-permute-start(bf16[192,1024]{1,0:T(8,128)(2,1)S(1)} %fusion.22), channel_id=1, source_target_pairs={{0,2},{1,3},{2,0},{3,1},{4,6},{5,7},{6,4},{7,5},{8,10},{9,11},{10,... | collective-permute-start | bytes 1179656 | tf_op jit(solution)/shard_map/ppermute | solution.py:58
  64.5 12.9 %collective-permute-start.17 = (bf16[96,1024]{1,0:T(8,128)(2,1)S(1)}, bf16[96,1024]{1,0:T(8,128)(2,1)S(1)}, u32[]{:S(2)}, u32[]{:S(2)}) collective-permute-start(bf16[96,1024]{1,0:T(8,128)(2,1)S(1)} %get-tuple-element.19), channel_id=1, source_target_pairs={{0,16},{1,17},{2,18},{3,19},{4,20},{5,21},{6,22},{7,23},{8,24},{9,... | collective-permute-start | bytes 589832 | tf_op jit(solution)/shard_map/ppermute | solution.py:58
  79.4 5.7 %collective-permute-start.25 = (bf16[96,1024]{1,0:T(8,128)(2,1)S(1)}, bf16[96,1024]{1,0:T(8,128)(2,1)S(1)}, u32[]{:S(2)}, u32[]{:S(2)}) collective-permute-start(bf16[96,1024]{1,0:T(8,128)(2,1)S(1)} %get-tuple-element.16), channel_id=1, source_target_pairs={{0,16},{1,17},{2,18},{3,19},{4,20},{5,21},{6,22},{7,23},{8,24},{9,... | collective-permute-start | bytes 589832 | tf_op jit(solution)/shard_map/ppermute | solution.py:58
  80.7 5.7 %collective-permute-start.18 = (bf16[96,1024]{1,0:T(8,128)(2,1)S(1)}, bf16[96,1024]{1,0:T(8,128)(2,1)S(1)}, u32[]{:S(2)}, u32[]{:S(2)}) collective-permute-start(bf16[96,1024]{1,0:T(8,128)(2,1)S(1)} %get-tuple-element.17), channel_id=1, source_target_pairs={{0,8},{1,9},{2,10},{3,11},{4,12},{5,13},{6,14},{7,15},{8,0},{9,1},... | collective-permute-start | bytes 589832 | tf_op jit(solution)/shard_map/ppermute | solution.py:58
  82.1 5.9 %collective-permute-start.19 = (bf16[192,1024]{1,0:T(8,128)(2,1)S(1)}, bf16[192,1024]{1,0:T(8,128)(2,1)S(1)}, u32[]{:S(2)}, u32[]{:S(2)}) collective-permute-start(bf16[192,1024]{1,0:T(8,128)(2,1)S(1)} %fusion.22), channel_id=1, source_target_pairs={{1,2},{2,1},{5,6},{6,5},{9,10},{10,9},{13,14},{14,13},{17,18},{18,... | collective-permute-start | bytes 1179656 | tf_op jit(solution)/shard_map/ppermute | solution.py:58
  82.8 8.8 %collective-permute-start.21 = (bf16[192,1024]{1,0:T(8,128)(2,1)S(1)}, bf16[192,1024]{1,0:T(8,128)(2,1)S(1)}, u32[]{:S(2)}, u32[]{:S(2)}) collective-permute-start(bf16[192,1024]{1,0:T(8,128)(2,1)S(1)} %collective-permute-done.20), channel_id=1, source_target_pairs={{0,1},{1,0},{2,3},{3,2},{4,5},{5,4},{6,7},{7,6},{8,9},{9,8},{10,11... | collective-permute-start | bytes 1179656 | tf_op jit(solution)/shard_map/ppermute | solution.py:58
  87.3 5.7 %collective-permute-start.22 = (bf16[96,1024]{1,0:T(8,128)(2,1)S(1)}, bf16[96,1024]{1,0:T(8,128)(2,1)S(1)}, u32[]{:S(2)}, u32[]{:S(2)}) collective-permute-start(bf16[96,1024]{1,0:T(8,128)(2,1)S(1)} %get-tuple-element.15), channel_id=1, source_target_pairs={{0,16},{1,17},{2,18},{3,19},{4,20},{5,21},{6,22},{7,23},{8,24},{9,... | collective-permute-start | bytes 589832 | tf_op jit(solution)/shard_map/ppermute | solution.py:58
  91.7 5.8 %collective-permute-start.26 = (bf16[96,1024]{1,0:T(8,128)(2,1)S(1)}, bf16[96,1024]{1,0:T(8,128)(2,1)S(1)}, u32[]{:S(2)}, u32[]{:S(2)}) collective-permute-start(bf16[96,1024]{1,0:T(8,128)(2,1)S(1)} %get-tuple-element.14), channel_id=1, source_target_pairs={{0,8},{1,9},{2,10},{3,11},{4,12},{5,13},{6,14},{7,15},{8,0},{9,1},... | collective-permute-start | bytes 589832 | tf_op jit(solution)/shard_map/ppermute | solution.py:58
  93.0 6.6 %collective-permute-start.23 = (bf16[96,1024]{1,0:T(8,128)(2,1)S(1)}, bf16[96,1024]{1,0:T(8,128)(2,1)S(1)}, u32[]{:S(2)}, u32[]{:S(2)}) collective-permute-start(bf16[96,1024]{1,0:T(8,128)(2,1)S(1)} %broadcast_select_fusion.12), channel_id=1, source_target_pairs={{0,8},{1,9},{2,10},{3,11},{4,12},{5,13},{6,14},{7,15},{8,0},{9,1},... | collective-permute-start | bytes 589832 | tf_op jit(solution)/shard_map/ppermute | solution.py:58
  100.5 5.7 %collective-permute-start.27 = (bf16[96,1024]{1,0:T(8,128)(2,1)S(1)}, bf16[96,1024]{1,0:T(8,128)(2,1)S(1)}, u32[]{:S(2)}, u32[]{:S(2)}) collective-permute-start(bf16[96,1024]{1,0:T(8,128)(2,1)S(1)} %get-tuple-element.13), channel_id=1, source_target_pairs={{0,16},{1,17},{2,18},{3,19},{4,20},{5,21},{6,22},{7,23},{8,24},{9,... | collective-permute-start | bytes 589832 | tf_op jit(solution)/shard_map/ppermute | solution.py:58
  106.3 5.7 %collective-permute-start.28 = (bf16[96,1024]{1,0:T(8,128)(2,1)S(1)}, bf16[96,1024]{1,0:T(8,128)(2,1)S(1)}, u32[]{:S(2)}, u32[]{:S(2)}) collective-permute-start(bf16[96,1024]{1,0:T(8,128)(2,1)S(1)} %get-tuple-element.29), channel_id=1, source_target_pairs={{0,8},{1,9},{2,10},{3,11},{4,12},{5,13},{6,14},{7,15},{8,0},{9,1},... | collective-permute-start | bytes 589832 | tf_op jit(solution)/shard_map/ppermute | solution.py:58
  107.1 7.7 %collective-permute-start.31 = (bf16[768,1024]{1,0:T(8,128)(2,1)}, bf16[768,1024]{1,0:T(8,128)(2,1)}, u32[]{:S(2)}, u32[]{:S(2)}) collective-permute-start(bf16[768,1024]{1,0:T(8,128)(2,1)} %get-tuple-element.6), channel_id=1, source_target_pairs={{0,4},{1,5},{2,6},{3,7},{4,0},{5,1},{6,2},{7,3},{8,12},{9,13},{10,... | collective-permute-start | bytes 4718600 | tf_op jit(solution)/shard_map/ppermute | solution.py:58
  107.1 7.3 %collective-permute-start.29 = (bf16[96,1024]{1,0:T(8,128)(2,1)S(1)}, bf16[96,1024]{1,0:T(8,128)(2,1)S(1)}, u32[]{:S(2)}, u32[]{:S(2)}) collective-permute-start(bf16[96,1024]{1,0:T(8,128)(2,1)S(1)} %get-tuple-element.12), channel_id=1, source_target_pairs={{0,16},{1,17},{2,18},{3,19},{4,20},{5,21},{6,22},{7,23},{8,24},{9,... | collective-permute-start | bytes 589832 | tf_op jit(solution)/shard_map/ppermute | solution.py:58
  114.7 8.1 %collective-permute-start.30 = (bf16[768,1024]{1,0:T(8,128)(2,1)S(1)}, bf16[768,1024]{1,0:T(8,128)(2,1)}, u32[]{:S(2)}, u32[]{:S(2)}) collective-permute-start(bf16[768,1024]{1,0:T(8,128)(2,1)S(1)} %select_dynamic-update-slice_fusion.8), channel_id=1, source_target_pairs={{0,4},{1,5},{2,6},{3,7},{4,0},{5,1},{6,2},{7,3},{8,12},{9,13},{10,... | collective-permute-start | bytes 4718600 | tf_op jit(solution)/shard_map/ppermute | solution.py:58
  (10 other events, 162.1 us)

commit v2 on v1

--- a/solution.py
+++ b/solution.py
@@ -1,6 +1,8 @@
 import jax
 import jax.numpy as jnp
 from jax import lax
+from jax.experimental import pallas as pl
+from jax.experimental.pallas import tpu as pltpu
 from jax.sharding import PartitionSpec as P
 
 EPS = 1e-05
@@ -16,6 +18,43 @@
     return lax.dot_general(
         left, right, (((0,), (0,)), ((), ())), preferred_element_type=jnp.float32
     )
+
+
+ROWS = 256
+
+
+def gram_rows_kernel(scale, _place, left, right, *rest):
+    rest[-1][...] = scale * lax.dot_general(
+        left[...], right[...], (((0,), (0,)), ((), ())), preferred_element_type=jnp.float32
+    )
+
+
+def gram_rows(left, right, place, scale, rows_all, into=None):
+    depth, rows = left.shape
+    steps = rows // ROWS
+    columns = right.shape[1]
+    grid = pltpu.PrefetchScalarGridSpec(
+        num_scalar_prefetch=1,
+        grid=(steps,),
+        in_specs=[
+            pl.BlockSpec((depth, ROWS), lambda i, place: (0, i)),
+            pl.BlockSpec((depth, columns), lambda i, place: (0, 0)),
+        ]
+        + ([] if into is None else [pl.BlockSpec(memory_space=pl.ANY)]),
+        out_specs=pl.BlockSpec((ROWS, columns), lambda i, place: (place[0] * steps + i, 0)),
+    )
+    return pl.pallas_call(
+        lambda *refs: gram_rows_kernel(scale, *refs),
+        out_shape=jax.ShapeDtypeStruct((rows_all, columns), jnp.float32),
+        grid_spec=grid,
+        input_output_aliases={} if into is None else {3: 0},
+        compiler_params=pltpu.CompilerParams(vmem_limit_bytes=24 * 1024 * 1024),
+        cost_estimate=pl.CostEstimate(
+            flops=2 * depth * rows * columns,
+            bytes_accessed=4 * rows * columns + 2 * depth * (rows + columns),
+            transcendentals=0,
+        ),
+    )(place, left, right, *([] if into is None else [into]))
 
 
 def normalize(hidden_states, sums, norm_gain, features):
@@ -89,55 +128,88 @@
     def z_middle(x):
         return go(x, lambda d, c: (d, 3 - c) if c in (1, 2) else None)
 
-    def gather_z(own):
-        b = z2(own)
-        a = z1(own)
-        middle = z_middle(own)
-        ends = z1(b)
-        last = jnp.where((z == 1) | (z == 2), middle, ends)
-        return [own, a, b, last]
-
+    def tie(*values):
+        return lax.optimization_barrier(values)
+
+    half = tokens // 2
+    root = role == 0
+
+    def send(new, back=None, last=False):
+        low, high = (new[half:], new[:half]) if last else (new[:half], new[half:])
+        if back is not None:
+            low = jnp.where(root, low, back[1])
+            high = jnp.where(root, high, back[0])
+        return along_x(low), along_y(high)
+
+    def assemble(own, got):
+        n = len(own)
+        pieces = []
+        for c in range(n):
+            low, high = own[c][:half], own[c][half:]
+            x0, y0 = got[c]
+            x1, y1 = got[c + 1]
+            if c < n - 1:
+                x2, y2 = got[c + 2]
+                pieces.append(lax.select_n(role, low, x0, x2, y1))
+                pieces.append(lax.select_n(role, high, y2, y0, x1))
+            else:
+                pieces.append(lax.select_n(role, low, x0, y1, y1))
+                pieces.append(lax.select_n(role, high, x1, y0, x1))
+        return jnp.concatenate(pieces, axis=0)
+
+    inner = (z == 1) | (z == 2)
+    scale = 1.0 / (tokens * n_ctx)
+    rows_all = 2 * width
+    mine_at = jnp.reshape(parity, (1,)).astype(jnp.int32)
+    other_at = 1 - mine_at
+
+    g0 = out_grads
+    g2, g1 = z2(g0), z1(g0)
     sums = squares(hidden_states)
     sums = sums + core(sums)
     sums = (sums + along_x(sums)) + (along_y(sums) + across(sums))
-    normed = normalize(hidden_states, sums, norm_gain, width * n_dp)
-
-    g = gather_z(out_grads)
-    x = gather_z(normed)
-    order = [g[0], x[0], g[1], g[2], g[3], x[1], x[2], x[3]]
-    half = tokens // 2
-    n = len(order)
-    rx, ry = [], []
-    for r in range(n + 1):
-        source = order[min(r, n - 1)]
-        low, high = source[:half], source[half:]
-        if r == n:
-            low, high = high, low
-        px = low if r == 0 else jnp.where(role == 0, low, ry[r - 1])
-        py = high if r == 0 else jnp.where(role == 0, high, rx[r - 1])
-        rx.append(along_x(px))
-        ry.append(along_y(py))
-    stripes = []
-    for c in range(n):
-        low, high = order[c][:half], order[c][half:]
-        if c < n - 1:
-            got_low = lax.select_n(role, low, rx[c], rx[c + 2], ry[c + 1])
-            got_high = lax.select_n(role, high, ry[c + 2], ry[c], rx[c + 1])
-        else:
-            got_low = lax.select_n(role, low, rx[c], ry[c + 1], ry[c + 1])
-            got_high = lax.select_n(role, high, rx[c + 1], ry[c], rx[c + 1])
-        stripes += [got_low, got_high]
-
-    def factor(picks, chunks):
-        mine = jnp.concatenate([s for p in picks for s in stripes[2 * p : 2 * p + 2]], axis=0)
-        other = core(mine)
-        first = jnp.where(parity == 0, mine, other)
-        second = jnp.where(parity == 0, other, mine)
-        stripe = jnp.concatenate([first, second], axis=1)
-        return gram(stripe, jnp.concatenate(chunks, axis=0)) / (tokens * n_ctx)
-
-    g_factor = factor([0, 2, 3, 4], g)
-    a_factor = factor([1, 5, 6, 7], x)
+    e0 = send(g0)
+    x0 = normalize(hidden_states, sums, norm_gain, width * n_dp)
+    *e0, x0 = tie(*e0, x0)
+    o0 = send(x0)
+    x1 = z1(x0)
+    g1_, g2_, g0_ = tie(g1, g2, g0)
+    g_ends, g_middle = z1(g2_), z_middle(g0_)
+    o0x, o0y, e0x, e0y, g1, g2, x0_ = tie(*o0, *e0, g1, g2, x0)
+    o0, e0 = (o0x, o0y), (e0x, e0y)
+    e1 = send(g1, e0)
+    x2 = z2(x0_)
+    e1x, e1y, g_ends, g_middle, g2_ = tie(*e1, g_ends, g_middle, g2)
+    e1 = (e1x, e1y)
+    e2 = send(g2_, e1)
+    e2x, e2y, x1, o0x, o0y = tie(*e2, x1, *o0)
+    e2, o0 = (e2x, e2y), (o0x, o0y)
+    g3 = jnp.where(inner, g_middle, g_ends)
+    e3, o1 = send(g3, e2), send(x1, o0)
+    x2, x0_ = tie(x2, x0_)
+    x_ends, x_middle = z1(x2), z_middle(x0_)
+    e3x, e3y, o1x, o1y, x2_ = tie(*e3, *o1, x2)
+    e3, o1 = (e3x, e3y), (o1x, o1y)
+    e4, o2 = send(g3, e3, last=True), send(x2_, o1)
+    e4x, e4y, o2x, o2y, x_ends, x_middle = tie(*e4, *o2, x_ends, x_middle)
+    e4, o2 = (e4x, e4y), (o2x, o2y)
+    x3 = jnp.where(inner, x_middle, x_ends)
+    o3 = send(x3, o2)
+    g_mine = assemble([g0, g1, g2, g3], [e0, e1, e2, e3, e4])
+    g_other = core(g_mine)
+    g_column = jnp.concatenate([g0, g1, g2, g3], axis=0)
+    g_factor = gram_rows(g_mine, g_column, mine_at, scale, rows_all)
+    o3x, o3y, g_factor, g_other = tie(*o3, g_factor, g_other)
+    o3 = (o3x, o3y)
+    o4 = send(x3, o3, last=True)
+    g_factor = gram_rows(g_other, g_column, other_at, scale, rows_all, g_factor)
+    x_column = jnp.concatenate([x0, x1, x2, x3], axis=0)
+    o4x, o4y, g_factor, x_column = tie(*o4, g_factor, x_column)
+    o4 = (o4x, o4y)
+    x_mine = assemble([x0, x1, x2, x3], [o0, o1, o2, o3, o4])
+    x_other = core(x_mine)
+    a_factor = gram_rows(x_mine, x_column, mine_at, scale, rows_all)
+    a_factor = gram_rows(x_other, x_column, other_at, scale, rows_all, a_factor)
     return a_factor, g_factor
 
 

time: 131 us -> 99.4 us (0.76)
  waiting for transfers between devices: 68.2 us -> 27.8 us
  Pallas kernels: 0 us -> 15.8 us
  matrix products: 11.7 us -> 0 us
  starting transfers between devices: 32.6 us -> 43.8 us
  other arithmetic: 16.1 us -> 8.16 us
    ppermute x32 -> x34, waiting for transfers between devices: 68.2 us -> 27.8 us  [swap(): return lax.ppermute(x, AXES, pairs)]
    pallas_call x0 -> x4, Pallas kernels: none -> 15.8 us  [gram_rows(): pl.pallas_call(lambda *refs: gram_rows_kernel(scale, *refs), out_shape=ja...]
    dot_general x2 -> x0, matrix products: 11.7 us -> none  [gram(): lax.dot_general(left, right, (((0,), (0,)), ((), ())), preferred_element_...]
    ppermute x32 -> x34, starting transfers between devices: 32.6 us -> 43.8 us  [swap(): return lax.ppermute(x, AXES, pairs)]
    select_n x15 -> x10, other arithmetic: 9.14 us -> 2.4 us  [the longest x8 1.21 us: send(): high = jnp.where(root, high, back[0])]
    unnamed x6 -> x10, other arithmetic: 2.87 us -> 2.27 us
  transfers between devices with their start and end apart: 32 -> 34, of which waited for: 18 -> 20; matrix products, arithmetic and copies ran while one was open for 14% -> 7% of each run, Pallas kernels for 0% -> 12%
where the time goes in v2:
time: 99.4 us; the launch traced here: 98.2 us
  starting transfers between devices  43.8 us (44%)
  waiting for transfers between devices  27.8 us (28%)
  Pallas kernels  15.8 us (16%)
  other arithmetic  8.16 us (8%)
  local copies, waits for them, and re-layouts  1.51 us (2%)
  between operations  1.12 us (1%)
    ppermute x34, starting transfers between devices, swap(): return lax.ppermute(x, AXES, pairs)  43.8 us
    ppermute x34, waiting for transfers between devices, swap(): return lax.ppermute(x, AXES, pairs)  27.8 us
    pallas_call x4, Pallas kernels, gram_rows(): pl.pallas_call(lambda *refs: gram_rows_kernel(scale, *refs), out_shape=ja...  15.8 us
    unnamed x10, other arithmetic  2.27 us
  transfers between devices with their start and end apart: 34, of which 20 were waited for; matrix products, arithmetic and copies ran while one was open for 7% of the time, Pallas kernels for 12%

profile of v2, /device:TPU:0, one launch (start us, length us, event | category | flops | bytes accessed | tf_op | source)
XLA Modules:
  0.0 98.2 jit_solution(5980639327640684450)
XLA Ops:
  0.6 1.2 %fusion = f32[192]{0:T(256)S(1)} fusion(bf16[192,1024]{1,0:T(8,128)(2,1)} %param.3), kind=kLoop, calls=%fused_computation.4 | loop fusion | flops 589632 | bytes 393984 | tf_op jit(solution)/shard_map/reduce_sum | solution.py:69
  2.4 3.7 %collective-permute-start.9 = (bf16[192,1024]{1,0:T(8,128)(2,1)}, bf16[192,1024]{1,0:T(8,128)(2,1)S(1)}, u32[]{:S(2)}, u32[]{:S(2)}) collective-permute-start(bf16[192,1024]{1,0:T(8,128)(2,1)} %param.4), channel_id=1, source_target_pairs={{0,2},{1,3},{2,0},{3,1},{4,6},{5,7},{6,4},{7,5},{8,10},{9,11},{10,... | collective-permute-start | bytes 1179656 | tf_op jit(solution)/shard_map/ppermute | solution.py:97
  6.0 1.6 %collective-permute-start.8 = (bf16[192,1024]{1,0:T(8,128)(2,1)}, bf16[192,1024]{1,0:T(8,128)(2,1)S(1)}, u32[]{:S(2)}, u32[]{:S(2)}) collective-permute-start(bf16[192,1024]{1,0:T(8,128)(2,1)} %param.4), channel_id=1, source_target_pairs={{0,1},{1,0},{2,3},{3,2},{4,5},{5,4},{6,7},{7,6},{8,9},{9,8},{10,11... | collective-permute-start | bytes 1179656 | tf_op jit(solution)/shard_map/ppermute | solution.py:97
  7.6 2.4 %collective-permute-start.5 = (f32[192,1]{0,1:T(1,128)S(1)}, f32[192,1]{0,1:T(1,128)S(1)}, u32[]{:S(2)}, u32[]{:S(2)}) collective-permute-start(f32[192,1]{0,1:T(1,128)S(1)} %add.24), channel_id=1, source_target_pairs={{0,24},{1,25},{2,26},{3,27},{4,28},{5,29},{6,30},{7,31},{8,16},{9,... | collective-permute-start | bytes 2312 | tf_op jit(solution)/shard_map/ppermute | solution.py:97
  12.8 1.5 %collective-permute-start.1 = (bf16[96,1024]{1,0:T(8,128)(2,1)S(1)}, bf16[96,1024]{1,0:T(8,128)(2,1)S(1)}, u32[]{:S(2)}, u32[]{:S(2)}) collective-permute-start(bf16[96,1024]{1,0:T(8,128)(2,1)S(1)} %get-tuple-element.106), channel_id=1, source_target_pairs={{0,16},{1,17},{2,18},{3,19},{4,20},{5,21},{6,22},{7,23},{8,24},{9,... | collective-permute-start | bytes 589832 | tf_op jit(solution)/shard_map/ppermute | solution.py:97
  14.4 1.5 %collective-permute-start = (bf16[96,1024]{1,0:T(8,128)(2,1)S(1)}, bf16[96,1024]{1,0:T(8,128)(2,1)S(1)}, u32[]{:S(2)}, u32[]{:S(2)}) collective-permute-start(bf16[96,1024]{1,0:T(8,128)(2,1)S(1)} %get-tuple-element.107), channel_id=1, source_target_pairs={{0,8},{1,9},{2,10},{3,11},{4,12},{5,13},{6,14},{7,15},{8,0},{9,1},... | collective-permute-start | bytes 589832 | tf_op jit(solution)/shard_map/ppermute | solution.py:97
  17.0 1.7 %collective-permute-done.1 = bf16[96,1024]{1,0:T(8,128)(2,1)S(1)} collective-permute-done((bf16[96,1024]{1,0:T(8,128)(2,1)S(1)}, bf16[96,1024]{1,0:T(8,128)(2,1)S(1)}, u32[]{:S(2)}, u32[]{:S(2)}) %collective-permute-start.1) | collective-permute-done | bytes 196640 | tf_op jit(solution)/shard_map/ppermute | solution.py:97
  18.7 1.3 %collective-permute-done = bf16[96,1024]{1,0:T(8,128)(2,1)S(1)} collective-permute-done((bf16[96,1024]{1,0:T(8,128)(2,1)S(1)}, bf16[96,1024]{1,0:T(8,128)(2,1)S(1)}, u32[]{:S(2)}, u32[]{:S(2)}) %collective-permute-start) | collective-permute-done | bytes 196640 | tf_op jit(solution)/shard_map/ppermute | solution.py:97
  20.6 1.5 %collective-permute-start.6 = (bf16[96,1024]{1,0:T(8,128)(2,1)S(1)}, bf16[96,1024]{1,0:T(8,128)(2,1)S(1)}, u32[]{:S(2)}, u32[]{:S(2)}) collective-permute-start(bf16[96,1024]{1,0:T(8,128)(2,1)S(1)} %get-tuple-element.105), channel_id=1, source_target_pairs={{0,8},{1,9},{2,10},{3,11},{4,12},{5,13},{6,14},{7,15},{8,0},{9,1},... | collective-permute-start | bytes 589832 | tf_op jit(solution)/shard_map/ppermute | solution.py:97
  22.1 2.3 %collective-permute-done.9 = bf16[192,1024]{1,0:T(8,128)(2,1)S(1)} collective-permute-done((bf16[192,1024]{1,0:T(8,128)(2,1)}, bf16[192,1024]{1,0:T(8,128)(2,1)S(1)}, u32[]{:S(2)}, u32[]{:S(2)}) %collective-permute-start.9) | collective-permute-done | bytes 393248 | tf_op jit(solution)/shard_map/ppermute | solution.py:97
  27.5 1.6 %collective-permute-start.11 = (bf16[96,1024]{1,0:T(8,128)(2,1)S(1)}, bf16[96,1024]{1,0:T(8,128)(2,1)S(1)}, u32[]{:S(2)}, u32[]{:S(2)}) collective-permute-start(bf16[96,1024]{1,0:T(8,128)(2,1)S(1)} %get-tuple-element.102), channel_id=1, source_target_pairs={{0,16},{1,17},{2,18},{3,19},{4,20},{5,21},{6,22},{7,23},{8,24},{9,... | collective-permute-start | bytes 589832 | tf_op jit(solution)/shard_map/ppermute | solution.py:97
  29.1 1.5 %collective-permute-start.10 = (bf16[96,1024]{1,0:T(8,128)(2,1)S(1)}, bf16[96,1024]{1,0:T(8,128)(2,1)S(1)}, u32[]{:S(2)}, u32[]{:S(2)}) collective-permute-start(bf16[96,1024]{1,0:T(8,128)(2,1)S(1)} %get-tuple-element.103), channel_id=1, source_target_pairs={{0,8},{1,9},{2,10},{3,11},{4,12},{5,13},{6,14},{7,15},{8,0},{9,1},... | collective-permute-start | bytes 589832 | tf_op jit(solution)/shard_map/ppermute | solution.py:97
  30.6 3.6 %collective-permute-start.16 = (bf16[192,1024]{1,0:T(8,128)(2,1)S(1)}, bf16[192,1024]{1,0:T(8,128)(2,1)S(1)}, u32[]{:S(2)}, u32[]{:S(2)}) collective-permute-start(bf16[192,1024]{1,0:T(8,128)(2,1)S(1)} %fusion.2), channel_id=1, source_target_pairs={{0,1},{1,0},{2,3},{3,2},{4,5},{5,4},{6,7},{7,6},{8,9},{9,8},{10,11... | collective-permute-start | bytes 1179656 | tf_op jit(solution)/shard_map/ppermute | solution.py:97
  34.2 3.3 %collective-permute-start.21 = (bf16[192,1024]{1,0:T(8,128)(2,1)S(1)}, bf16[192,1024]{1,0:T(8,128)(2,1)S(1)}, u32[]{:S(2)}, u32[]{:S(2)}) collective-permute-start(bf16[192,1024]{1,0:T(8,128)(2,1)S(1)} %fusion.2), channel_id=1, source_target_pairs={{0,2},{1,3},{2,0},{3,1},{4,6},{5,7},{6,4},{7,5},{8,10},{9,11},{10,... | collective-permute-start | bytes 1179656 | tf_op jit(solution)/shard_map/ppermute | solution.py:97
  37.6 1.6 %collective-permute-start.15 = (bf16[96,1024]{1,0:T(8,128)(2,1)S(1)}, bf16[96,1024]{1,0:T(8,128)(2,1)S(1)}, u32[]{:S(2)}, u32[]{:S(2)}) collective-permute-start(bf16[96,1024]{1,0:T(8,128)(2,1)S(1)} %get-tuple-element.100), channel_id=1, source_target_pairs={{0,16},{1,17},{2,18},{3,19},{4,20},{5,21},{6,22},{7,23},{8,24},{9,... | collective-permute-start | bytes 589832 | tf_op jit(solution)/shard_map/ppermute | solution.py:97
  39.2 3.3 %collective-permute-start.14 = (bf16[96,1024]{1,0:T(8,128)(2,1)S(1)}, bf16[96,1024]{1,0:T(8,128)(2,1)S(1)}, u32[]{:S(2)}, u32[]{:S(2)}) collective-permute-start(bf16[96,1024]{1,0:T(8,128)(2,1)S(1)} %get-tuple-element.101), channel_id=1, source_target_pairs={{0,8},{1,9},{2,10},{3,11},{4,12},{5,13},{6,14},{7,15},{8,0},{9,1},... | collective-permute-start | bytes 589832 | tf_op jit(solution)/shard_map/ppermute | solution.py:97
  42.5 7.6 %collective-permute-done.16 = bf16[192,1024]{1,0:T(8,128)(2,1)S(1)} collective-permute-done((bf16[192,1024]{1,0:T(8,128)(2,1)S(1)}, bf16[192,1024]{1,0:T(8,128)(2,1)S(1)}, u32[]{:S(2)}, u32[]{:S(2)}) %collective-permute-start.16) | collective-permute-done | bytes 393248 | tf_op jit(solution)/shard_map/ppermute | solution.py:97
  50.2 1.5 %collective-permute-start.20 = (bf16[96,1024]{1,0:T(8,128)(2,1)S(1)}, bf16[96,1024]{1,0:T(8,128)(2,1)S(1)}, u32[]{:S(2)}, u32[]{:S(2)}) collective-permute-start(bf16[96,1024]{1,0:T(8,128)(2,1)S(1)} %get-tuple-element.96), channel_id=1, source_target_pairs={{0,16},{1,17},{2,18},{3,19},{4,20},{5,21},{6,22},{7,23},{8,24},{9,... | collective-permute-start | bytes 589832 | tf_op jit(solution)/shard_map/ppermute | solution.py:97
  51.7 1.5 %collective-permute-start.19 = (bf16[96,1024]{1,0:T(8,128)(2,1)S(1)}, bf16[96,1024]{1,0:T(8,128)(2,1)S(1)}, u32[]{:S(2)}, u32[]{:S(2)}) collective-permute-start(bf16[96,1024]{1,0:T(8,128)(2,1)S(1)} %get-tuple-element.97), channel_id=1, source_target_pairs={{0,8},{1,9},{2,10},{3,11},{4,12},{5,13},{6,14},{7,15},{8,0},{9,1},... | collective-permute-start | bytes 589832 | tf_op jit(solution)/shard_map/ppermute | solution.py:97
  54.8 1.6 %collective-permute-done.21 = bf16[192,1024]{1,0:T(8,128)(2,1)S(1)} collective-permute-done((bf16[192,1024]{1,0:T(8,128)(2,1)S(1)}, bf16[192,1024]{1,0:T(8,128)(2,1)S(1)}, u32[]{:S(2)}, u32[]{:S(2)}) %collective-permute-start.21) | collective-permute-done | bytes 393248 | tf_op jit(solution)/shard_map/ppermute | solution.py:97
  58.6 1.5 %collective-permute-done.18 = bf16[96,1024]{1,0:T(8,128)(2,1)S(1)} collective-permute-done((bf16[96,1024]{1,0:T(8,128)(2,1)S(1)}, bf16[96,1024]{1,0:T(8,128)(2,1)S(1)}, u32[]{:S(2)}, u32[]{:S(2)}) %collective-permute-start.18) | collective-permute-done | bytes 196640 | tf_op jit(solution)/shard_map/ppermute | solution.py:97
  61.1 1.2 %collective-permute-start.23 = (bf16[96,1024]{1,0:T(8,128)(2,1)S(1)}, bf16[96,1024]{1,0:T(8,128)(2,1)S(1)}, u32[]{:S(2)}, u32[]{:S(2)}) collective-permute-start(bf16[96,1024]{1,0:T(8,128)(2,1)S(1)} %get-tuple-element.94), channel_id=1, source_target_pairs={{0,16},{1,17},{2,18},{3,19},{4,20},{5,21},{6,22},{7,23},{8,24},{9,... | collective-permute-start | bytes 589832 | tf_op jit(solution)/shard_map/ppermute | solution.py:97
  63.1 1.2 %collective-permute-start.25 = (bf16[96,1024]{1,0:T(8,128)(2,1)S(1)}, bf16[96,1024]{1,0:T(8,128)(2,1)S(1)}, u32[]{:S(2)}, u32[]{:S(2)}) collective-permute-start(bf16[96,1024]{1,0:T(8,128)(2,1)S(1)} %get-tuple-element.92), channel_id=1, source_target_pairs={{0,16},{1,17},{2,18},{3,19},{4,20},{5,21},{6,22},{7,23},{8,24},{9,... | collective-permute-start | bytes 589832 | tf_op jit(solution)/shard_map/ppermute | solution.py:97
  67.3 1.2 %collective-permute-done.22 = bf16[96,1024]{1,0:T(8,128)(2,1)S(1)} collective-permute-done((bf16[96,1024]{1,0:T(8,128)(2,1)S(1)}, bf16[96,1024]{1,0:T(8,128)(2,1)S(1)}, u32[]{:S(2)}, u32[]{:S(2)}) %collective-permute-start.22) | collective-permute-done | bytes 196640 | tf_op jit(solution)/shard_map/ppermute | solution.py:97
  69.5 1.2 %collective-permute-done.24 = bf16[96,1024]{1,0:T(8,128)(2,1)S(1)} collective-permute-done((bf16[96,1024]{1,0:T(8,128)(2,1)S(1)}, bf16[96,1024]{1,0:T(8,128)(2,1)S(1)}, u32[]{:S(2)}, u32[]{:S(2)}) %collective-permute-start.24) | collective-permute-done | bytes 196640 | tf_op jit(solution)/shard_map/ppermute | solution.py:97
  71.6 1.2 %select_dynamic-update-slice_fusion.15 = bf16[768,1024]{1,0:T(8,128)(2,1)S(1)} fusion(bf16[96,1024]{1,0:T(8,128)(2,1)} %copy-done.12, bf16[96,1024]{1,0:T(8,128)(2,1)} %copy-done.16, bf16[96,1024]{1,0:T(8,128)(2,1)} %copy-done.28, pred[]{:T(512)S(6)} %select_n.345, pred[]{:T(512)S(6)} %select_n.337, pred[]{:T(512)S(6)} %select_n.335, ...), kind=kLoop, calls=%fused_computation.24 | loop fusion | flops 294911 | bytes 983043
  76.2 4.0 %shard_map.50.refs_3_ = f32[2048,1024]{1,0:T(8,128)} custom-call(s32[1]{0:T(128)} %bitcast.refs_0_, bf16[768,1024]{1,0:T(8,128)(2,1)S(1)} %select_dynamic-update-slice_fusion.6.refs_1_, bf16[768,1024]{1,0:T(8,128)(2,1)S(1)} %pad_maximum_fusion.refs_2_), custom_call_target="tpu_custom_call" | custom-call | flops 1610612736 | bytes 7340032 | tf_op jit(solution)/shard_map/pallas_call | solution.py:46
  80.1 1.5 %collective-permute-done.29 = bf16[96,1024]{1,0:T(8,128)(2,1)S(1)} collective-permute-done((bf16[96,1024]{1,0:T(8,128)(2,1)S(1)}, bf16[96,1024]{1,0:T(8,128)(2,1)S(1)}, u32[]{:S(2)}, u32[]{:S(2)}) %collective-permute-start.29) | collective-permute-done | bytes 196640 | tf_op jit(solution)/shard_map/ppermute | solution.py:97
  82.4 1.4 %collective-permute-start.32 = (bf16[96,1024]{1,0:T(8,128)(2,1)S(1)}, bf16[96,1024]{1,0:T(8,128)(2,1)S(1)}, u32[]{:S(2)}, u32[]{:S(2)}) collective-permute-start(bf16[96,1024]{1,0:T(8,128)(2,1)S(1)} %get-tuple-element.88), channel_id=1, source_target_pairs={{0,16},{1,17},{2,18},{3,19},{4,20},{5,21},{6,22},{7,23},{8,24},{9,... | collective-permute-start | bytes 589832 | tf_op jit(solution)/shard_map/ppermute | solution.py:97
  84.6 4.0 %shard_map.51 = f32[2048,1024]{1,0:T(8,128)} custom-call(s32[1]{0:T(128)S(6)} %sub.7.refs_0_, bf16[768,1024]{1,0:T(8,128)(2,1)S(1)} %collective-permute-done.30.refs_1_, bf16[768,1024]{1,0:T(8,128)(2,1)S(1)} %pad_maximum_fusion.refs_2_, f32[2048,1024]{1,0:T(8,128)} %shard_map.50.refs_3_), custom_call_target="tpu_custom_call", output_to_operand_aliasing={{}: (3, {})} | custom-call | flops 1610612736 | bytes 7340032 | tf_op jit(solution)/shard_map/pallas_call | solution.py:46
  90.3 4.0 %shard_map.52.refs_3_ = f32[2048,1024]{1,0:T(8,128)} custom-call(s32[1]{0:T(128)} %bitcast.refs_0_, bf16[768,1024]{1,0:T(8,128)(2,1)S(1)} %select_dynamic-update-slice_fusion.refs_1_, bf16[768,1024]{1,0:T(8,128)(2,1)S(1)} %pad_maximum_fusion.1.refs_2_), custom_call_target="tpu_custom_call" | custom-call | flops 1610612736 | bytes 7340032 | tf_op jit(solution)/shard_map/pallas_call | solution.py:46
  94.2 3.9 %shard_map.53 = f32[2048,1024]{1,0:T(8,128)} custom-call(s32[1]{0:T(128)S(6)} %sub.7.refs_0_, bf16[768,1024]{1,0:T(8,128)(2,1)S(1)} %collective-permute-done.33.refs_1_, bf16[768,1024]{1,0:T(8,128)(2,1)S(1)} %pad_maximum_fusion.1.refs_2_, f32[2048,1024]{1,0:T(8,128)} %shard_map.52.refs_3_), custom_call_target="tpu_custom_call", output_to_operand_aliasing={{}: (3, {})} | custom-call | flops 1610612736 | bytes 7340032 | tf_op jit(solution)/shard_map/pallas_call | solution.py:46
  (137 shorter events, 24.9 us)
Async XLA Ops:
  1.8 5.8 %collective-permute-start.2 = (f32[192,1]{0,1:T(1,128)S(1)}, f32[192,1]{0,1:T(1,128)S(1)}, u32[]{:S(2)}, u32[]{:S(2)}) collective-permute-start(f32[192,1]{0,1:T(1,128)S(1)} %bitcast.5), channel_id=1, source_target_pairs={{0,4},{1,5},{2,6},{3,7},{4,0},{5,1},{6,2},{7,3},{8,12},{9,13},{10,... | collective-permute-start | bytes 2312 | tf_op jit(solution)/shard_map/ppermute | solution.py:97
  2.4 22.1 %collective-permute-start.9 = (bf16[192,1024]{1,0:T(8,128)(2,1)}, bf16[192,1024]{1,0:T(8,128)(2,1)S(1)}, u32[]{:S(2)}, u32[]{:S(2)}) collective-permute-start(bf16[192,1024]{1,0:T(8,128)(2,1)} %param.4), channel_id=1, source_target_pairs={{0,2},{1,3},{2,0},{3,1},{4,6},{5,7},{6,4},{7,5},{8,10},{9,11},{10,... | collective-permute-start | bytes 1179656 | tf_op jit(solution)/shard_map/ppermute | solution.py:97
  6.0 18.6 %collective-permute-start.8 = (bf16[192,1024]{1,0:T(8,128)(2,1)}, bf16[192,1024]{1,0:T(8,128)(2,1)S(1)}, u32[]{:S(2)}, u32[]{:S(2)}) collective-permute-start(bf16[192,1024]{1,0:T(8,128)(2,1)} %param.4), channel_id=1, source_target_pairs={{0,1},{1,0},{2,3},{3,2},{4,5},{5,4},{6,7},{7,6},{8,9},{9,8},{10,11... | collective-permute-start | bytes 1179656 | tf_op jit(solution)/shard_map/ppermute | solution.py:97
  7.6 5.2 %collective-permute-start.5 = (f32[192,1]{0,1:T(1,128)S(1)}, f32[192,1]{0,1:T(1,128)S(1)}, u32[]{:S(2)}, u32[]{:S(2)}) collective-permute-start(f32[192,1]{0,1:T(1,128)S(1)} %add.24), channel_id=1, source_target_pairs={{0,24},{1,25},{2,26},{3,27},{4,28},{5,29},{6,30},{7,31},{8,16},{9,... | collective-permute-start | bytes 2312 | tf_op jit(solution)/shard_map/ppermute | solution.py:97
  10.6 5.3 %collective-permute-start.3 = (f32[192,1]{0,1:T(1,128)S(1)}, f32[192,1]{0,1:T(1,128)S(1)}, u32[]{:S(2)}, u32[]{:S(2)}) collective-permute-start(f32[192,1]{0,1:T(1,128)S(1)} %add.24), channel_id=1, source_target_pairs={{0,8},{1,9},{2,10},{3,11},{4,12},{5,13},{6,14},{7,15},{8,0},{9,1},... | collective-permute-start | bytes 2312 | tf_op jit(solution)/shard_map/ppermute | solution.py:97
  12.8 5.9 %collective-permute-start.1 = (bf16[96,1024]{1,0:T(8,128)(2,1)S(1)}, bf16[96,1024]{1,0:T(8,128)(2,1)S(1)}, u32[]{:S(2)}, u32[]{:S(2)}) collective-permute-start(bf16[96,1024]{1,0:T(8,128)(2,1)S(1)} %get-tuple-element.106), channel_id=1, source_target_pairs={{0,16},{1,17},{2,18},{3,19},{4,20},{5,21},{6,22},{7,23},{8,24},{9,... | collective-permute-start | bytes 589832 | tf_op jit(solution)/shard_map/ppermute | solution.py:97
  14.4 5.7 %collective-permute-start = (bf16[96,1024]{1,0:T(8,128)(2,1)S(1)}, bf16[96,1024]{1,0:T(8,128)(2,1)S(1)}, u32[]{:S(2)}, u32[]{:S(2)}) collective-permute-start(bf16[96,1024]{1,0:T(8,128)(2,1)S(1)} %get-tuple-element.107), channel_id=1, source_target_pairs={{0,8},{1,9},{2,10},{3,11},{4,12},{5,13},{6,14},{7,15},{8,0},{9,1},... | collective-permute-start | bytes 589832 | tf_op jit(solution)/shard_map/ppermute | solution.py:97
  20.1 5.7 %collective-permute-start.7 = (bf16[96,1024]{1,0:T(8,128)(2,1)S(1)}, bf16[96,1024]{1,0:T(8,128)(2,1)S(1)}, u32[]{:S(2)}, u32[]{:S(2)}) collective-permute-start(bf16[96,1024]{1,0:T(8,128)(2,1)S(1)} %get-tuple-element.104), channel_id=1, source_target_pairs={{0,16},{1,17},{2,18},{3,19},{4,20},{5,21},{6,22},{7,23},{8,24},{9,... | collective-permute-start | bytes 589832 | tf_op jit(solution)/shard_map/ppermute | solution.py:97
  20.6 5.7 %collective-permute-start.6 = (bf16[96,1024]{1,0:T(8,128)(2,1)S(1)}, bf16[96,1024]{1,0:T(8,128)(2,1)S(1)}, u32[]{:S(2)}, u32[]{:S(2)}) collective-permute-start(bf16[96,1024]{1,0:T(8,128)(2,1)S(1)} %get-tuple-element.105), channel_id=1, source_target_pairs={{0,8},{1,9},{2,10},{3,11},{4,12},{5,13},{6,14},{7,15},{8,0},{9,1},... | collective-permute-start | bytes 589832 | tf_op jit(solution)/shard_map/ppermute | solution.py:97
  26.3 11.2 %collective-permute-start.12 = (bf16[192,1024]{1,0:T(8,128)(2,1)S(1)}, bf16[192,1024]{1,0:T(8,128)(2,1)S(1)}, u32[]{:S(2)}, u32[]{:S(2)}) collective-permute-start(bf16[192,1024]{1,0:T(8,128)(2,1)S(1)} %collective-permute-done.9), channel_id=1, source_target_pairs={{0,1},{1,0},{2,3},{3,2},{4,5},{5,4},{6,7},{7,6},{8,9},{9,8},{10,11... | collective-permute-start | bytes 1179656 | tf_op jit(solution)/shard_map/ppermute | solution.py:97
  26.8 10.8 %collective-permute-start.13 = (bf16[192,1024]{1,0:T(8,128)(2,1)S(1)}, bf16[192,1024]{1,0:T(8,128)(2,1)S(1)}, u32[]{:S(2)}, u32[]{:S(2)}) collective-permute-start(bf16[192,1024]{1,0:T(8,128)(2,1)S(1)} %copy-done.2), channel_id=1, source_target_pairs={{1,2},{2,1},{5,6},{6,5},{9,10},{10,9},{13,14},{14,13},{17,18},{18,... | collective-permute-start | bytes 1179656 | tf_op jit(solution)/shard_map/ppermute | solution.py:97
  27.5 6.7 %collective-permute-start.11 = (bf16[96,1024]{1,0:T(8,128)(2,1)S(1)}, bf16[96,1024]{1,0:T(8,128)(2,1)S(1)}, u32[]{:S(2)}, u32[]{:S(2)}) collective-permute-start(bf16[96,1024]{1,0:T(8,128)(2,1)S(1)} %get-tuple-element.102), channel_id=1, source_target_pairs={{0,16},{1,17},{2,18},{3,19},{4,20},{5,21},{6,22},{7,23},{8,24},{9,... | collective-permute-start | bytes 589832 | tf_op jit(solution)/shard_map/ppermute | solution.py:97
  29.1 8.4 %collective-permute-start.10 = (bf16[96,1024]{1,0:T(8,128)(2,1)S(1)}, bf16[96,1024]{1,0:T(8,128)(2,1)S(1)}, u32[]{:S(2)}, u32[]{:S(2)}) collective-permute-start(bf16[96,1024]{1,0:T(8,128)(2,1)S(1)} %get-tuple-element.103), channel_id=1, source_target_pairs={{0,8},{1,9},{2,10},{3,11},{4,12},{5,13},{6,14},{7,15},{8,0},{9,1},... | collective-permute-start | bytes 589832 | tf_op jit(solution)/shard_map/ppermute | solution.py:97
  30.6 19.5 %collective-permute-start.16 = (bf16[192,1024]{1,0:T(8,128)(2,1)S(1)}, bf16[192,1024]{1,0:T(8,128)(2,1)S(1)}, u32[]{:S(2)}, u32[]{:S(2)}) collective-permute-start(bf16[192,1024]{1,0:T(8,128)(2,1)S(1)} %fusion.2), channel_id=1, source_target_pairs={{0,1},{1,0},{2,3},{3,2},{4,5},{5,4},{6,7},{7,6},{8,9},{9,8},{10,11... | collective-permute-start | bytes 1179656 | tf_op jit(solution)/shard_map/ppermute | solution.py:97
  34.2 22.2 %collective-permute-start.21 = (bf16[192,1024]{1,0:T(8,128)(2,1)S(1)}, bf16[192,1024]{1,0:T(8,128)(2,1)S(1)}, u32[]{:S(2)}, u32[]{:S(2)}) collective-permute-start(bf16[192,1024]{1,0:T(8,128)(2,1)S(1)} %fusion.2), channel_id=1, source_target_pairs={{0,2},{1,3},{2,0},{3,1},{4,6},{5,7},{6,4},{7,5},{8,10},{9,11},{10,... | collective-permute-start | bytes 1179656 | tf_op jit(solution)/shard_map/ppermute | solution.py:97
  37.6 12.5 %collective-permute-start.15 = (bf16[96,1024]{1,0:T(8,128)(2,1)S(1)}, bf16[96,1024]{1,0:T(8,128)(2,1)S(1)}, u32[]{:S(2)}, u32[]{:S(2)}) collective-permute-start(bf16[96,1024]{1,0:T(8,128)(2,1)S(1)} %get-tuple-element.100), channel_id=1, source_target_pairs={{0,16},{1,17},{2,18},{3,19},{4,20},{5,21},{6,22},{7,23},{8,24},{9,... | collective-permute-start | bytes 589832 | tf_op jit(solution)/shard_map/ppermute | solution.py:97
  39.2 10.9 %collective-permute-start.14 = (bf16[96,1024]{1,0:T(8,128)(2,1)S(1)}, bf16[96,1024]{1,0:T(8,128)(2,1)S(1)}, u32[]{:S(2)}, u32[]{:S(2)}) collective-permute-start(bf16[96,1024]{1,0:T(8,128)(2,1)S(1)} %get-tuple-element.101), channel_id=1, source_target_pairs={{0,8},{1,9},{2,10},{3,11},{4,12},{5,13},{6,14},{7,15},{8,0},{9,1},... | collective-permute-start | bytes 589832 | tf_op jit(solution)/shard_map/ppermute | solution.py:97
  50.2 7.8 %collective-permute-start.20 = (bf16[96,1024]{1,0:T(8,128)(2,1)S(1)}, bf16[96,1024]{1,0:T(8,128)(2,1)S(1)}, u32[]{:S(2)}, u32[]{:S(2)}) collective-permute-start(bf16[96,1024]{1,0:T(8,128)(2,1)S(1)} %get-tuple-element.96), channel_id=1, source_target_pairs={{0,16},{1,17},{2,18},{3,19},{4,20},{5,21},{6,22},{7,23},{8,24},{9,... | collective-permute-start | bytes 589832 | tf_op jit(solution)/shard_map/ppermute | solution.py:97
  51.7 6.9 %collective-permute-start.19 = (bf16[96,1024]{1,0:T(8,128)(2,1)S(1)}, bf16[96,1024]{1,0:T(8,128)(2,1)S(1)}, u32[]{:S(2)}, u32[]{:S(2)}) collective-permute-start(bf16[96,1024]{1,0:T(8,128)(2,1)S(1)} %get-tuple-element.97), channel_id=1, source_target_pairs={{0,8},{1,9},{2,10},{3,11},{4,12},{5,13},{6,14},{7,15},{8,0},{9,1},... | collective-permute-start | bytes 589832 | tf_op jit(solution)/shard_map/ppermute | solution.py:97
  53.6 6.5 %collective-permute-start.18 = (bf16[96,1024]{1,0:T(8,128)(2,1)S(1)}, bf16[96,1024]{1,0:T(8,128)(2,1)S(1)}, u32[]{:S(2)}, u32[]{:S(2)}) collective-permute-start(bf16[96,1024]{1,0:T(8,128)(2,1)S(1)} %get-tuple-element.98), channel_id=1, source_target_pairs={{0,16},{1,17},{2,18},{3,19},{4,20},{5,21},{6,22},{7,23},{8,24},{9,... | collective-permute-start | bytes 589832 | tf_op jit(solution)/shard_map/ppermute | solution.py:97
  54.2 6.4 %collective-permute-start.17 = (bf16[96,1024]{1,0:T(8,128)(2,1)S(1)}, bf16[96,1024]{1,0:T(8,128)(2,1)S(1)}, u32[]{:S(2)}, u32[]{:S(2)}) collective-permute-start(bf16[96,1024]{1,0:T(8,128)(2,1)S(1)} %get-tuple-element.99), channel_id=1, source_target_pairs={{0,8},{1,9},{2,10},{3,11},{4,12},{5,13},{6,14},{7,15},{8,0},{9,1},... | collective-permute-start | bytes 589832 | tf_op jit(solution)/shard_map/ppermute | solution.py:97
  56.5 7.9 %collective-permute-start.27 = (bf16[192,1024]{1,0:T(8,128)(2,1)S(1)}, bf16[192,1024]{1,0:T(8,128)(2,1)S(1)}, u32[]{:S(2)}, u32[]{:S(2)}) collective-permute-start(bf16[192,1024]{1,0:T(8,128)(2,1)S(1)} %fusion.2), channel_id=1, source_target_pairs={{1,2},{2,1},{5,6},{6,5},{9,10},{10,9},{13,14},{14,13},{17,18},{18,... | collective-permute-start | bytes 1179656 | tf_op jit(solution)/shard_map/ppermute | solution.py:97
  58.0 8.5 %collective-permute-start.26 = (bf16[192,1024]{1,0:T(8,128)(2,1)S(1)}, bf16[192,1024]{1,0:T(8,128)(2,1)S(1)}, u32[]{:S(2)}, u32[]{:S(2)}) collective-permute-start(bf16[192,1024]{1,0:T(8,128)(2,1)S(1)} %collective-permute-done.21), channel_id=1, source_target_pairs={{0,1},{1,0},{2,3},{3,2},{4,5},{5,4},{6,7},{7,6},{8,9},{9,8},{10,11... | collective-permute-start | bytes 1179656 | tf_op jit(solution)/shard_map/ppermute | solution.py:97
  61.1 6.3 %collective-permute-start.23 = (bf16[96,1024]{1,0:T(8,128)(2,1)S(1)}, bf16[96,1024]{1,0:T(8,128)(2,1)S(1)}, u32[]{:S(2)}, u32[]{:S(2)}) collective-permute-start(bf16[96,1024]{1,0:T(8,128)(2,1)S(1)} %get-tuple-element.94), channel_id=1, source_target_pairs={{0,16},{1,17},{2,18},{3,19},{4,20},{5,21},{6,22},{7,23},{8,24},{9,... | collective-permute-start | bytes 589832 | tf_op jit(solution)/shard_map/ppermute | solution.py:97
  62.3 6.2 %collective-permute-start.22 = (bf16[96,1024]{1,0:T(8,128)(2,1)S(1)}, bf16[96,1024]{1,0:T(8,128)(2,1)S(1)}, u32[]{:S(2)}, u32[]{:S(2)}) collective-permute-start(bf16[96,1024]{1,0:T(8,128)(2,1)S(1)} %get-tuple-element.95), channel_id=1, source_target_pairs={{0,8},{1,9},{2,10},{3,11},{4,12},{5,13},{6,14},{7,15},{8,0},{9,1},... | collective-permute-start | bytes 589832 | tf_op jit(solution)/shard_map/ppermute | solution.py:97
  63.1 6.4 %collective-permute-start.25 = (bf16[96,1024]{1,0:T(8,128)(2,1)S(1)}, bf16[96,1024]{1,0:T(8,128)(2,1)S(1)}, u32[]{:S(2)}, u32[]{:S(2)}) collective-permute-start(bf16[96,1024]{1,0:T(8,128)(2,1)S(1)} %get-tuple-element.92), channel_id=1, source_target_pairs={{0,16},{1,17},{2,18},{3,19},{4,20},{5,21},{6,22},{7,23},{8,24},{9,... | collective-permute-start | bytes 589832 | tf_op jit(solution)/shard_map/ppermute | solution.py:97
  64.3 6.3 %collective-permute-start.24 = (bf16[96,1024]{1,0:T(8,128)(2,1)S(1)}, bf16[96,1024]{1,0:T(8,128)(2,1)S(1)}, u32[]{:S(2)}, u32[]{:S(2)}) collective-permute-start(bf16[96,1024]{1,0:T(8,128)(2,1)S(1)} %get-tuple-element.93), channel_id=1, source_target_pairs={{0,8},{1,9},{2,10},{3,11},{4,12},{5,13},{6,14},{7,15},{8,0},{9,1},... | collective-permute-start | bytes 589832 | tf_op jit(solution)/shard_map/ppermute | solution.py:97
  71.4 10.6 %collective-permute-start.30 = (bf16[768,1024]{1,0:T(8,128)(2,1)S(1)}, bf16[768,1024]{1,0:T(8,128)(2,1)S(1)}, u32[]{:S(2)}, u32[]{:S(2)}) collective-permute-start(bf16[768,1024]{1,0:T(8,128)(2,1)S(1)} %select_dynamic-update-slice_fusion.6.refs_1_), channel_id=1, source_target_pairs={{0,4},{1,5},{2,6},{3,7},{4,0},{5,1},{6,2},{7,3},{8,12},{9,13},{10,... | collective-permute-start | bytes 4718600 | tf_op jit(solution)/shard_map/ppermute | solution.py:97
  74.3 7.3 %collective-permute-start.29 = (bf16[96,1024]{1,0:T(8,128)(2,1)S(1)}, bf16[96,1024]{1,0:T(8,128)(2,1)S(1)}, u32[]{:S(2)}, u32[]{:S(2)}) collective-permute-start(bf16[96,1024]{1,0:T(8,128)(2,1)S(1)} %get-tuple-element.90), channel_id=1, source_target_pairs={{0,16},{1,17},{2,18},{3,19},{4,20},{5,21},{6,22},{7,23},{8,24},{9,... | collective-permute-start | bytes 589832 | tf_op jit(solution)/shard_map/ppermute | solution.py:97
  75.0 7.0 %collective-permute-start.28 = (bf16[96,1024]{1,0:T(8,128)(2,1)S(1)}, bf16[96,1024]{1,0:T(8,128)(2,1)S(1)}, u32[]{:S(2)}, u32[]{:S(2)}) collective-permute-start(bf16[96,1024]{1,0:T(8,128)(2,1)S(1)} %get-tuple-element.91), channel_id=1, source_target_pairs={{0,8},{1,9},{2,10},{3,11},{4,12},{5,13},{6,14},{7,15},{8,0},{9,1},... | collective-permute-start | bytes 589832 | tf_op jit(solution)/shard_map/ppermute | solution.py:97
  82.4 6.2 %collective-permute-start.32 = (bf16[96,1024]{1,0:T(8,128)(2,1)S(1)}, bf16[96,1024]{1,0:T(8,128)(2,1)S(1)}, u32[]{:S(2)}, u32[]{:S(2)}) collective-permute-start(bf16[96,1024]{1,0:T(8,128)(2,1)S(1)} %get-tuple-element.88), channel_id=1, source_target_pairs={{0,16},{1,17},{2,18},{3,19},{4,20},{5,21},{6,22},{7,23},{8,24},{9,... | collective-permute-start | bytes 589832 | tf_op jit(solution)/shard_map/ppermute | solution.py:97
  83.9 5.9 %collective-permute-start.31 = (bf16[96,1024]{1,0:T(8,128)(2,1)S(1)}, bf16[96,1024]{1,0:T(8,128)(2,1)S(1)}, u32[]{:S(2)}, u32[]{:S(2)}) collective-permute-start(bf16[96,1024]{1,0:T(8,128)(2,1)S(1)} %get-tuple-element.89), channel_id=1, source_target_pairs={{0,8},{1,9},{2,10},{3,11},{4,12},{5,13},{6,14},{7,15},{8,0},{9,1},... | collective-permute-start | bytes 589832 | tf_op jit(solution)/shard_map/ppermute | solution.py:97
  (35 other events, 357.5 us)

commit v3 on v2

--- a/solution.py
+++ b/solution.py
@@ -20,7 +20,7 @@
     )
 
 
-ROWS = 256
+ROWS = 512
 
 
 def gram_rows_kernel(scale, _place, left, right, *rest):
@@ -48,7 +48,7 @@
         out_shape=jax.ShapeDtypeStruct((rows_all, columns), jnp.float32),
         grid_spec=grid,
         input_output_aliases={} if into is None else {3: 0},
-        compiler_params=pltpu.CompilerParams(vmem_limit_bytes=24 * 1024 * 1024),
+        compiler_params=pltpu.CompilerParams(vmem_limit_bytes=32 * 1024 * 1024),
         cost_estimate=pl.CostEstimate(
             flops=2 * depth * rows * columns,
             bytes_accessed=4 * rows * columns + 2 * depth * (rows + columns),
@@ -119,14 +119,10 @@
     def across(x):
         return go(x, lambda d, c: (d ^ 6, c))
 
-    def z1(x):
-        return go(x, lambda d, c: (d, c ^ 1))
-
-    def z2(x):
-        return go(x, lambda d, c: (d, c ^ 2))
-
-    def z_middle(x):
-        return go(x, lambda d, c: (d, 3 - c) if c in (1, 2) else None)
+    ring = (0, 1, 3, 2)
+
+    def along_z(x):
+        return go(x, lambda d, c: (d, ring[(ring.index(c) + 1) % 4]))
 
     def tie(*values):
         return lax.optimization_barrier(values)
@@ -157,56 +153,48 @@
                 pieces.append(lax.select_n(role, high, x1, y0, x1))
         return jnp.concatenate(pieces, axis=0)
 
-    inner = (z == 1) | (z == 2)
     scale = 1.0 / (tokens * n_ctx)
     rows_all = 2 * width
     mine_at = jnp.reshape(parity, (1,)).astype(jnp.int32)
     other_at = 1 - mine_at
 
     g0 = out_grads
-    g2, g1 = z2(g0), z1(g0)
+    g1 = along_z(g0)
     sums = squares(hidden_states)
     sums = sums + core(sums)
     sums = (sums + along_x(sums)) + (along_y(sums) + across(sums))
     e0 = send(g0)
     x0 = normalize(hidden_states, sums, norm_gain, width * n_dp)
-    *e0, x0 = tie(*e0, x0)
-    o0 = send(x0)
-    x1 = z1(x0)
-    g1_, g2_, g0_ = tie(g1, g2, g0)
-    g_ends, g_middle = z1(g2_), z_middle(g0_)
-    o0x, o0y, e0x, e0y, g1, g2, x0_ = tie(*o0, *e0, g1, g2, x0)
-    o0, e0 = (o0x, o0y), (e0x, e0y)
-    e1 = send(g1, e0)
-    x2 = z2(x0_)
-    e1x, e1y, g_ends, g_middle, g2_ = tie(*e1, g_ends, g_middle, g2)
-    e1 = (e1x, e1y)
-    e2 = send(g2_, e1)
-    e2x, e2y, x1, o0x, o0y = tie(*e2, x1, *o0)
-    e2, o0 = (e2x, e2y), (o0x, o0y)
-    g3 = jnp.where(inner, g_middle, g_ends)
-    e3, o1 = send(g3, e2), send(x1, o0)
-    x2, x0_ = tie(x2, x0_)
-    x_ends, x_middle = z1(x2), z_middle(x0_)
-    e3x, e3y, o1x, o1y, x2_ = tie(*e3, *o1, x2)
-    e3, o1 = (e3x, e3y), (o1x, o1y)
-    e4, o2 = send(g3, e3, last=True), send(x2_, o1)
-    e4x, e4y, o2x, o2y, x_ends, x_middle = tie(*e4, *o2, x_ends, x_middle)
-    e4, o2 = (e4x, e4y), (o2x, o2y)
-    x3 = jnp.where(inner, x_middle, x_ends)
-    o3 = send(x3, o2)
-    g_mine = assemble([g0, g1, g2, g3], [e0, e1, e2, e3, e4])
+    e0x, e0y = e0
+    x0, g1 = tie(x0, g1)
+    g2 = along_z(g1)
+    o0x, o0y = send(x0)
+    x1 = along_z(x0)
+    g3 = along_z(g2)
+    o0x, o0y, e0x, e0y, g1, g2 = tie(o0x, o0y, e0x, e0y, g1, g2)
+    e1x, e1y = send(g1, (e0x, e0y))
+    e1x, e1y, g2, x1 = tie(e1x, e1y, g2, x1)
+    x2 = along_z(x1)
+    e2x, e2y = send(g2, (e1x, e1y))
+    e2x, e2y, o0x, o0y, g3 = tie(e2x, e2y, o0x, o0y, g3)
+    e3x, e3y = send(g3, (e2x, e2y))
+    o1x, o1y = send(x1, (o0x, o0y))
+    e3x, e3y, o1x, o1y, x2 = tie(e3x, e3y, o1x, o1y, x2)
+    x3 = along_z(x2)
+    e4x, e4y = send(g3, (e3x, e3y), last=True)
+    o2x, o2y = send(x2, (o1x, o1y))
+    e4x, e4y, o2x, o2y, x3, g1, g2, g3 = tie(e4x, e4y, o2x, o2y, x3, g1, g2, g3)
+    o3x, o3y = send(x3, (o2x, o2y))
+    g_mine = assemble([g0, g1, g2, g3], [(e0x, e0y), (e1x, e1y), (e2x, e2y), (e3x, e3y), (e4x, e4y)])
     g_other = core(g_mine)
     g_column = jnp.concatenate([g0, g1, g2, g3], axis=0)
     g_factor = gram_rows(g_mine, g_column, mine_at, scale, rows_all)
-    o3x, o3y, g_factor, g_other = tie(*o3, g_factor, g_other)
-    o3 = (o3x, o3y)
-    o4 = send(x3, o3, last=True)
+    o3x, o3y, g_factor, x0, x1, x2, x3, g_other = tie(o3x, o3y, g_factor, x0, x1, x2, x3, g_other)
+    o4x, o4y = send(x3, (o3x, o3y), last=True)
     g_factor = gram_rows(g_other, g_column, other_at, scale, rows_all, g_factor)
     x_column = jnp.concatenate([x0, x1, x2, x3], axis=0)
-    o4x, o4y, g_factor, x_column = tie(*o4, g_factor, x_column)
-    o4 = (o4x, o4y)
-    x_mine = assemble([x0, x1, x2, x3], [o0, o1, o2, o3, o4])
+    o4x, o4y, g_factor, x_column = tie(o4x, o4y, g_factor, x_column)
+    x_mine = assemble([x0, x1, x2, x3], [(o0x, o0y), (o1x, o1y), (o2x, o2y), (o3x, o3y), (o4x, o4y)])
     x_other = core(x_mine)
     a_factor = gram_rows(x_mine, x_column, mine_at, scale, rows_all)
     a_factor = gram_rows(x_other, x_column, other_at, scale, rows_all, a_factor)

time: 99.4 us -> 96 us (0.966)
  starting transfers between devices: 43.8 us -> 38.8 us
  Pallas kernels: 15.8 us -> 14 us
  local copies, waits for them, and re-layouts: 1.51 us -> 3.18 us
    ppermute x34 -> x32, starting transfers between devices: 43.8 us -> 38.8 us  [swap(): return lax.ppermute(x, AXES, pairs)]
    pallas_call x4, Pallas kernels: 15.8 us -> 14 us  [gram_rows(): pl.pallas_call(lambda *refs: gram_rows_kernel(scale, *refs), out_shape=ja...]
    unnamed x66 -> x77, local copies, waits for them, and re-layouts: 0.44 us -> 2.07 us
    select_n x8, other arithmetic: 1.21 us -> 2.8 us  [send(): high = jnp.where(root, high, back[0])]
    select_n x2 -> x0, other arithmetic: 1.19 us -> none  [the longest x1 1.14 us: square_plane(): x3 = jnp.where(inner, x_middle, x_ends)]
    ppermute x34 -> x32, waiting for transfers between devices: 27.8 us -> 28.7 us  [swap(): return lax.ppermute(x, AXES, pairs)]
    unnamed x10 -> x12, other arithmetic: 2.27 us -> 2.35 us
  transfers between devices with their start and end apart: 34 -> 32, of which waited for: 20 -> 16; matrix products, arithmetic and copies ran while one was open for 7% -> 8% of each run, Pallas kernels for 12% -> 11%
where the time goes in v3:
time: 96 us; the launch traced here: 94.4 us
  starting transfers between devices  38.8 us (40%)
  waiting for transfers between devices  28.7 us (30%)
  Pallas kernels  14 us (15%)
  other arithmetic  8.51 us (9%)
  local copies, waits for them, and re-layouts  3.18 us (3%)
  between operations  1.17 us (1%)
    ppermute x32, starting transfers between devices, swap(): return lax.ppermute(x, AXES, pairs)  38.8 us
    ppermute x32, waiting for transfers between devices, swap(): return lax.ppermute(x, AXES, pairs)  28.7 us
    pallas_call x4, Pallas kernels, gram_rows(): pl.pallas_call(lambda *refs: gram_rows_kernel(scale, *refs), out_shape=ja...  14 us
    select_n x8, other arithmetic, send(): high = jnp.where(root, high, back[0])  2.8 us
    unnamed x12, other arithmetic  2.35 us
    unnamed x77, local copies, waits for them, and re-layouts  2.07 us
  transfers between devices with their start and end apart: 32, of which 16 were waited for; matrix products, arithmetic and copies ran while one was open for 8% of the time, Pallas kernels for 11%

profile of v3, /device:TPU:0, one launch (start us, length us, event | category | flops | bytes accessed | tf_op | source)
XLA Modules:
  0.0 94.4 jit_solution(5237211075857846762)
XLA Ops:
  2.3 2.6 %collective-permute-start.4 = (bf16[192,1024]{1,0:T(8,128)(2,1)}, bf16[192,1024]{1,0:T(8,128)(2,1)S(1)}, u32[]{:S(2)}, u32[]{:S(2)}) collective-permute-start(bf16[192,1024]{1,0:T(8,128)(2,1)} %param.4), channel_id=1, source_target_pairs={{0,1},{1,3},{2,0},{3,2},{4,5},{5,7},{6,4},{7,6},{8,9},{9,11},{10,8... | collective-permute-start | bytes 1179656 | tf_op jit(solution)/shard_map/ppermute | solution.py:97
  4.9 2.4 %collective-permute-start.3 = (f32[192,1]{0,1:T(1,128)S(1)}, f32[192,1]{0,1:T(1,128)S(1)}, u32[]{:S(2)}, u32[]{:S(2)}) collective-permute-start(f32[192,1]{0,1:T(1,128)S(1)} %add.24), channel_id=1, source_target_pairs={{0,24},{1,25},{2,26},{3,27},{4,28},{5,29},{6,30},{7,31},{8,16},{9,... | collective-permute-start | bytes 2312 | tf_op jit(solution)/shard_map/ppermute | solution.py:97
  9.5 1.6 %collective-permute-start.8 = (bf16[96,1024]{1,0:T(8,128)(2,1)S(1)}, bf16[96,1024]{1,0:T(8,128)(2,1)S(1)}, u32[]{:S(2)}, u32[]{:S(2)}) collective-permute-start(bf16[96,1024]{1,0:T(8,128)(2,1)S(1)} %get-tuple-element.102), channel_id=1, source_target_pairs={{0,16},{1,17},{2,18},{3,19},{4,20},{5,21},{6,22},{7,23},{8,24},{9,... | collective-permute-start | bytes 589832 | tf_op jit(solution)/shard_map/ppermute | solution.py:97
  11.8 1.5 %collective-permute-start.7 = (bf16[96,1024]{1,0:T(8,128)(2,1)S(1)}, bf16[96,1024]{1,0:T(8,128)(2,1)S(1)}, u32[]{:S(2)}, u32[]{:S(2)}) collective-permute-start(bf16[96,1024]{1,0:T(8,128)(2,1)S(1)} %get-tuple-element.103), channel_id=1, source_target_pairs={{0,8},{1,9},{2,10},{3,11},{4,12},{5,13},{6,14},{7,15},{8,0},{9,1},... | collective-permute-start | bytes 589832 | tf_op jit(solution)/shard_map/ppermute | solution.py:97
  13.3 1.2 %fusion.2 = bf16[192,1024]{1,0:T(8,128)(2,1)S(1)} fusion(bf16[192,1024]{1,0:T(8,128)(2,1)} %param.3, f32[1024]{0:T(1024)S(1)} %bitcast.4, f32[192]{0:T(256)S(1)} %bitcast.7), kind=kLoop, calls=%fused_computation.5 | loop fusion | flops 786432 | bytes 791296 | tf_op jit(solution)/shard_map/convert_element_type | solution.py:64
  14.4 1.4 %collective-permute-done.4 = bf16[192,1024]{1,0:T(8,128)(2,1)S(1)} collective-permute-done((bf16[192,1024]{1,0:T(8,128)(2,1)}, bf16[192,1024]{1,0:T(8,128)(2,1)S(1)}, u32[]{:S(2)}, u32[]{:S(2)}) %collective-permute-start.4) | collective-permute-done | bytes 393248 | tf_op jit(solution)/shard_map/ppermute | solution.py:97
  15.9 1.2 %collective-permute-start.9 = (bf16[192,1024]{1,0:T(8,128)(2,1)S(1)}, bf16[192,1024]{1,0:T(8,128)(2,1)S(1)}, u32[]{:S(2)}, u32[]{:S(2)}) collective-permute-start(bf16[192,1024]{1,0:T(8,128)(2,1)S(1)} %collective-permute-done.4), channel_id=1, source_target_pairs={{0,1},{1,3},{2,0},{3,2},{4,5},{5,7},{6,4},{7,6},{8,9},{9,11},{10,8... | collective-permute-start | bytes 1179656 | tf_op jit(solution)/shard_map/ppermute | solution.py:97
  17.1 1.3 %collective-permute-start.6 = (bf16[96,1024]{1,0:T(8,128)(2,1)S(1)}, bf16[96,1024]{1,0:T(8,128)(2,1)S(1)}, u32[]{:S(2)}, u32[]{:S(2)}) collective-permute-start(bf16[96,1024]{1,0:T(8,128)(2,1)S(1)} %get-tuple-element.104), channel_id=1, source_target_pairs={{0,16},{1,17},{2,18},{3,19},{4,20},{5,21},{6,22},{7,23},{8,24},{9,... | collective-permute-start | bytes 589832 | tf_op jit(solution)/shard_map/ppermute | solution.py:97
  18.4 1.5 %collective-permute-start.5 = (bf16[96,1024]{1,0:T(8,128)(2,1)S(1)}, bf16[96,1024]{1,0:T(8,128)(2,1)S(1)}, u32[]{:S(2)}, u32[]{:S(2)}) collective-permute-start(bf16[96,1024]{1,0:T(8,128)(2,1)S(1)} %get-tuple-element.105), channel_id=1, source_target_pairs={{0,8},{1,9},{2,10},{3,11},{4,12},{5,13},{6,14},{7,15},{8,0},{9,1},... | collective-permute-start | bytes 589832 | tf_op jit(solution)/shard_map/ppermute | solution.py:97
  19.9 3.3 %collective-permute-start.12 = (bf16[192,1024]{1,0:T(8,128)(2,1)S(1)}, bf16[192,1024]{1,0:T(8,128)(2,1)S(1)}, u32[]{:S(2)}, u32[]{:S(2)}) collective-permute-start(bf16[192,1024]{1,0:T(8,128)(2,1)S(1)} %fusion.2), channel_id=1, source_target_pairs={{0,1},{1,3},{2,0},{3,2},{4,5},{5,7},{6,4},{7,6},{8,9},{9,11},{10,8... | collective-permute-start | bytes 1179656 | tf_op jit(solution)/shard_map/ppermute | solution.py:97
  24.4 4.4 %collective-permute-done.9 = bf16[192,1024]{1,0:T(8,128)(2,1)S(1)} collective-permute-done((bf16[192,1024]{1,0:T(8,128)(2,1)S(1)}, bf16[192,1024]{1,0:T(8,128)(2,1)S(1)}, u32[]{:S(2)}, u32[]{:S(2)}) %collective-permute-start.9) | collective-permute-done | bytes 393248 | tf_op jit(solution)/shard_map/ppermute | solution.py:97
  28.8 1.7 %collective-permute-start.11 = (bf16[96,1024]{1,0:T(8,128)(2,1)S(1)}, bf16[96,1024]{1,0:T(8,128)(2,1)S(1)}, u32[]{:S(2)}, u32[]{:S(2)}) collective-permute-start(bf16[96,1024]{1,0:T(8,128)(2,1)S(1)} %get-tuple-element.100), channel_id=1, source_target_pairs={{0,16},{1,17},{2,18},{3,19},{4,20},{5,21},{6,22},{7,23},{8,24},{9,... | collective-permute-start | bytes 589832 | tf_op jit(solution)/shard_map/ppermute | solution.py:97
  30.5 1.5 %collective-permute-start.10 = (bf16[96,1024]{1,0:T(8,128)(2,1)S(1)}, bf16[96,1024]{1,0:T(8,128)(2,1)S(1)}, u32[]{:S(2)}, u32[]{:S(2)}) collective-permute-start(bf16[96,1024]{1,0:T(8,128)(2,1)S(1)} %get-tuple-element.101), channel_id=1, source_target_pairs={{0,8},{1,9},{2,10},{3,11},{4,12},{5,13},{6,14},{7,15},{8,0},{9,1},... | collective-permute-start | bytes 589832 | tf_op jit(solution)/shard_map/ppermute | solution.py:97
  32.8 4.4 %collective-permute-done.12 = bf16[192,1024]{1,0:T(8,128)(2,1)S(1)} collective-permute-done((bf16[192,1024]{1,0:T(8,128)(2,1)S(1)}, bf16[192,1024]{1,0:T(8,128)(2,1)S(1)}, u32[]{:S(2)}, u32[]{:S(2)}) %collective-permute-start.12) | collective-permute-done | bytes 393248 | tf_op jit(solution)/shard_map/ppermute | solution.py:97
  37.9 1.6 %collective-permute-start.14 = (bf16[96,1024]{1,0:T(8,128)(2,1)S(1)}, bf16[96,1024]{1,0:T(8,128)(2,1)S(1)}, u32[]{:S(2)}, u32[]{:S(2)}) collective-permute-start(bf16[96,1024]{1,0:T(8,128)(2,1)S(1)} %get-tuple-element.98), channel_id=1, source_target_pairs={{0,16},{1,17},{2,18},{3,19},{4,20},{5,21},{6,22},{7,23},{8,24},{9,... | collective-permute-start | bytes 589832 | tf_op jit(solution)/shard_map/ppermute | solution.py:97
  39.5 1.5 %collective-permute-start.13 = (bf16[96,1024]{1,0:T(8,128)(2,1)S(1)}, bf16[96,1024]{1,0:T(8,128)(2,1)S(1)}, u32[]{:S(2)}, u32[]{:S(2)}) collective-permute-start(bf16[96,1024]{1,0:T(8,128)(2,1)S(1)} %get-tuple-element.99), channel_id=1, source_target_pairs={{0,8},{1,9},{2,10},{3,11},{4,12},{5,13},{6,14},{7,15},{8,0},{9,1},... | collective-permute-start | bytes 589832 | tf_op jit(solution)/shard_map/ppermute | solution.py:97
  41.8 3.8 %collective-permute-done.15 = bf16[192,1024]{1,0:T(8,128)(2,1)S(1)} collective-permute-done((bf16[192,1024]{1,0:T(8,128)(2,1)S(1)}, bf16[192,1024]{1,0:T(8,128)(2,1)S(1)}, u32[]{:S(2)}, u32[]{:S(2)}) %collective-permute-start.15) | collective-permute-done | bytes 393248 | tf_op jit(solution)/shard_map/ppermute | solution.py:97
  45.7 1.7 %collective-permute-start.19 = (bf16[96,1024]{1,0:T(8,128)(2,1)S(1)}, bf16[96,1024]{1,0:T(8,128)(2,1)S(1)}, u32[]{:S(2)}, u32[]{:S(2)}) collective-permute-start(bf16[96,1024]{1,0:T(8,128)(2,1)S(1)} %get-tuple-element.94), channel_id=1, source_target_pairs={{0,16},{1,17},{2,18},{3,19},{4,20},{5,21},{6,22},{7,23},{8,24},{9,... | collective-permute-start | bytes 589832 | tf_op jit(solution)/shard_map/ppermute | solution.py:97
  47.4 1.5 %collective-permute-start.18 = (bf16[96,1024]{1,0:T(8,128)(2,1)S(1)}, bf16[96,1024]{1,0:T(8,128)(2,1)S(1)}, u32[]{:S(2)}, u32[]{:S(2)}) collective-permute-start(bf16[96,1024]{1,0:T(8,128)(2,1)S(1)} %get-tuple-element.95), channel_id=1, source_target_pairs={{0,8},{1,9},{2,10},{3,11},{4,12},{5,13},{6,14},{7,15},{8,0},{9,1},... | collective-permute-start | bytes 589832 | tf_op jit(solution)/shard_map/ppermute | solution.py:97
  50.0 1.2 %broadcast_select_fusion.4 = (bf16[96,1024]{1,0:T(8,128)(2,1)S(1)}, bf16[96,1024]{1,0:T(8,128)(2,1)S(1)}, bf16[768,1024]{1,0:T(8,128)(2,1)S(1)}) fusion(bf16[96,1024]{1,0:T(8,128)(2,1)} %copy-done.14, pred[]{:T(512)S(6)} %eq.5, bf16[192,1024]{1,0:T(8,128)(2,1)S(1)} %collective-permute-done.15, bf16[96,1024]{1,0:T(8,128)(2,1)} %copy-done.20, ...), kind=kLoop, calls=%fused_computation.36 | loop fusion | flops 491520 | bytes 1966084 | tf_op jit(solution)/shard_map/jit(_where)/select_n | solution.py:137
  52.6 2.1 %collective-permute-done.18 = bf16[96,1024]{1,0:T(8,128)(2,1)S(1)} collective-permute-done((bf16[96,1024]{1,0:T(8,128)(2,1)S(1)}, bf16[96,1024]{1,0:T(8,128)(2,1)S(1)}, u32[]{:S(2)}, u32[]{:S(2)}) %collective-permute-start.18) | collective-permute-done | bytes 196640 | tf_op jit(solution)/shard_map/ppermute | solution.py:97
  54.7 2.2 %collective-permute-done.17 = bf16[96,1024]{1,0:T(8,128)(2,1)S(1)} collective-permute-done((bf16[96,1024]{1,0:T(8,128)(2,1)S(1)}, bf16[96,1024]{1,0:T(8,128)(2,1)S(1)}, u32[]{:S(2)}, u32[]{:S(2)}) %collective-permute-start.17) | collective-permute-done | bytes 196640 | tf_op jit(solution)/shard_map/ppermute | solution.py:97
  58.6 1.5 %collective-permute-start.24 = (bf16[96,1024]{1,0:T(8,128)(2,1)S(1)}, bf16[96,1024]{1,0:T(8,128)(2,1)S(1)}, u32[]{:S(2)}, u32[]{:S(2)}) collective-permute-start(bf16[96,1024]{1,0:T(8,128)(2,1)S(1)} %get-tuple-element.90), channel_id=1, source_target_pairs={{0,16},{1,17},{2,18},{3,19},{4,20},{5,21},{6,22},{7,23},{8,24},{9,... | collective-permute-start | bytes 589832 | tf_op jit(solution)/shard_map/ppermute | solution.py:97
  61.4 1.4 %collective-permute-start.21 = (bf16[96,1024]{1,0:T(8,128)(2,1)S(1)}, bf16[96,1024]{1,0:T(8,128)(2,1)S(1)}, u32[]{:S(2)}, u32[]{:S(2)}) collective-permute-start(bf16[96,1024]{1,0:T(8,128)(2,1)S(1)} %get-tuple-element.93), channel_id=1, source_target_pairs={{0,8},{1,9},{2,10},{3,11},{4,12},{5,13},{6,14},{7,15},{8,0},{9,1},... | collective-permute-start | bytes 589832 | tf_op jit(solution)/shard_map/ppermute | solution.py:97
  62.8 2.0 %collective-permute-done.24 = bf16[96,1024]{1,0:T(8,128)(2,1)S(1)} collective-permute-done((bf16[96,1024]{1,0:T(8,128)(2,1)S(1)}, bf16[96,1024]{1,0:T(8,128)(2,1)S(1)}, u32[]{:S(2)}, u32[]{:S(2)}) %collective-permute-start.24) | collective-permute-done | bytes 196640 | tf_op jit(solution)/shard_map/ppermute | solution.py:97
  65.7 1.2 %collective-permute-done.22 = bf16[96,1024]{1,0:T(8,128)(2,1)S(1)} collective-permute-done((bf16[96,1024]{1,0:T(8,128)(2,1)S(1)}, bf16[96,1024]{1,0:T(8,128)(2,1)S(1)}, u32[]{:S(2)}, u32[]{:S(2)}) %collective-permute-start.22) | collective-permute-done | bytes 196640 | tf_op jit(solution)/shard_map/ppermute | solution.py:97
  72.2 1.2 %collective-permute-start.26 = (bf16[96,1024]{1,0:T(8,128)(2,1)S(1)}, bf16[96,1024]{1,0:T(8,128)(2,1)S(1)}, u32[]{:S(2)}, u32[]{:S(2)}) collective-permute-start(bf16[96,1024]{1,0:T(8,128)(2,1)S(1)} %get-tuple-element.89), channel_id=1, source_target_pairs={{0,8},{1,9},{2,10},{3,11},{4,12},{5,13},{6,14},{7,15},{8,0},{9,1},... | collective-permute-start | bytes 589832 | tf_op jit(solution)/shard_map/ppermute | solution.py:97
  73.6 3.5 %shard_map.50.refs_3_ = f32[2048,1024]{1,0:T(8,128)} custom-call(s32[1]{0:T(128)} %bitcast.refs_0_, bf16[768,1024]{1,0:T(8,128)(2,1)S(1)} %select_dynamic-update-slice_fusion.8.refs_1_, bf16[768,1024]{1,0:T(8,128)(2,1)S(1)} %constant_dynamic-update-slice_fusion.refs_2_), custom_call_target="tpu_custom_call" | custom-call | flops 1610612736 | bytes 7340032 | tf_op jit(solution)/shard_map/pallas_call | solution.py:46
  77.1 1.3 %collective-permute-done.27 = bf16[96,1024]{1,0:T(8,128)(2,1)S(1)} collective-permute-done((bf16[96,1024]{1,0:T(8,128)(2,1)S(1)}, bf16[96,1024]{1,0:T(8,128)(2,1)S(1)}, u32[]{:S(2)}, u32[]{:S(2)}) %collective-permute-start.27) | collective-permute-done | bytes 196640 | tf_op jit(solution)/shard_map/ppermute | solution.py:97
  82.0 3.5 %shard_map.51 = f32[2048,1024]{1,0:T(8,128)} custom-call(s32[1]{0:T(128)S(6)} %sub.7.refs_0_, bf16[768,1024]{1,0:T(8,128)(2,1)S(1)} %collective-permute-done.28.refs_1_, bf16[768,1024]{1,0:T(8,128)(2,1)S(1)} %constant_dynamic-update-slice_fusion.refs_2_, f32[2048,1024]{1,0:T(8,128)} %shard_map.50.refs_3_), custom_call_target="tpu_custom_call", output_to_operand_aliasing={{}: (3, {})} | custom-call | flops 1610612736 | bytes 7340032 | tf_op jit(solution)/shard_map/pallas_call | solution.py:46
  87.4 3.5 %shard_map.52.refs_3_ = f32[2048,1024]{1,0:T(8,128)} custom-call(s32[1]{0:T(128)} %bitcast.refs_0_, bf16[768,1024]{1,0:T(8,128)(2,1)S(1)} %select_dynamic-update-slice_fusion.refs_1_, bf16[768,1024]{1,0:T(8,128)(2,1)S(1)} %pad_maximum_fusion.refs_2_), custom_call_target="tpu_custom_call" | custom-call | flops 1610612736 | bytes 7340032 | tf_op jit(solution)/shard_map/pallas_call | solution.py:46
  90.9 3.5 %shard_map.53 = f32[2048,1024]{1,0:T(8,128)} custom-call(s32[1]{0:T(128)S(6)} %sub.7.refs_0_, bf16[768,1024]{1,0:T(8,128)(2,1)S(1)} %collective-permute-done.31.refs_1_, bf16[768,1024]{1,0:T(8,128)(2,1)S(1)} %pad_maximum_fusion.refs_2_, f32[2048,1024]{1,0:T(8,128)} %shard_map.52.refs_3_), custom_call_target="tpu_custom_call", output_to_operand_aliasing={{}: (3, {})} | custom-call | flops 1610612736 | bytes 7340032 | tf_op jit(solution)/shard_map/pallas_call | solution.py:46
  (144 shorter events, 25.0 us)
Async XLA Ops:
  1.8 3.2 %collective-permute-start = (f32[192,1]{0,1:T(1,128)S(1)}, f32[192,1]{0,1:T(1,128)S(1)}, u32[]{:S(2)}, u32[]{:S(2)}) collective-permute-start(f32[192,1]{0,1:T(1,128)S(1)} %bitcast.5), channel_id=1, source_target_pairs={{0,4},{1,5},{2,6},{3,7},{4,0},{5,1},{6,2},{7,3},{8,12},{9,13},{10,... | collective-permute-start | bytes 2312 | tf_op jit(solution)/shard_map/ppermute | solution.py:97
  2.3 13.6 %collective-permute-start.4 = (bf16[192,1024]{1,0:T(8,128)(2,1)}, bf16[192,1024]{1,0:T(8,128)(2,1)S(1)}, u32[]{:S(2)}, u32[]{:S(2)}) collective-permute-start(bf16[192,1024]{1,0:T(8,128)(2,1)} %param.4), channel_id=1, source_target_pairs={{0,1},{1,3},{2,0},{3,2},{4,5},{5,7},{6,4},{7,6},{8,9},{9,11},{10,8... | collective-permute-start | bytes 1179656 | tf_op jit(solution)/shard_map/ppermute | solution.py:97
  4.9 6.8 %collective-permute-start.3 = (f32[192,1]{0,1:T(1,128)S(1)}, f32[192,1]{0,1:T(1,128)S(1)}, u32[]{:S(2)}, u32[]{:S(2)}) collective-permute-start(f32[192,1]{0,1:T(1,128)S(1)} %add.24), channel_id=1, source_target_pairs={{0,24},{1,25},{2,26},{3,27},{4,28},{5,29},{6,30},{7,31},{8,16},{9,... | collective-permute-start | bytes 2312 | tf_op jit(solution)/shard_map/ppermute | solution.py:97
  7.4 5.9 %collective-permute-start.2 = (f32[192,1]{0,1:T(1,128)S(1)}, f32[192,1]{0,1:T(1,128)S(1)}, u32[]{:S(2)}, u32[]{:S(2)}) collective-permute-start(f32[192,1]{0,1:T(1,128)S(1)} %add.24), channel_id=1, source_target_pairs={{0,16},{1,17},{2,18},{3,19},{4,20},{5,21},{6,22},{7,23},{8,24},{9,... | collective-permute-start | bytes 2312 | tf_op jit(solution)/shard_map/ppermute | solution.py:97
  7.9 5.4 %collective-permute-start.1 = (f32[192,1]{0,1:T(1,128)S(1)}, f32[192,1]{0,1:T(1,128)S(1)}, u32[]{:S(2)}, u32[]{:S(2)}) collective-permute-start(f32[192,1]{0,1:T(1,128)S(1)} %add.24), channel_id=1, source_target_pairs={{0,8},{1,9},{2,10},{3,11},{4,12},{5,13},{6,14},{7,15},{8,0},{9,1},... | collective-permute-start | bytes 2312 | tf_op jit(solution)/shard_map/ppermute | solution.py:97
  9.5 10.5 %collective-permute-start.8 = (bf16[96,1024]{1,0:T(8,128)(2,1)S(1)}, bf16[96,1024]{1,0:T(8,128)(2,1)S(1)}, u32[]{:S(2)}, u32[]{:S(2)}) collective-permute-start(bf16[96,1024]{1,0:T(8,128)(2,1)S(1)} %get-tuple-element.102), channel_id=1, source_target_pairs={{0,16},{1,17},{2,18},{3,19},{4,20},{5,21},{6,22},{7,23},{8,24},{9,... | collective-permute-start | bytes 589832 | tf_op jit(solution)/shard_map/ppermute | solution.py:97
  11.8 11.5 %collective-permute-start.7 = (bf16[96,1024]{1,0:T(8,128)(2,1)S(1)}, bf16[96,1024]{1,0:T(8,128)(2,1)S(1)}, u32[]{:S(2)}, u32[]{:S(2)}) collective-permute-start(bf16[96,1024]{1,0:T(8,128)(2,1)S(1)} %get-tuple-element.103), channel_id=1, source_target_pairs={{0,8},{1,9},{2,10},{3,11},{4,12},{5,13},{6,14},{7,15},{8,0},{9,1},... | collective-permute-start | bytes 589832 | tf_op jit(solution)/shard_map/ppermute | solution.py:97
  15.9 12.9 %collective-permute-start.9 = (bf16[192,1024]{1,0:T(8,128)(2,1)S(1)}, bf16[192,1024]{1,0:T(8,128)(2,1)S(1)}, u32[]{:S(2)}, u32[]{:S(2)}) collective-permute-start(bf16[192,1024]{1,0:T(8,128)(2,1)S(1)} %collective-permute-done.4), channel_id=1, source_target_pairs={{0,1},{1,3},{2,0},{3,2},{4,5},{5,7},{6,4},{7,6},{8,9},{9,11},{10,8... | collective-permute-start | bytes 1179656 | tf_op jit(solution)/shard_map/ppermute | solution.py:97
  17.1 6.1 %collective-permute-start.6 = (bf16[96,1024]{1,0:T(8,128)(2,1)S(1)}, bf16[96,1024]{1,0:T(8,128)(2,1)S(1)}, u32[]{:S(2)}, u32[]{:S(2)}) collective-permute-start(bf16[96,1024]{1,0:T(8,128)(2,1)S(1)} %get-tuple-element.104), channel_id=1, source_target_pairs={{0,16},{1,17},{2,18},{3,19},{4,20},{5,21},{6,22},{7,23},{8,24},{9,... | collective-permute-start | bytes 589832 | tf_op jit(solution)/shard_map/ppermute | solution.py:97
  18.4 5.9 %collective-permute-start.5 = (bf16[96,1024]{1,0:T(8,128)(2,1)S(1)}, bf16[96,1024]{1,0:T(8,128)(2,1)S(1)}, u32[]{:S(2)}, u32[]{:S(2)}) collective-permute-start(bf16[96,1024]{1,0:T(8,128)(2,1)S(1)} %get-tuple-element.105), channel_id=1, source_target_pairs={{0,8},{1,9},{2,10},{3,11},{4,12},{5,13},{6,14},{7,15},{8,0},{9,1},... | collective-permute-start | bytes 589832 | tf_op jit(solution)/shard_map/ppermute | solution.py:97
  19.9 17.3 %collective-permute-start.12 = (bf16[192,1024]{1,0:T(8,128)(2,1)S(1)}, bf16[192,1024]{1,0:T(8,128)(2,1)S(1)}, u32[]{:S(2)}, u32[]{:S(2)}) collective-permute-start(bf16[192,1024]{1,0:T(8,128)(2,1)S(1)} %fusion.2), channel_id=1, source_target_pairs={{0,1},{1,3},{2,0},{3,2},{4,5},{5,7},{6,4},{7,6},{8,9},{9,11},{10,8... | collective-permute-start | bytes 1179656 | tf_op jit(solution)/shard_map/ppermute | solution.py:97
  28.8 8.4 %collective-permute-start.11 = (bf16[96,1024]{1,0:T(8,128)(2,1)S(1)}, bf16[96,1024]{1,0:T(8,128)(2,1)S(1)}, u32[]{:S(2)}, u32[]{:S(2)}) collective-permute-start(bf16[96,1024]{1,0:T(8,128)(2,1)S(1)} %get-tuple-element.100), channel_id=1, source_target_pairs={{0,16},{1,17},{2,18},{3,19},{4,20},{5,21},{6,22},{7,23},{8,24},{9,... | collective-permute-start | bytes 589832 | tf_op jit(solution)/shard_map/ppermute | solution.py:97
  30.5 6.7 %collective-permute-start.10 = (bf16[96,1024]{1,0:T(8,128)(2,1)S(1)}, bf16[96,1024]{1,0:T(8,128)(2,1)S(1)}, u32[]{:S(2)}, u32[]{:S(2)}) collective-permute-start(bf16[96,1024]{1,0:T(8,128)(2,1)S(1)} %get-tuple-element.101), channel_id=1, source_target_pairs={{0,8},{1,9},{2,10},{3,11},{4,12},{5,13},{6,14},{7,15},{8,0},{9,1},... | collective-permute-start | bytes 589832 | tf_op jit(solution)/shard_map/ppermute | solution.py:97
  32.0 13.6 %collective-permute-start.15 = (bf16[192,1024]{1,0:T(8,128)(2,1)S(1)}, bf16[192,1024]{1,0:T(8,128)(2,1)S(1)}, u32[]{:S(2)}, u32[]{:S(2)}) collective-permute-start(bf16[192,1024]{1,0:T(8,128)(2,1)S(1)} %collective-permute-done.9), channel_id=1, source_target_pairs={{0,1},{1,3},{2,0},{3,2},{4,5},{5,7},{6,4},{7,6},{8,9},{9,11},{10,8... | collective-permute-start | bytes 1179656 | tf_op jit(solution)/shard_map/ppermute | solution.py:97
  37.9 7.7 %collective-permute-start.14 = (bf16[96,1024]{1,0:T(8,128)(2,1)S(1)}, bf16[96,1024]{1,0:T(8,128)(2,1)S(1)}, u32[]{:S(2)}, u32[]{:S(2)}) collective-permute-start(bf16[96,1024]{1,0:T(8,128)(2,1)S(1)} %get-tuple-element.98), channel_id=1, source_target_pairs={{0,16},{1,17},{2,18},{3,19},{4,20},{5,21},{6,22},{7,23},{8,24},{9,... | collective-permute-start | bytes 589832 | tf_op jit(solution)/shard_map/ppermute | solution.py:97
  39.5 6.1 %collective-permute-start.13 = (bf16[96,1024]{1,0:T(8,128)(2,1)S(1)}, bf16[96,1024]{1,0:T(8,128)(2,1)S(1)}, u32[]{:S(2)}, u32[]{:S(2)}) collective-permute-start(bf16[96,1024]{1,0:T(8,128)(2,1)S(1)} %get-tuple-element.99), channel_id=1, source_target_pairs={{0,8},{1,9},{2,10},{3,11},{4,12},{5,13},{6,14},{7,15},{8,0},{9,1},... | collective-permute-start | bytes 589832 | tf_op jit(solution)/shard_map/ppermute | solution.py:97
  41.0 13.7 %collective-permute-start.20 = (bf16[192,1024]{1,0:T(8,128)(2,1)S(1)}, bf16[192,1024]{1,0:T(8,128)(2,1)S(1)}, u32[]{:S(2)}, u32[]{:S(2)}) collective-permute-start(bf16[192,1024]{1,0:T(8,128)(2,1)S(1)} %collective-permute-done.12), channel_id=1, source_target_pairs={{0,1},{1,3},{2,0},{3,2},{4,5},{5,7},{6,4},{7,6},{8,9},{9,11},{10,8... | collective-permute-start | bytes 1179656 | tf_op jit(solution)/shard_map/ppermute | solution.py:97
  45.7 6.9 %collective-permute-start.19 = (bf16[96,1024]{1,0:T(8,128)(2,1)S(1)}, bf16[96,1024]{1,0:T(8,128)(2,1)S(1)}, u32[]{:S(2)}, u32[]{:S(2)}) collective-permute-start(bf16[96,1024]{1,0:T(8,128)(2,1)S(1)} %get-tuple-element.94), channel_id=1, source_target_pairs={{0,16},{1,17},{2,18},{3,19},{4,20},{5,21},{6,22},{7,23},{8,24},{9,... | collective-permute-start | bytes 589832 | tf_op jit(solution)/shard_map/ppermute | solution.py:97
  47.4 7.3 %collective-permute-start.18 = (bf16[96,1024]{1,0:T(8,128)(2,1)S(1)}, bf16[96,1024]{1,0:T(8,128)(2,1)S(1)}, u32[]{:S(2)}, u32[]{:S(2)}) collective-permute-start(bf16[96,1024]{1,0:T(8,128)(2,1)S(1)} %get-tuple-element.95), channel_id=1, source_target_pairs={{0,8},{1,9},{2,10},{3,11},{4,12},{5,13},{6,14},{7,15},{8,0},{9,1},... | collective-permute-start | bytes 589832 | tf_op jit(solution)/shard_map/ppermute | solution.py:97
  51.2 5.7 %collective-permute-start.17 = (bf16[96,1024]{1,0:T(8,128)(2,1)S(1)}, bf16[96,1024]{1,0:T(8,128)(2,1)S(1)}, u32[]{:S(2)}, u32[]{:S(2)}) collective-permute-start(bf16[96,1024]{1,0:T(8,128)(2,1)S(1)} %get-tuple-element.96), channel_id=1, source_target_pairs={{0,16},{1,17},{2,18},{3,19},{4,20},{5,21},{6,22},{7,23},{8,24},{9,... | collective-permute-start | bytes 589832 | tf_op jit(solution)/shard_map/ppermute | solution.py:97
  52.1 5.7 %collective-permute-start.16 = (bf16[96,1024]{1,0:T(8,128)(2,1)S(1)}, bf16[96,1024]{1,0:T(8,128)(2,1)S(1)}, u32[]{:S(2)}, u32[]{:S(2)}) collective-permute-start(bf16[96,1024]{1,0:T(8,128)(2,1)S(1)} %get-tuple-element.97), channel_id=1, source_target_pairs={{0,8},{1,9},{2,10},{3,11},{4,12},{5,13},{6,14},{7,15},{8,0},{9,1},... | collective-permute-start | bytes 589832 | tf_op jit(solution)/shard_map/ppermute | solution.py:97
  57.7 10.1 %collective-permute-start.25 = (bf16[192,1024]{1,0:T(8,128)(2,1)S(1)}, bf16[192,1024]{1,0:T(8,128)(2,1)S(1)}, u32[]{:S(2)}, u32[]{:S(2)}) collective-permute-start(bf16[192,1024]{1,0:T(8,128)(2,1)S(1)} %collective-permute-done.20), channel_id=1, source_target_pairs={{0,1},{1,3},{2,0},{3,2},{4,5},{5,7},{6,4},{7,6},{8,9},{9,11},{10,8... | collective-permute-start | bytes 1179656 | tf_op jit(solution)/shard_map/ppermute | solution.py:97
  58.6 6.3 %collective-permute-start.24 = (bf16[96,1024]{1,0:T(8,128)(2,1)S(1)}, bf16[96,1024]{1,0:T(8,128)(2,1)S(1)}, u32[]{:S(2)}, u32[]{:S(2)}) collective-permute-start(bf16[96,1024]{1,0:T(8,128)(2,1)S(1)} %get-tuple-element.90), channel_id=1, source_target_pairs={{0,16},{1,17},{2,18},{3,19},{4,20},{5,21},{6,22},{7,23},{8,24},{9,... | collective-permute-start | bytes 589832 | tf_op jit(solution)/shard_map/ppermute | solution.py:97
  60.1 5.7 %collective-permute-start.23 = (bf16[96,1024]{1,0:T(8,128)(2,1)S(1)}, bf16[96,1024]{1,0:T(8,128)(2,1)S(1)}, u32[]{:S(2)}, u32[]{:S(2)}) collective-permute-start(bf16[96,1024]{1,0:T(8,128)(2,1)S(1)} %get-tuple-element.91), channel_id=1, source_target_pairs={{0,8},{1,9},{2,10},{3,11},{4,12},{5,13},{6,14},{7,15},{8,0},{9,1},... | collective-permute-start | bytes 589832 | tf_op jit(solution)/shard_map/ppermute | solution.py:97
  60.5 6.5 %collective-permute-start.22 = (bf16[96,1024]{1,0:T(8,128)(2,1)S(1)}, bf16[96,1024]{1,0:T(8,128)(2,1)S(1)}, u32[]{:S(2)}, u32[]{:S(2)}) collective-permute-start(bf16[96,1024]{1,0:T(8,128)(2,1)S(1)} %get-tuple-element.92), channel_id=1, source_target_pairs={{0,16},{1,17},{2,18},{3,19},{4,20},{5,21},{6,22},{7,23},{8,24},{9,... | collective-permute-start | bytes 589832 | tf_op jit(solution)/shard_map/ppermute | solution.py:97
  61.4 6.4 %collective-permute-start.21 = (bf16[96,1024]{1,0:T(8,128)(2,1)S(1)}, bf16[96,1024]{1,0:T(8,128)(2,1)S(1)}, u32[]{:S(2)}, u32[]{:S(2)}) collective-permute-start(bf16[96,1024]{1,0:T(8,128)(2,1)S(1)} %get-tuple-element.93), channel_id=1, source_target_pairs={{0,8},{1,9},{2,10},{3,11},{4,12},{5,13},{6,14},{7,15},{8,0},{9,1},... | collective-permute-start | bytes 589832 | tf_op jit(solution)/shard_map/ppermute | solution.py:97
  68.8 10.4 %collective-permute-start.28 = (bf16[768,1024]{1,0:T(8,128)(2,1)S(1)}, bf16[768,1024]{1,0:T(8,128)(2,1)S(1)}, u32[]{:S(2)}, u32[]{:S(2)}) collective-permute-start(bf16[768,1024]{1,0:T(8,128)(2,1)S(1)} %select_dynamic-update-slice_fusion.8.refs_1_), channel_id=1, source_target_pairs={{0,4},{1,5},{2,6},{3,7},{4,0},{5,1},{6,2},{7,3},{8,12},{9,13},{10,... | collective-permute-start | bytes 4718600 | tf_op jit(solution)/shard_map/ppermute | solution.py:97
  71.1 7.3 %collective-permute-start.27 = (bf16[96,1024]{1,0:T(8,128)(2,1)S(1)}, bf16[96,1024]{1,0:T(8,128)(2,1)S(1)}, u32[]{:S(2)}, u32[]{:S(2)}) collective-permute-start(bf16[96,1024]{1,0:T(8,128)(2,1)S(1)} %get-tuple-element.88), channel_id=1, source_target_pairs={{0,16},{1,17},{2,18},{3,19},{4,20},{5,21},{6,22},{7,23},{8,24},{9,... | collective-permute-start | bytes 589832 | tf_op jit(solution)/shard_map/ppermute | solution.py:97
  72.2 7.0 %collective-permute-start.26 = (bf16[96,1024]{1,0:T(8,128)(2,1)S(1)}, bf16[96,1024]{1,0:T(8,128)(2,1)S(1)}, u32[]{:S(2)}, u32[]{:S(2)}) collective-permute-start(bf16[96,1024]{1,0:T(8,128)(2,1)S(1)} %get-tuple-element.89), channel_id=1, source_target_pairs={{0,8},{1,9},{2,10},{3,11},{4,12},{5,13},{6,14},{7,15},{8,0},{9,1},... | collective-permute-start | bytes 589832 | tf_op jit(solution)/shard_map/ppermute | solution.py:97
  80.0 6.2 %collective-permute-start.30 = (bf16[96,1024]{1,0:T(8,128)(2,1)S(1)}, bf16[96,1024]{1,0:T(8,128)(2,1)S(1)}, u32[]{:S(2)}, u32[]{:S(2)}) collective-permute-start(bf16[96,1024]{1,0:T(8,128)(2,1)S(1)} %get-tuple-element.86), channel_id=1, source_target_pairs={{0,16},{1,17},{2,18},{3,19},{4,20},{5,21},{6,22},{7,23},{8,24},{9,... | collective-permute-start | bytes 589832 | tf_op jit(solution)/shard_map/ppermute | solution.py:97
  81.0 5.9 %collective-permute-start.29 = (bf16[96,1024]{1,0:T(8,128)(2,1)S(1)}, bf16[96,1024]{1,0:T(8,128)(2,1)S(1)}, u32[]{:S(2)}, u32[]{:S(2)}) collective-permute-start(bf16[96,1024]{1,0:T(8,128)(2,1)S(1)} %get-tuple-element.87), channel_id=1, source_target_pairs={{0,8},{1,9},{2,10},{3,11},{4,12},{5,13},{6,14},{7,15},{8,0},{9,1},... | collective-permute-start | bytes 589832 | tf_op jit(solution)/shard_map/ppermute | solution.py:97
  87.3 3.6 %collective-permute-start.31 = (bf16[768,1024]{1,0:T(8,128)(2,1)S(1)}, bf16[768,1024]{1,0:T(8,128)(2,1)S(1)}, u32[]{:S(2)}, u32[]{:S(2)}) collective-permute-start(bf16[768,1024]{1,0:T(8,128)(2,1)S(1)} %select_dynamic-update-slice_fusion.refs_1_), channel_id=1, source_target_pairs={{0,4},{1,5},{2,6},{3,7},{4,0},{5,1},{6,2},{7,3},{8,12},{9,13},{10,... | collective-permute-start | bytes 4718600 | tf_op jit(solution)/shard_map/ppermute | solution.py:97
  (37 other events, 380.7 us)

commit v4 on v3

--- a/solution.py
+++ b/solution.py
@@ -121,8 +121,8 @@
 
     ring = (0, 1, 3, 2)
 
-    def along_z(x):
-        return go(x, lambda d, c: (d, ring[(ring.index(c) + 1) % 4]))
+    def along_z(x, step):
+        return go(x, lambda d, c: (d, ring[(ring.index(c) + step) % 4]))
 
     def tie(*values):
         return lax.optimization_barrier(values)
@@ -137,14 +137,13 @@
             high = jnp.where(root, high, back[0])
         return along_x(low), along_y(high)
 
-    def assemble(own, got):
-        n = len(own)
+    def assemble(picks, chunks, got):
         pieces = []
-        for c in range(n):
-            low, high = own[c][:half], own[c][half:]
+        for c, chunk in zip(picks, chunks):
+            low, high = chunk[:half], chunk[half:]
             x0, y0 = got[c]
             x1, y1 = got[c + 1]
-            if c < n - 1:
+            if c + 2 < len(got):
                 x2, y2 = got[c + 2]
                 pieces.append(lax.select_n(role, low, x0, x2, y1))
                 pieces.append(lax.select_n(role, high, y2, y0, x1))
@@ -159,42 +158,41 @@
     other_at = 1 - mine_at
 
     g0 = out_grads
-    g1 = along_z(g0)
+    g1 = along_z(g0, 1)
+    r0x, r0y = send(g0)
     sums = squares(hidden_states)
     sums = sums + core(sums)
     sums = (sums + along_x(sums)) + (along_y(sums) + across(sums))
-    e0 = send(g0)
     x0 = normalize(hidden_states, sums, norm_gain, width * n_dp)
-    e0x, e0y = e0
-    x0, g1 = tie(x0, g1)
-    g2 = along_z(g1)
-    o0x, o0y = send(x0)
-    x1 = along_z(x0)
-    g3 = along_z(g2)
-    o0x, o0y, e0x, e0y, g1, g2 = tie(o0x, o0y, e0x, e0y, g1, g2)
-    e1x, e1y = send(g1, (e0x, e0y))
-    e1x, e1y, g2, x1 = tie(e1x, e1y, g2, x1)
-    x2 = along_z(x1)
-    e2x, e2y = send(g2, (e1x, e1y))
-    e2x, e2y, o0x, o0y, g3 = tie(e2x, e2y, o0x, o0y, g3)
-    e3x, e3y = send(g3, (e2x, e2y))
-    o1x, o1y = send(x1, (o0x, o0y))
-    e3x, e3y, o1x, o1y, x2 = tie(e3x, e3y, o1x, o1y, x2)
-    x3 = along_z(x2)
-    e4x, e4y = send(g3, (e3x, e3y), last=True)
-    o2x, o2y = send(x2, (o1x, o1y))
-    e4x, e4y, o2x, o2y, x3, g1, g2, g3 = tie(e4x, e4y, o2x, o2y, x3, g1, g2, g3)
-    o3x, o3y = send(x3, (o2x, o2y))
-    g_mine = assemble([g0, g1, g2, g3], [(e0x, e0y), (e1x, e1y), (e2x, e2y), (e3x, e3y), (e4x, e4y)])
+    r0x, r0y, g1 = tie(r0x, r0y, g1)
+    r1x, r1y = send(g1, (r0x, r0y))
+    x1 = along_z(x0, 1)
+    g2 = along_z(g1, 1)
+    g3 = along_z(g2, 1)
+    r1x, r1y, g2 = tie(r1x, r1y, g2)
+    r2x, r2y = send(g2, (r1x, r1y))
+    r2x, r2y, x0 = tie(r2x, r2y, x0)
+    r3x, r3y = send(x0, (r2x, r2y))
+    x2 = along_z(x1, 1)
+    r3x, r3y, g3 = tie(r3x, r3y, g3)
+    r4x, r4y = send(g3, (r3x, r3y))
+    r4x, r4y, x1 = tie(r4x, r4y, x1)
+    r5x, r5y = send(x1, (r4x, r4y))
+    x3 = along_z(x2, 1)
+    r5x, r5y, x2 = tie(r5x, r5y, x2)
+    r6x, r6y = send(x2, (r5x, r5y))
+    r6x, r6y, x3 = tie(r6x, r6y, x3)
+    r7x, r7y = send(x3, (r6x, r6y))
+    g_mine = assemble([0, 1, 2, 4], [g0, g1, g2, g3], [(r0x, r0y), (r1x, r1y), (r2x, r2y), (r3x, r3y), (r4x, r4y), (r5x, r5y), (r6x, r6y)])
     g_other = core(g_mine)
     g_column = jnp.concatenate([g0, g1, g2, g3], axis=0)
     g_factor = gram_rows(g_mine, g_column, mine_at, scale, rows_all)
-    o3x, o3y, g_factor, x0, x1, x2, x3, g_other = tie(o3x, o3y, g_factor, x0, x1, x2, x3, g_other)
-    o4x, o4y = send(x3, (o3x, o3y), last=True)
+    r7x, r7y, g_factor, g_other, x0, x1, x2, x3 = tie(r7x, r7y, g_factor, g_other, x0, x1, x2, x3)
+    r8x, r8y = send(x3, (r7x, r7y), last=True)
     g_factor = gram_rows(g_other, g_column, other_at, scale, rows_all, g_factor)
     x_column = jnp.concatenate([x0, x1, x2, x3], axis=0)
-    o4x, o4y, g_factor, x_column = tie(o4x, o4y, g_factor, x_column)
-    x_mine = assemble([x0, x1, x2, x3], [(o0x, o0y), (o1x, o1y), (o2x, o2y), (o3x, o3y), (o4x, o4y)])
+    r8x, r8y, x_column, g_factor = tie(r8x, r8y, x_column, g_factor)
+    x_mine = assemble([3, 5, 6, 7], [x0, x1, x2, x3], [(r0x, r0y), (r1x, r1y), (r2x, r2y), (r3x, r3y), (r4x, r4y), (r5x, r5y), (r6x, r6y), (r7x, r7y), (r8x, r8y)])
     x_other = core(x_mine)
     a_factor = gram_rows(x_mine, x_column, mine_at, scale, rows_all)
     a_factor = gram_rows(x_other, x_column, other_at, scale, rows_all, a_factor)

time: 96 us -> 91.2 us (0.950); the launches traced: 94.4 us -> 91 us
  starting transfers between devices: 38.8 us -> 35.4 us
  other arithmetic: 8.51 us -> 5.63 us
  waiting for transfers between devices: 28.7 us -> 31.5 us
    ppermute x32 -> x30, starting transfers between devices: 38.8 us -> 35.4 us  [swap(): return lax.ppermute(x, AXES, pairs)]
    ppermute x32 -> x30, waiting for transfers between devices: 28.7 us -> 31.5 us  [swap(): return lax.ppermute(x, AXES, pairs)]
    unnamed x12 -> x10, other arithmetic: 2.35 us -> 1.21 us
    convert_element_type x1, other arithmetic: 1.16 us -> 0.16 us  [normalize(): return (hidden_states.astype(jnp.float32) * inv_rms * norm_gain.astype(jn...]
    unnamed x77 -> x65, local copies, waits for them, and re-layouts: 2.07 us -> 2.29 us
  transfers between devices with their start and end apart: 32 -> 30, of which waited for: 16 -> 16; matrix products, arithmetic and copies ran while one was open for 8% -> 7% of each run, Pallas kernels for 11% -> 12%
where the time goes in v4:
time: 91.2 us; the launch traced here: 91 us
  starting transfers between devices  35.4 us (39%)
  waiting for transfers between devices  31.5 us (35%)
  Pallas kernels  14 us (15%)
  other arithmetic  5.63 us (6%)
  local copies, waits for them, and re-layouts  3.36 us (4%)
  between operations  1.16 us (1%)
    ppermute x30, starting transfers between devices, swap(): return lax.ppermute(x, AXES, pairs)  35.4 us
    ppermute x30, waiting for transfers between devices, swap(): return lax.ppermute(x, AXES, pairs)  31.5 us
    pallas_call x4, Pallas kernels, gram_rows(): pl.pallas_call(lambda *refs: gram_rows_kernel(scale, *refs), out_shape=ja...  14 us
    unnamed x65, local copies, waits for them, and re-layouts  2.29 us
    select_n x8, other arithmetic, send(): high = jnp.where(root, high, back[0])  2.16 us
  transfers between devices with their start and end apart: 30, of which 16 were waited for; matrix products, arithmetic and copies ran while one was open for 7% of the time, Pallas kernels for 12%

profile of v4, /device:TPU:0, one launch (start us, length us, event | category | flops | bytes accessed | tf_op | source)
XLA Modules:
  0.0 91.0 jit_solution(14406679913883950734)
XLA Ops:
  0.6 3.1 %collective-permute-start.2 = (bf16[192,1024]{1,0:T(8,128)(2,1)}, bf16[192,1024]{1,0:T(8,128)(2,1)S(1)}, u32[]{:S(2)}, u32[]{:S(2)}) collective-permute-start(bf16[192,1024]{1,0:T(8,128)(2,1)} %param.4), channel_id=1, source_target_pairs={{0,1},{1,3},{2,0},{3,2},{4,5},{5,7},{6,4},{7,6},{8,9},{9,11},{10,8... | collective-permute-start | bytes 1179656 | tf_op jit(solution)/shard_map/ppermute | solution.py:97
  4.8 1.6 %collective-permute-start.1 = (bf16[96,1024]{1,0:T(8,128)(2,1)S(1)}, bf16[96,1024]{1,0:T(8,128)(2,1)S(1)}, u32[]{:S(2)}, u32[]{:S(2)}) collective-permute-start(bf16[96,1024]{1,0:T(8,128)(2,1)S(1)} %get-tuple-element.84), channel_id=1, source_target_pairs={{0,16},{1,17},{2,18},{3,19},{4,20},{5,21},{6,22},{7,23},{8,24},{9,... | collective-permute-start | bytes 589832 | tf_op jit(solution)/shard_map/ppermute | solution.py:97
  6.4 1.5 %collective-permute-start = (bf16[96,1024]{1,0:T(8,128)(2,1)S(1)}, bf16[96,1024]{1,0:T(8,128)(2,1)S(1)}, u32[]{:S(2)}, u32[]{:S(2)}) collective-permute-start(bf16[96,1024]{1,0:T(8,128)(2,1)S(1)} %get-tuple-element.85), channel_id=1, source_target_pairs={{0,8},{1,9},{2,10},{3,11},{4,12},{5,13},{6,14},{7,15},{8,0},{9,1},... | collective-permute-start | bytes 589832 | tf_op jit(solution)/shard_map/ppermute | solution.py:97
  7.8 1.2 %fusion = f32[192]{0:T(256)S(1)} fusion(bf16[192,1024]{1,0:T(8,128)(2,1)} %param.3), kind=kLoop, calls=%fused_computation.3 | loop fusion | flops 589632 | bytes 393984 | tf_op jit(solution)/shard_map/reduce_sum | solution.py:69
  10.7 1.5 %collective-permute-start.10 = (f32[192,1]{0,1:T(1,128)S(1)}, f32[192,1]{0,1:T(1,128)S(1)}, u32[]{:S(2)}, u32[]{:S(2)}) collective-permute-start(f32[192,1]{0,1:T(1,128)S(1)} %add.24), channel_id=1, source_target_pairs={{0,16},{1,17},{2,18},{3,19},{4,20},{5,21},{6,22},{7,23},{8,24},{9,... | collective-permute-start | bytes 2312 | tf_op jit(solution)/shard_map/ppermute | solution.py:97
  12.2 1.5 %collective-permute-start.9 = (f32[192,1]{0,1:T(1,128)S(1)}, f32[192,1]{0,1:T(1,128)S(1)}, u32[]{:S(2)}, u32[]{:S(2)}) collective-permute-start(f32[192,1]{0,1:T(1,128)S(1)} %add.24), channel_id=1, source_target_pairs={{0,8},{1,9},{2,10},{3,11},{4,12},{5,13},{6,14},{7,15},{8,0},{9,1},... | collective-permute-start | bytes 2312 | tf_op jit(solution)/shard_map/ppermute | solution.py:97
  14.0 2.3 %collective-permute-start.5 = (bf16[192,1024]{1,0:T(8,128)(2,1)S(1)}, bf16[192,1024]{1,0:T(8,128)(2,1)S(1)}, u32[]{:S(2)}, u32[]{:S(2)}) collective-permute-start(bf16[192,1024]{1,0:T(8,128)(2,1)S(1)} %collective-permute-done.2), channel_id=1, source_target_pairs={{0,1},{1,3},{2,0},{3,2},{4,5},{5,7},{6,4},{7,6},{8,9},{9,11},{10,8... | collective-permute-start | bytes 1179656 | tf_op jit(solution)/shard_map/ppermute | solution.py:97
  17.0 1.1 %collective-permute-start.3 = (bf16[96,1024]{1,0:T(8,128)(2,1)S(1)}, bf16[96,1024]{1,0:T(8,128)(2,1)S(1)}, u32[]{:S(2)}, u32[]{:S(2)}) collective-permute-start(bf16[96,1024]{1,0:T(8,128)(2,1)S(1)} %get-tuple-element.83), channel_id=1, source_target_pairs={{0,8},{1,9},{2,10},{3,11},{4,12},{5,13},{6,14},{7,15},{8,0},{9,1},... | collective-permute-start | bytes 589832 | tf_op jit(solution)/shard_map/ppermute | solution.py:97
  18.1 4.2 %collective-permute-done.4 = bf16[96,1024]{1,0:T(8,128)(2,1)S(1)} collective-permute-done((bf16[96,1024]{1,0:T(8,128)(2,1)S(1)}, bf16[96,1024]{1,0:T(8,128)(2,1)S(1)}, u32[]{:S(2)}, u32[]{:S(2)}) %collective-permute-start.4) | collective-permute-done | bytes 196640 | tf_op jit(solution)/shard_map/ppermute | solution.py:97
  22.6 2.6 %collective-permute-done.5 = bf16[192,1024]{1,0:T(8,128)(2,1)S(1)} collective-permute-done((bf16[192,1024]{1,0:T(8,128)(2,1)S(1)}, bf16[192,1024]{1,0:T(8,128)(2,1)S(1)}, u32[]{:S(2)}, u32[]{:S(2)}) %collective-permute-start.5) | collective-permute-done | bytes 393248 | tf_op jit(solution)/shard_map/ppermute | solution.py:97
  25.3 1.3 %collective-permute-start.7 = (bf16[96,1024]{1,0:T(8,128)(2,1)S(1)}, bf16[96,1024]{1,0:T(8,128)(2,1)S(1)}, u32[]{:S(2)}, u32[]{:S(2)}) collective-permute-start(bf16[96,1024]{1,0:T(8,128)(2,1)S(1)} %get-tuple-element.80), channel_id=1, source_target_pairs={{0,16},{1,17},{2,18},{3,19},{4,20},{5,21},{6,22},{7,23},{8,24},{9,... | collective-permute-start | bytes 589832 | tf_op jit(solution)/shard_map/ppermute | solution.py:97
  26.6 1.5 %collective-permute-start.6 = (bf16[96,1024]{1,0:T(8,128)(2,1)S(1)}, bf16[96,1024]{1,0:T(8,128)(2,1)S(1)}, u32[]{:S(2)}, u32[]{:S(2)}) collective-permute-start(bf16[96,1024]{1,0:T(8,128)(2,1)S(1)} %get-tuple-element.81), channel_id=1, source_target_pairs={{0,8},{1,9},{2,10},{3,11},{4,12},{5,13},{6,14},{7,15},{8,0},{9,1},... | collective-permute-start | bytes 589832 | tf_op jit(solution)/shard_map/ppermute | solution.py:97
  29.1 1.9 %collective-permute-done.7 = bf16[96,1024]{1,0:T(8,128)(2,1)S(1)} collective-permute-done((bf16[96,1024]{1,0:T(8,128)(2,1)S(1)}, bf16[96,1024]{1,0:T(8,128)(2,1)S(1)}, u32[]{:S(2)}, u32[]{:S(2)}) %collective-permute-start.7) | collective-permute-done | bytes 196640 | tf_op jit(solution)/shard_map/ppermute | solution.py:97
  31.0 1.2 %collective-permute-done.6 = bf16[96,1024]{1,0:T(8,128)(2,1)S(1)} collective-permute-done((bf16[96,1024]{1,0:T(8,128)(2,1)S(1)}, bf16[96,1024]{1,0:T(8,128)(2,1)S(1)}, u32[]{:S(2)}, u32[]{:S(2)}) %collective-permute-start.6) | collective-permute-done | bytes 196640 | tf_op jit(solution)/shard_map/ppermute | solution.py:97
  33.5 1.2 %collective-permute-start.12 = (bf16[96,1024]{1,0:T(8,128)(2,1)S(1)}, bf16[96,1024]{1,0:T(8,128)(2,1)S(1)}, u32[]{:S(2)}, u32[]{:S(2)}) collective-permute-start(bf16[96,1024]{1,0:T(8,128)(2,1)S(1)} %get-tuple-element.79), channel_id=1, source_target_pairs={{0,8},{1,9},{2,10},{3,11},{4,12},{5,13},{6,14},{7,15},{8,0},{9,1},... | collective-permute-start | bytes 589832 | tf_op jit(solution)/shard_map/ppermute | solution.py:97
  35.5 5.4 %collective-permute-done.14 = bf16[192,1024]{1,0:T(8,128)(2,1)S(1)} collective-permute-done((bf16[192,1024]{1,0:T(8,128)(2,1)S(1)}, bf16[192,1024]{1,0:T(8,128)(2,1)S(1)}, u32[]{:S(2)}, u32[]{:S(2)}) %collective-permute-start.14) | collective-permute-done | bytes 393248 | tf_op jit(solution)/shard_map/ppermute | solution.py:97
  41.5 2.0 %collective-permute-start.15 = (bf16[96,1024]{1,0:T(8,128)(2,1)S(1)}, bf16[96,1024]{1,0:T(8,128)(2,1)S(1)}, u32[]{:S(2)}, u32[]{:S(2)}) collective-permute-start(bf16[96,1024]{1,0:T(8,128)(2,1)S(1)} %get-tuple-element.77), channel_id=1, source_target_pairs={{0,8},{1,9},{2,10},{3,11},{4,12},{5,13},{6,14},{7,15},{8,0},{9,1},... | collective-permute-start | bytes 589832 | tf_op jit(solution)/shard_map/ppermute | solution.py:97
  43.5 2.7 %collective-permute-done.17 = bf16[192,1024]{1,0:T(8,128)(2,1)S(1)} collective-permute-done((bf16[192,1024]{1,0:T(8,128)(2,1)S(1)}, bf16[192,1024]{1,0:T(8,128)(2,1)S(1)}, u32[]{:S(2)}, u32[]{:S(2)}) %collective-permute-start.17) | collective-permute-done | bytes 393248 | tf_op jit(solution)/shard_map/ppermute | solution.py:97
  48.2 2.1 %collective-permute-start.19 = (bf16[96,1024]{1,0:T(8,128)(2,1)S(1)}, bf16[96,1024]{1,0:T(8,128)(2,1)S(1)}, u32[]{:S(2)}, u32[]{:S(2)}) collective-permute-start(bf16[96,1024]{1,0:T(8,128)(2,1)S(1)} %get-tuple-element.74), channel_id=1, source_target_pairs={{0,16},{1,17},{2,18},{3,19},{4,20},{5,21},{6,22},{7,23},{8,24},{9,... | collective-permute-start | bytes 589832 | tf_op jit(solution)/shard_map/ppermute | solution.py:97
  50.8 4.6 %collective-permute-done.20 = bf16[192,1024]{1,0:T(8,128)(2,1)S(1)} collective-permute-done((bf16[192,1024]{1,0:T(8,128)(2,1)S(1)}, bf16[192,1024]{1,0:T(8,128)(2,1)S(1)}, u32[]{:S(2)}, u32[]{:S(2)}) %collective-permute-start.20) | collective-permute-done | bytes 393248 | tf_op jit(solution)/shard_map/ppermute | solution.py:97
  56.3 1.4 %collective-permute-start.22 = (bf16[96,1024]{1,0:T(8,128)(2,1)S(1)}, bf16[96,1024]{1,0:T(8,128)(2,1)S(1)}, u32[]{:S(2)}, u32[]{:S(2)}) collective-permute-start(bf16[96,1024]{1,0:T(8,128)(2,1)S(1)} %get-tuple-element.72), channel_id=1, source_target_pairs={{0,16},{1,17},{2,18},{3,19},{4,20},{5,21},{6,22},{7,23},{8,24},{9,... | collective-permute-start | bytes 589832 | tf_op jit(solution)/shard_map/ppermute | solution.py:97
  57.6 2.5 %collective-permute-start.21 = (bf16[96,1024]{1,0:T(8,128)(2,1)S(1)}, bf16[96,1024]{1,0:T(8,128)(2,1)S(1)}, u32[]{:S(2)}, u32[]{:S(2)}) collective-permute-start(bf16[96,1024]{1,0:T(8,128)(2,1)S(1)} %get-tuple-element.73), channel_id=1, source_target_pairs={{0,8},{1,9},{2,10},{3,11},{4,12},{5,13},{6,14},{7,15},{8,0},{9,1},... | collective-permute-start | bytes 589832 | tf_op jit(solution)/shard_map/ppermute | solution.py:97
  60.1 4.0 %collective-permute-done.23 = bf16[192,1024]{1,0:T(8,128)(2,1)S(1)} collective-permute-done((bf16[192,1024]{1,0:T(8,128)(2,1)S(1)}, bf16[192,1024]{1,0:T(8,128)(2,1)S(1)}, u32[]{:S(2)}, u32[]{:S(2)}) %collective-permute-start.23) | collective-permute-done | bytes 393248 | tf_op jit(solution)/shard_map/ppermute | solution.py:97
  65.5 1.1 %constant_dynamic-update-slice_fusion.3 = bf16[768,1024]{1,0:T(8,128)(2,1)S(1)} fusion(bf16[192,1024]{1,0:T(8,128)(2,1)} %param.4), kind=kLoop, calls=%fused_computation.41 | loop fusion | bytes 786432
  68.4 1.0 %collective-permute-start.24 = (bf16[96,1024]{1,0:T(8,128)(2,1)S(1)}, bf16[96,1024]{1,0:T(8,128)(2,1)S(1)}, u32[]{:S(2)}, u32[]{:S(2)}) collective-permute-start(bf16[96,1024]{1,0:T(8,128)(2,1)S(1)} %copy-done.29), channel_id=1, source_target_pairs={{0,8},{1,9},{2,10},{3,11},{4,12},{5,13},{6,14},{7,15},{8,0},{9,1},... | collective-permute-start | bytes 589832 | tf_op jit(solution)/shard_map/ppermute | solution.py:97
  69.6 3.5 %shard_map.50.refs_3_ = f32[2048,1024]{1,0:T(8,128)} custom-call(s32[1]{0:T(128)} %bitcast.refs_0_, bf16[768,1024]{1,0:T(8,128)(2,1)S(1)} %get-tuple-element.89.refs_1_, bf16[768,1024]{1,0:T(8,128)(2,1)S(1)} %constant_dynamic-update-slice_fusion.refs_2_), custom_call_target="tpu_custom_call" | custom-call | flops 1610612736 | bytes 7340032 | tf_op jit(solution)/shard_map/pallas_call | solution.py:46
  73.1 1.9 %collective-permute-done.25 = bf16[96,1024]{1,0:T(8,128)(2,1)S(1)} collective-permute-done((bf16[96,1024]{1,0:T(8,128)(2,1)S(1)}, bf16[96,1024]{1,0:T(8,128)(2,1)S(1)}, u32[]{:S(2)}, u32[]{:S(2)}) %collective-permute-start.25) | collective-permute-done | bytes 196640 | tf_op jit(solution)/shard_map/ppermute | solution.py:97
  76.2 1.4 %collective-permute-start.28 = (bf16[96,1024]{1,0:T(8,128)(2,1)S(1)}, bf16[96,1024]{1,0:T(8,128)(2,1)S(1)}, u32[]{:S(2)}, u32[]{:S(2)}) collective-permute-start(bf16[96,1024]{1,0:T(8,128)(2,1)S(1)} %get-tuple-element.68), channel_id=1, source_target_pairs={{0,16},{1,17},{2,18},{3,19},{4,20},{5,21},{6,22},{7,23},{8,24},{9,... | collective-permute-start | bytes 589832 | tf_op jit(solution)/shard_map/ppermute | solution.py:97
  77.6 1.7 %collective-permute-start.27 = (bf16[96,1024]{1,0:T(8,128)(2,1)S(1)}, bf16[96,1024]{1,0:T(8,128)(2,1)S(1)}, u32[]{:S(2)}, u32[]{:S(2)}) collective-permute-start(bf16[96,1024]{1,0:T(8,128)(2,1)S(1)} %get-tuple-element.69), channel_id=1, source_target_pairs={{0,8},{1,9},{2,10},{3,11},{4,12},{5,13},{6,14},{7,15},{8,0},{9,1},... | collective-permute-start | bytes 589832 | tf_op jit(solution)/shard_map/ppermute | solution.py:97
  79.2 3.5 %shard_map.51 = f32[2048,1024]{1,0:T(8,128)} custom-call(s32[1]{0:T(128)S(6)} %sub.7.refs_0_, bf16[768,1024]{1,0:T(8,128)(2,1)S(1)} %collective-permute-done.26.refs_1_, bf16[768,1024]{1,0:T(8,128)(2,1)S(1)} %constant_dynamic-update-slice_fusion.refs_2_, f32[2048,1024]{1,0:T(8,128)} %shard_map.50.refs_3_), custom_call_target="tpu_custom_call", output_to_operand_aliasing={{}: (3, {})} | custom-call | flops 1610612736 | bytes 7340032 | tf_op jit(solution)/shard_map/pallas_call | solution.py:46
  84.0 3.5 %shard_map.52.refs_3_ = f32[2048,1024]{1,0:T(8,128)} custom-call(s32[1]{0:T(128)} %bitcast.refs_0_, bf16[768,1024]{1,0:T(8,128)(2,1)S(1)} %select_dynamic-update-slice_fusion.refs_1_, bf16[768,1024]{1,0:T(8,128)(2,1)S(1)} %pad_maximum_fusion.refs_2_), custom_call_target="tpu_custom_call" | custom-call | flops 1610612736 | bytes 7340032 | tf_op jit(solution)/shard_map/pallas_call | solution.py:46
  87.5 3.5 %shard_map.53 = f32[2048,1024]{1,0:T(8,128)} custom-call(s32[1]{0:T(128)S(6)} %sub.7.refs_0_, bf16[768,1024]{1,0:T(8,128)(2,1)S(1)} %collective-permute-done.29.refs_1_, bf16[768,1024]{1,0:T(8,128)(2,1)S(1)} %pad_maximum_fusion.refs_2_, f32[2048,1024]{1,0:T(8,128)} %shard_map.52.refs_3_), custom_call_target="tpu_custom_call", output_to_operand_aliasing={{}: (3, {})} | custom-call | flops 1610612736 | bytes 7340032 | tf_op jit(solution)/shard_map/pallas_call | solution.py:46
  (124 shorter events, 16.3 us)
Async XLA Ops:
  0.6 13.4 %collective-permute-start.2 = (bf16[192,1024]{1,0:T(8,128)(2,1)}, bf16[192,1024]{1,0:T(8,128)(2,1)S(1)}, u32[]{:S(2)}, u32[]{:S(2)}) collective-permute-start(bf16[192,1024]{1,0:T(8,128)(2,1)} %param.4), channel_id=1, source_target_pairs={{0,1},{1,3},{2,0},{3,2},{4,5},{5,7},{6,4},{7,6},{8,9},{9,11},{10,8... | collective-permute-start | bytes 1179656 | tf_op jit(solution)/shard_map/ppermute | solution.py:97
  4.8 23.3 %copy-start.28 = (bf16[192,1024]{1,0:T(8,128)(2,1)S(1)}, bf16[192,1024]{1,0:T(8,128)(2,1)}, u32[]{:S(2)}) copy-start(bf16[192,1024]{1,0:T(8,128)(2,1)} %param.3) | copy-start | bytes 1179652
  4.8 7.4 %collective-permute-start.1 = (bf16[96,1024]{1,0:T(8,128)(2,1)S(1)}, bf16[96,1024]{1,0:T(8,128)(2,1)S(1)}, u32[]{:S(2)}, u32[]{:S(2)}) collective-permute-start(bf16[96,1024]{1,0:T(8,128)(2,1)S(1)} %get-tuple-element.84), channel_id=1, source_target_pairs={{0,16},{1,17},{2,18},{3,19},{4,20},{5,21},{6,22},{7,23},{8,24},{9,... | collective-permute-start | bytes 589832 | tf_op jit(solution)/shard_map/ppermute | solution.py:97
  6.4 7.3 %collective-permute-start = (bf16[96,1024]{1,0:T(8,128)(2,1)S(1)}, bf16[96,1024]{1,0:T(8,128)(2,1)S(1)}, u32[]{:S(2)}, u32[]{:S(2)}) collective-permute-start(bf16[96,1024]{1,0:T(8,128)(2,1)S(1)} %get-tuple-element.85), channel_id=1, source_target_pairs={{0,8},{1,9},{2,10},{3,11},{4,12},{5,13},{6,14},{7,15},{8,0},{9,1},... | collective-permute-start | bytes 589832 | tf_op jit(solution)/shard_map/ppermute | solution.py:97
  9.0 1.2 %collective-permute-start.8 = (f32[192,1]{0,1:T(1,128)S(1)}, f32[192,1]{0,1:T(1,128)S(1)}, u32[]{:S(2)}, u32[]{:S(2)}) collective-permute-start(f32[192,1]{0,1:T(1,128)S(1)} %bitcast.5), channel_id=1, source_target_pairs={{0,4},{1,5},{2,6},{3,7},{4,0},{5,1},{6,2},{7,3},{8,12},{9,13},{10,... | collective-permute-start | bytes 2312 | tf_op jit(solution)/shard_map/ppermute | solution.py:97
  10.2 6.8 %collective-permute-start.11 = (f32[192,1]{0,1:T(1,128)S(1)}, f32[192,1]{0,1:T(1,128)S(1)}, u32[]{:S(2)}, u32[]{:S(2)}) collective-permute-start(f32[192,1]{0,1:T(1,128)S(1)} %add.24), channel_id=1, source_target_pairs={{0,24},{1,25},{2,26},{3,27},{4,28},{5,29},{6,30},{7,31},{8,16},{9,... | collective-permute-start | bytes 2312 | tf_op jit(solution)/shard_map/ppermute | solution.py:97
  10.7 7.4 %collective-permute-start.10 = (f32[192,1]{0,1:T(1,128)S(1)}, f32[192,1]{0,1:T(1,128)S(1)}, u32[]{:S(2)}, u32[]{:S(2)}) collective-permute-start(f32[192,1]{0,1:T(1,128)S(1)} %add.24), channel_id=1, source_target_pairs={{0,16},{1,17},{2,18},{3,19},{4,20},{5,21},{6,22},{7,23},{8,24},{9,... | collective-permute-start | bytes 2312 | tf_op jit(solution)/shard_map/ppermute | solution.py:97
  12.2 5.9 %collective-permute-start.9 = (f32[192,1]{0,1:T(1,128)S(1)}, f32[192,1]{0,1:T(1,128)S(1)}, u32[]{:S(2)}, u32[]{:S(2)}) collective-permute-start(f32[192,1]{0,1:T(1,128)S(1)} %add.24), channel_id=1, source_target_pairs={{0,8},{1,9},{2,10},{3,11},{4,12},{5,13},{6,14},{7,15},{8,0},{9,1},... | collective-permute-start | bytes 2312 | tf_op jit(solution)/shard_map/ppermute | solution.py:97
  14.0 27.0 %copy-start.3 = (bf16[192,1024]{1,0:T(8,128)(2,1)}, bf16[192,1024]{1,0:T(8,128)(2,1)S(1)}, u32[]{:S(2)}) copy-start(bf16[192,1024]{1,0:T(8,128)(2,1)S(1)} %collective-permute-done.2) | copy-start | bytes 1179652
  14.0 11.2 %collective-permute-start.5 = (bf16[192,1024]{1,0:T(8,128)(2,1)S(1)}, bf16[192,1024]{1,0:T(8,128)(2,1)S(1)}, u32[]{:S(2)}, u32[]{:S(2)}) collective-permute-start(bf16[192,1024]{1,0:T(8,128)(2,1)S(1)} %collective-permute-done.2), channel_id=1, source_target_pairs={{0,1},{1,3},{2,0},{3,2},{4,5},{5,7},{6,4},{7,6},{8,9},{9,11},{10,8... | collective-permute-start | bytes 1179656 | tf_op jit(solution)/shard_map/ppermute | solution.py:97
  16.4 5.9 %collective-permute-start.4 = (bf16[96,1024]{1,0:T(8,128)(2,1)S(1)}, bf16[96,1024]{1,0:T(8,128)(2,1)S(1)}, u32[]{:S(2)}, u32[]{:S(2)}) collective-permute-start(bf16[96,1024]{1,0:T(8,128)(2,1)S(1)} %get-tuple-element.82), channel_id=1, source_target_pairs={{0,16},{1,17},{2,18},{3,19},{4,20},{5,21},{6,22},{7,23},{8,24},{9,... | collective-permute-start | bytes 589832 | tf_op jit(solution)/shard_map/ppermute | solution.py:97
  17.0 5.7 %collective-permute-start.3 = (bf16[96,1024]{1,0:T(8,128)(2,1)S(1)}, bf16[96,1024]{1,0:T(8,128)(2,1)S(1)}, u32[]{:S(2)}, u32[]{:S(2)}) collective-permute-start(bf16[96,1024]{1,0:T(8,128)(2,1)S(1)} %get-tuple-element.83), channel_id=1, source_target_pairs={{0,8},{1,9},{2,10},{3,11},{4,12},{5,13},{6,14},{7,15},{8,0},{9,1},... | collective-permute-start | bytes 589832 | tf_op jit(solution)/shard_map/ppermute | solution.py:97
  25.3 5.7 %collective-permute-start.7 = (bf16[96,1024]{1,0:T(8,128)(2,1)S(1)}, bf16[96,1024]{1,0:T(8,128)(2,1)S(1)}, u32[]{:S(2)}, u32[]{:S(2)}) collective-permute-start(bf16[96,1024]{1,0:T(8,128)(2,1)S(1)} %get-tuple-element.80), channel_id=1, source_target_pairs={{0,16},{1,17},{2,18},{3,19},{4,20},{5,21},{6,22},{7,23},{8,24},{9,... | collective-permute-start | bytes 589832 | tf_op jit(solution)/shard_map/ppermute | solution.py:97
  26.6 5.7 %collective-permute-start.6 = (bf16[96,1024]{1,0:T(8,128)(2,1)S(1)}, bf16[96,1024]{1,0:T(8,128)(2,1)S(1)}, u32[]{:S(2)}, u32[]{:S(2)}) collective-permute-start(bf16[96,1024]{1,0:T(8,128)(2,1)S(1)} %get-tuple-element.81), channel_id=1, source_target_pairs={{0,8},{1,9},{2,10},{3,11},{4,12},{5,13},{6,14},{7,15},{8,0},{9,1},... | collective-permute-start | bytes 589832 | tf_op jit(solution)/shard_map/ppermute | solution.py:97
  28.3 12.7 %collective-permute-start.14 = (bf16[192,1024]{1,0:T(8,128)(2,1)S(1)}, bf16[192,1024]{1,0:T(8,128)(2,1)S(1)}, u32[]{:S(2)}, u32[]{:S(2)}) collective-permute-start(bf16[192,1024]{1,0:T(8,128)(2,1)S(1)} %collective-permute-done.5), channel_id=1, source_target_pairs={{0,1},{1,3},{2,0},{3,2},{4,5},{5,7},{6,4},{7,6},{8,9},{9,11},{10,8... | collective-permute-start | bytes 1179656 | tf_op jit(solution)/shard_map/ppermute | solution.py:97
  32.7 8.3 %collective-permute-start.13 = (bf16[96,1024]{1,0:T(8,128)(2,1)S(1)}, bf16[96,1024]{1,0:T(8,128)(2,1)S(1)}, u32[]{:S(2)}, u32[]{:S(2)}) collective-permute-start(bf16[96,1024]{1,0:T(8,128)(2,1)S(1)} %get-tuple-element.78), channel_id=1, source_target_pairs={{0,16},{1,17},{2,18},{3,19},{4,20},{5,21},{6,22},{7,23},{8,24},{9,... | collective-permute-start | bytes 589832 | tf_op jit(solution)/shard_map/ppermute | solution.py:97
  33.5 7.4 %collective-permute-start.12 = (bf16[96,1024]{1,0:T(8,128)(2,1)S(1)}, bf16[96,1024]{1,0:T(8,128)(2,1)S(1)}, u32[]{:S(2)}, u32[]{:S(2)}) collective-permute-start(bf16[96,1024]{1,0:T(8,128)(2,1)S(1)} %get-tuple-element.79), channel_id=1, source_target_pairs={{0,8},{1,9},{2,10},{3,11},{4,12},{5,13},{6,14},{7,15},{8,0},{9,1},... | collective-permute-start | bytes 589832 | tf_op jit(solution)/shard_map/ppermute | solution.py:97
  34.7 11.4 %collective-permute-start.17 = (bf16[192,1024]{1,0:T(8,128)(2,1)S(1)}, bf16[192,1024]{1,0:T(8,128)(2,1)S(1)}, u32[]{:S(2)}, u32[]{:S(2)}) collective-permute-start(bf16[192,1024]{1,0:T(8,128)(2,1)S(1)} %fusion.2), channel_id=1, source_target_pairs={{0,1},{1,3},{2,0},{3,2},{4,5},{5,7},{6,4},{7,6},{8,9},{9,11},{10,8... | collective-permute-start | bytes 1179656 | tf_op jit(solution)/shard_map/ppermute | solution.py:97
  41.4 6.1 %collective-permute-start.16 = (bf16[96,1024]{1,0:T(8,128)(2,1)S(1)}, bf16[96,1024]{1,0:T(8,128)(2,1)S(1)}, u32[]{:S(2)}, u32[]{:S(2)}) collective-permute-start(bf16[96,1024]{1,0:T(8,128)(2,1)S(1)} %get-tuple-element.76), channel_id=1, source_target_pairs={{0,16},{1,17},{2,18},{3,19},{4,20},{5,21},{6,22},{7,23},{8,24},{9,... | collective-permute-start | bytes 589832 | tf_op jit(solution)/shard_map/ppermute | solution.py:97
  41.5 6.2 %collective-permute-start.15 = (bf16[96,1024]{1,0:T(8,128)(2,1)S(1)}, bf16[96,1024]{1,0:T(8,128)(2,1)S(1)}, u32[]{:S(2)}, u32[]{:S(2)}) collective-permute-start(bf16[96,1024]{1,0:T(8,128)(2,1)S(1)} %get-tuple-element.77), channel_id=1, source_target_pairs={{0,8},{1,9},{2,10},{3,11},{4,12},{5,13},{6,14},{7,15},{8,0},{9,1},... | collective-permute-start | bytes 589832 | tf_op jit(solution)/shard_map/ppermute | solution.py:97
  46.1 9.3 %collective-permute-start.20 = (bf16[192,1024]{1,0:T(8,128)(2,1)S(1)}, bf16[192,1024]{1,0:T(8,128)(2,1)S(1)}, u32[]{:S(2)}, u32[]{:S(2)}) collective-permute-start(bf16[192,1024]{1,0:T(8,128)(2,1)S(1)} %collective-permute-done.17), channel_id=1, source_target_pairs={{0,1},{1,3},{2,0},{3,2},{4,5},{5,7},{6,4},{7,6},{8,9},{9,11},{10,8... | collective-permute-start | bytes 1179656 | tf_op jit(solution)/shard_map/ppermute | solution.py:97
  48.2 8.1 %collective-permute-start.19 = (bf16[96,1024]{1,0:T(8,128)(2,1)S(1)}, bf16[96,1024]{1,0:T(8,128)(2,1)S(1)}, u32[]{:S(2)}, u32[]{:S(2)}) collective-permute-start(bf16[96,1024]{1,0:T(8,128)(2,1)S(1)} %get-tuple-element.74), channel_id=1, source_target_pairs={{0,16},{1,17},{2,18},{3,19},{4,20},{5,21},{6,22},{7,23},{8,24},{9,... | collective-permute-start | bytes 589832 | tf_op jit(solution)/shard_map/ppermute | solution.py:97
  50.3 5.9 %collective-permute-start.18 = (bf16[96,1024]{1,0:T(8,128)(2,1)S(1)}, bf16[96,1024]{1,0:T(8,128)(2,1)S(1)}, u32[]{:S(2)}, u32[]{:S(2)}) collective-permute-start(bf16[96,1024]{1,0:T(8,128)(2,1)S(1)} %get-tuple-element.75), channel_id=1, source_target_pairs={{0,8},{1,9},{2,10},{3,11},{4,12},{5,13},{6,14},{7,15},{8,0},{9,1},... | collective-permute-start | bytes 589832 | tf_op jit(solution)/shard_map/ppermute | solution.py:97
  55.4 8.7 %collective-permute-start.23 = (bf16[192,1024]{1,0:T(8,128)(2,1)S(1)}, bf16[192,1024]{1,0:T(8,128)(2,1)S(1)}, u32[]{:S(2)}, u32[]{:S(2)}) collective-permute-start(bf16[192,1024]{1,0:T(8,128)(2,1)S(1)} %collective-permute-done.20), channel_id=1, source_target_pairs={{0,1},{1,3},{2,0},{3,2},{4,5},{5,7},{6,4},{7,6},{8,9},{9,11},{10,8... | collective-permute-start | bytes 1179656 | tf_op jit(solution)/shard_map/ppermute | solution.py:97
  56.3 7.8 %collective-permute-start.22 = (bf16[96,1024]{1,0:T(8,128)(2,1)S(1)}, bf16[96,1024]{1,0:T(8,128)(2,1)S(1)}, u32[]{:S(2)}, u32[]{:S(2)}) collective-permute-start(bf16[96,1024]{1,0:T(8,128)(2,1)S(1)} %get-tuple-element.72), channel_id=1, source_target_pairs={{0,16},{1,17},{2,18},{3,19},{4,20},{5,21},{6,22},{7,23},{8,24},{9,... | collective-permute-start | bytes 589832 | tf_op jit(solution)/shard_map/ppermute | solution.py:97
  57.6 6.5 %collective-permute-start.21 = (bf16[96,1024]{1,0:T(8,128)(2,1)S(1)}, bf16[96,1024]{1,0:T(8,128)(2,1)S(1)}, u32[]{:S(2)}, u32[]{:S(2)}) collective-permute-start(bf16[96,1024]{1,0:T(8,128)(2,1)S(1)} %get-tuple-element.73), channel_id=1, source_target_pairs={{0,8},{1,9},{2,10},{3,11},{4,12},{5,13},{6,14},{7,15},{8,0},{9,1},... | collective-permute-start | bytes 589832 | tf_op jit(solution)/shard_map/ppermute | solution.py:97
  65.3 10.1 %collective-permute-start.26 = (bf16[768,1024]{1,0:T(8,128)(2,1)S(1)}, bf16[768,1024]{1,0:T(8,128)(2,1)S(1)}, u32[]{:S(2)}, u32[]{:S(2)}) collective-permute-start(bf16[768,1024]{1,0:T(8,128)(2,1)S(1)} %get-tuple-element.89.refs_1_), channel_id=1, source_target_pairs={{0,4},{1,5},{2,6},{3,7},{4,0},{5,1},{6,2},{7,3},{8,12},{9,13},{10,... | collective-permute-start | bytes 4718600 | tf_op jit(solution)/shard_map/ppermute | solution.py:97
  67.7 7.3 %collective-permute-start.25 = (bf16[96,1024]{1,0:T(8,128)(2,1)S(1)}, bf16[96,1024]{1,0:T(8,128)(2,1)S(1)}, u32[]{:S(2)}, u32[]{:S(2)}) collective-permute-start(bf16[96,1024]{1,0:T(8,128)(2,1)S(1)} %copy-done.30), channel_id=1, source_target_pairs={{0,16},{1,17},{2,18},{3,19},{4,20},{5,21},{6,22},{7,23},{8,24},{9,... | collective-permute-start | bytes 589832 | tf_op jit(solution)/shard_map/ppermute | solution.py:97
  68.4 7.0 %collective-permute-start.24 = (bf16[96,1024]{1,0:T(8,128)(2,1)S(1)}, bf16[96,1024]{1,0:T(8,128)(2,1)S(1)}, u32[]{:S(2)}, u32[]{:S(2)}) collective-permute-start(bf16[96,1024]{1,0:T(8,128)(2,1)S(1)} %copy-done.29), channel_id=1, source_target_pairs={{0,8},{1,9},{2,10},{3,11},{4,12},{5,13},{6,14},{7,15},{8,0},{9,1},... | collective-permute-start | bytes 589832 | tf_op jit(solution)/shard_map/ppermute | solution.py:97
  76.2 6.7 %collective-permute-start.28 = (bf16[96,1024]{1,0:T(8,128)(2,1)S(1)}, bf16[96,1024]{1,0:T(8,128)(2,1)S(1)}, u32[]{:S(2)}, u32[]{:S(2)}) collective-permute-start(bf16[96,1024]{1,0:T(8,128)(2,1)S(1)} %get-tuple-element.68), channel_id=1, source_target_pairs={{0,16},{1,17},{2,18},{3,19},{4,20},{5,21},{6,22},{7,23},{8,24},{9,... | collective-permute-start | bytes 589832 | tf_op jit(solution)/shard_map/ppermute | solution.py:97
  77.6 5.9 %collective-permute-start.27 = (bf16[96,1024]{1,0:T(8,128)(2,1)S(1)}, bf16[96,1024]{1,0:T(8,128)(2,1)S(1)}, u32[]{:S(2)}, u32[]{:S(2)}) collective-permute-start(bf16[96,1024]{1,0:T(8,128)(2,1)S(1)} %get-tuple-element.69), channel_id=1, source_target_pairs={{0,8},{1,9},{2,10},{3,11},{4,12},{5,13},{6,14},{7,15},{8,0},{9,1},... | collective-permute-start | bytes 589832 | tf_op jit(solution)/shard_map/ppermute | solution.py:97
  83.9 3.6 %collective-permute-start.29 = (bf16[768,1024]{1,0:T(8,128)(2,1)S(1)}, bf16[768,1024]{1,0:T(8,128)(2,1)S(1)}, u32[]{:S(2)}, u32[]{:S(2)}) collective-permute-start(bf16[768,1024]{1,0:T(8,128)(2,1)S(1)} %select_dynamic-update-slice_fusion.refs_1_), channel_id=1, source_target_pairs={{0,4},{1,5},{2,6},{3,7},{4,0},{5,1},{6,2},{7,3},{8,12},{9,13},{10,... | collective-permute-start | bytes 4718600 | tf_op jit(solution)/shard_map/ppermute | solution.py:97
  (29 other events, 214.8 us)

commit v5 on v4

--- a/solution.py
+++ b/solution.py
@@ -23,38 +23,37 @@
 ROWS = 512
 
 
-def gram_rows_kernel(scale, _place, left, right, *rest):
-    rest[-1][...] = scale * lax.dot_general(
-        left[...], right[...], (((0,), (0,)), ((), ())), preferred_element_type=jnp.float32
-    )
-
-
-def gram_rows(left, right, place, scale, rows_all, into=None):
+def gram_rows_kernel(scale, count, _place, left, *refs):
+    column = jnp.concatenate([ref[...] for ref in refs[:count]], axis=0)
+    refs[-1][...] = scale * lax.dot_general(
+        left[...], column, (((0,), (0,)), ((), ())), preferred_element_type=jnp.float32
+    )
+
+
+def gram_rows(left, chunks, place, scale, rows_all, into=None):
     depth, rows = left.shape
     steps = rows // ROWS
-    columns = right.shape[1]
+    columns = chunks[0].shape[1]
     grid = pltpu.PrefetchScalarGridSpec(
         num_scalar_prefetch=1,
         grid=(steps,),
-        in_specs=[
-            pl.BlockSpec((depth, ROWS), lambda i, place: (0, i)),
-            pl.BlockSpec((depth, columns), lambda i, place: (0, 0)),
-        ]
+        in_specs=[pl.BlockSpec((depth, ROWS), lambda i, place: (0, i))]
+        + [pl.BlockSpec(chunk.shape, lambda i, place: (0, 0)) for chunk in chunks]
         + ([] if into is None else [pl.BlockSpec(memory_space=pl.ANY)]),
         out_specs=pl.BlockSpec((ROWS, columns), lambda i, place: (place[0] * steps + i, 0)),
     )
     return pl.pallas_call(
-        lambda *refs: gram_rows_kernel(scale, *refs),
+        lambda *refs: gram_rows_kernel(scale, len(chunks), *refs),
         out_shape=jax.ShapeDtypeStruct((rows_all, columns), jnp.float32),
         grid_spec=grid,
-        input_output_aliases={} if into is None else {3: 0},
+        input_output_aliases={} if into is None else {2 + len(chunks): 0},
         compiler_params=pltpu.CompilerParams(vmem_limit_bytes=32 * 1024 * 1024),
         cost_estimate=pl.CostEstimate(
             flops=2 * depth * rows * columns,
             bytes_accessed=4 * rows * columns + 2 * depth * (rows + columns),
             transcendentals=0,
         ),
-    )(place, left, right, *([] if into is None else [into]))
+    )(place, left, *chunks, *([] if into is None else [into]))
 
 
 def normalize(hidden_states, sums, norm_gain, features):
@@ -158,7 +157,7 @@
     other_at = 1 - mine_at
 
     g0 = out_grads
-    g1 = along_z(g0, 1)
+    g1 = along_z(g0, 3)
     r0x, r0y = send(g0)
     sums = squares(hidden_states)
     sums = sums + core(sums)
@@ -166,36 +165,36 @@
     x0 = normalize(hidden_states, sums, norm_gain, width * n_dp)
     r0x, r0y, g1 = tie(r0x, r0y, g1)
     r1x, r1y = send(g1, (r0x, r0y))
-    x1 = along_z(x0, 1)
-    g2 = along_z(g1, 1)
-    g3 = along_z(g2, 1)
+    x1 = along_z(x0, 3)
+    g2 = along_z(g1, 3)
     r1x, r1y, g2 = tie(r1x, r1y, g2)
     r2x, r2y = send(g2, (r1x, r1y))
+    g3 = along_z(g2, 3)
     r2x, r2y, x0 = tie(r2x, r2y, x0)
     r3x, r3y = send(x0, (r2x, r2y))
-    x2 = along_z(x1, 1)
+    x2 = along_z(x1, 3)
     r3x, r3y, g3 = tie(r3x, r3y, g3)
     r4x, r4y = send(g3, (r3x, r3y))
     r4x, r4y, x1 = tie(r4x, r4y, x1)
     r5x, r5y = send(x1, (r4x, r4y))
-    x3 = along_z(x2, 1)
+    x3 = along_z(x2, 3)
     r5x, r5y, x2 = tie(r5x, r5y, x2)
     r6x, r6y = send(x2, (r5x, r5y))
-    r6x, r6y, x3 = tie(r6x, r6y, x3)
+    r6x, r6y, x3, g1, g2, g3 = tie(r6x, r6y, x3, g1, g2, g3)
     r7x, r7y = send(x3, (r6x, r6y))
     g_mine = assemble([0, 1, 2, 4], [g0, g1, g2, g3], [(r0x, r0y), (r1x, r1y), (r2x, r2y), (r3x, r3y), (r4x, r4y), (r5x, r5y), (r6x, r6y)])
     g_other = core(g_mine)
-    g_column = jnp.concatenate([g0, g1, g2, g3], axis=0)
-    g_factor = gram_rows(g_mine, g_column, mine_at, scale, rows_all)
-    r7x, r7y, g_factor, g_other, x0, x1, x2, x3 = tie(r7x, r7y, g_factor, g_other, x0, x1, x2, x3)
+    g_column = jnp.concatenate([g1, g2, g3], axis=0)
+    g_factor = gram_rows(g_mine, [g0, g_column], mine_at, scale, rows_all)
+    r7x, r7y, g_factor, g_other = tie(r7x, r7y, g_factor, g_other)
     r8x, r8y = send(x3, (r7x, r7y), last=True)
-    g_factor = gram_rows(g_other, g_column, other_at, scale, rows_all, g_factor)
+    g_factor = gram_rows(g_other, [g0, g_column], other_at, scale, rows_all, g_factor)
     x_column = jnp.concatenate([x0, x1, x2, x3], axis=0)
     r8x, r8y, x_column, g_factor = tie(r8x, r8y, x_column, g_factor)
     x_mine = assemble([3, 5, 6, 7], [x0, x1, x2, x3], [(r0x, r0y), (r1x, r1y), (r2x, r2y), (r3x, r3y), (r4x, r4y), (r5x, r5y), (r6x, r6y), (r7x, r7y), (r8x, r8y)])
     x_other = core(x_mine)
-    a_factor = gram_rows(x_mine, x_column, mine_at, scale, rows_all)
-    a_factor = gram_rows(x_other, x_column, other_at, scale, rows_all, a_factor)
+    a_factor = gram_rows(x_mine, [x_column], mine_at, scale, rows_all)
+    a_factor = gram_rows(x_other, [x_column], other_at, scale, rows_all, a_factor)
     return a_factor, g_factor
 
 

time: 91.2 us -> 90.4 us (level)
  waiting for transfers between devices: 31.5 us -> 23.1 us
  starting transfers between devices: 35.4 us -> 41.9 us
  Pallas kernels: 14 us -> 15 us
    ppermute x30, waiting for transfers between devices: 31.5 us -> 23.1 us  [swap(): return lax.ppermute(x, AXES, pairs)]
    ppermute x30, starting transfers between devices: 35.4 us -> 41.9 us  [swap(): return lax.ppermute(x, AXES, pairs)]
    pallas_call x4, Pallas kernels: 14 us -> 15 us  [gram_rows(): pl.pallas_call(lambda *refs: gram_rows_kernel(scale, len(chunks), *refs),...]
    unnamed x65 -> x54, local copies, waits for them, and re-layouts: 2.29 us -> 2.15 us
  transfers between devices with their start and end apart: 30 -> 30, of which waited for: 16 -> 14; matrix products, arithmetic and copies ran while one was open for 7% -> 7% of each run, Pallas kernels for 12% -> 13%
where the time goes in v5:
time: 90.4 us; the launch traced here: 89.8 us
  starting transfers between devices  41.9 us (46%)
  waiting for transfers between devices  23.1 us (26%)
  Pallas kernels  15 us (17%)
  other arithmetic  5.47 us (6%)
  local copies, waits for them, and re-layouts  3.23 us (4%)
  between operations  1.11 us (1%)
    ppermute x30, starting transfers between devices, swap(): return lax.ppermute(x, AXES, pairs)  41.9 us
    ppermute x30, waiting for transfers between devices, swap(): return lax.ppermute(x, AXES, pairs)  23.1 us
    pallas_call x4, Pallas kernels, gram_rows(): pl.pallas_call(lambda *refs: gram_rows_kernel(scale, len(chunks), *refs),...  15 us
    unnamed x54, local copies, waits for them, and re-layouts  2.15 us
    select_n x8, other arithmetic, send(): high = jnp.where(root, high, back[0])  1.92 us
  transfers between devices with their start and end apart: 30, of which 14 were waited for; matrix products, arithmetic and copies ran while one was open for 7% of the time, Pallas kernels for 13%

profile of v5, /device:TPU:0, one launch (start us, length us, event | category | flops | bytes accessed | tf_op | source)
XLA Modules:
  0.0 89.8 jit_solution(8470283586109643890)
XLA Ops:
  0.6 4.1 %collective-permute-start.2 = (bf16[192,1024]{1,0:T(8,128)(2,1)}, bf16[192,1024]{1,0:T(8,128)(2,1)S(1)}, u32[]{:S(2)}, u32[]{:S(2)}) collective-permute-start(bf16[192,1024]{1,0:T(8,128)(2,1)} %refs_2_.3), channel_id=1, source_target_pairs={{0,2},{1,0},{2,3},{3,1},{4,6},{5,4},{6,7},{7,5},{8,10},{9,8},{10,1... | collective-permute-start | bytes 1179656 | tf_op jit(solution)/shard_map/ppermute | solution.py:96
  4.7 1.0 %fusion.3 = (bf16[96,1024]{1,0:T(8,128)(2,1)S(1)}, bf16[96,1024]{1,0:T(8,128)(2,1)S(1)}) fusion(bf16[192,1024]{1,0:T(8,128)(2,1)} %refs_2_.3), kind=kLoop, calls=%fused_computation.42 | loop fusion | bytes 786432 | tf_op jit(solution)/shard_map/slice | solution.py:133
  5.8 1.6 %collective-permute-start.1 = (bf16[96,1024]{1,0:T(8,128)(2,1)S(1)}, bf16[96,1024]{1,0:T(8,128)(2,1)S(1)}, u32[]{:S(2)}, u32[]{:S(2)}) collective-permute-start(bf16[96,1024]{1,0:T(8,128)(2,1)S(1)} %get-tuple-element.84), channel_id=1, source_target_pairs={{0,16},{1,17},{2,18},{3,19},{4,20},{5,21},{6,22},{7,23},{8,24},{9,... | collective-permute-start | bytes 589832 | tf_op jit(solution)/shard_map/ppermute | solution.py:96
  7.4 1.5 %collective-permute-start = (bf16[96,1024]{1,0:T(8,128)(2,1)S(1)}, bf16[96,1024]{1,0:T(8,128)(2,1)S(1)}, u32[]{:S(2)}, u32[]{:S(2)}) collective-permute-start(bf16[96,1024]{1,0:T(8,128)(2,1)S(1)} %get-tuple-element.85), channel_id=1, source_target_pairs={{0,8},{1,9},{2,10},{3,11},{4,12},{5,13},{6,14},{7,15},{8,0},{9,1},... | collective-permute-start | bytes 589832 | tf_op jit(solution)/shard_map/ppermute | solution.py:96
  8.9 1.2 %fusion = f32[192]{0:T(256)S(1)} fusion(bf16[192,1024]{1,0:T(8,128)(2,1)} %param.3), kind=kLoop, calls=%fused_computation.3 | loop fusion | flops 589632 | bytes 393984 | tf_op jit(solution)/shard_map/reduce_sum | solution.py:68
  11.7 1.5 %collective-permute-start.10 = (f32[192,1]{0,1:T(1,128)S(1)}, f32[192,1]{0,1:T(1,128)S(1)}, u32[]{:S(2)}, u32[]{:S(2)}) collective-permute-start(f32[192,1]{0,1:T(1,128)S(1)} %add.24), channel_id=1, source_target_pairs={{0,16},{1,17},{2,18},{3,19},{4,20},{5,21},{6,22},{7,23},{8,24},{9,... | collective-permute-start | bytes 2312 | tf_op jit(solution)/shard_map/ppermute | solution.py:96
  13.2 1.5 %collective-permute-start.9 = (f32[192,1]{0,1:T(1,128)S(1)}, f32[192,1]{0,1:T(1,128)S(1)}, u32[]{:S(2)}, u32[]{:S(2)}) collective-permute-start(f32[192,1]{0,1:T(1,128)S(1)} %add.24), channel_id=1, source_target_pairs={{0,8},{1,9},{2,10},{3,11},{4,12},{5,13},{6,14},{7,15},{8,0},{9,1},... | collective-permute-start | bytes 2312 | tf_op jit(solution)/shard_map/ppermute | solution.py:96
  14.7 2.0 %collective-permute-start.5 = (bf16[192,1024]{1,0:T(8,128)(2,1)S(1)}, bf16[192,1024]{1,0:T(8,128)(2,1)S(1)}, u32[]{:S(2)}, u32[]{:S(2)}) collective-permute-start(bf16[192,1024]{1,0:T(8,128)(2,1)S(1)} %collective-permute-done.2), channel_id=1, source_target_pairs={{0,2},{1,0},{2,3},{3,1},{4,6},{5,4},{6,7},{7,5},{8,10},{9,8},{10,1... | collective-permute-start | bytes 1179656 | tf_op jit(solution)/shard_map/ppermute | solution.py:96
  16.7 1.6 %collective-permute-start.4 = (bf16[96,1024]{1,0:T(8,128)(2,1)S(1)}, bf16[96,1024]{1,0:T(8,128)(2,1)S(1)}, u32[]{:S(2)}, u32[]{:S(2)}) collective-permute-start(bf16[96,1024]{1,0:T(8,128)(2,1)S(1)} %get-tuple-element.82), channel_id=1, source_target_pairs={{0,16},{1,17},{2,18},{3,19},{4,20},{5,21},{6,22},{7,23},{8,24},{9,... | collective-permute-start | bytes 589832 | tf_op jit(solution)/shard_map/ppermute | solution.py:96
  18.3 1.5 %collective-permute-start.3 = (bf16[96,1024]{1,0:T(8,128)(2,1)S(1)}, bf16[96,1024]{1,0:T(8,128)(2,1)S(1)}, u32[]{:S(2)}, u32[]{:S(2)}) collective-permute-start(bf16[96,1024]{1,0:T(8,128)(2,1)S(1)} %get-tuple-element.83), channel_id=1, source_target_pairs={{0,8},{1,9},{2,10},{3,11},{4,12},{5,13},{6,14},{7,15},{8,0},{9,1},... | collective-permute-start | bytes 589832 | tf_op jit(solution)/shard_map/ppermute | solution.py:96
  19.8 2.6 %collective-permute-done.4 = bf16[96,1024]{1,0:T(8,128)(2,1)S(1)} collective-permute-done((bf16[96,1024]{1,0:T(8,128)(2,1)S(1)}, bf16[96,1024]{1,0:T(8,128)(2,1)S(1)}, u32[]{:S(2)}, u32[]{:S(2)}) %collective-permute-start.4) | collective-permute-done | bytes 196640 | tf_op jit(solution)/shard_map/ppermute | solution.py:96
  22.5 1.5 %collective-permute-done.3 = bf16[96,1024]{1,0:T(8,128)(2,1)S(1)} collective-permute-done((bf16[96,1024]{1,0:T(8,128)(2,1)S(1)}, bf16[96,1024]{1,0:T(8,128)(2,1)S(1)}, u32[]{:S(2)}, u32[]{:S(2)}) %collective-permute-start.3) | collective-permute-done | bytes 196640 | tf_op jit(solution)/shard_map/ppermute | solution.py:96
  24.0 1.2 %collective-permute-done.5 = bf16[192,1024]{1,0:T(8,128)(2,1)S(1)} collective-permute-done((bf16[192,1024]{1,0:T(8,128)(2,1)S(1)}, bf16[192,1024]{1,0:T(8,128)(2,1)S(1)}, u32[]{:S(2)}, u32[]{:S(2)}) %collective-permute-start.5) | collective-permute-done | bytes 393248 | tf_op jit(solution)/shard_map/ppermute | solution.py:96
  25.8 1.5 %collective-permute-start.6 = (bf16[96,1024]{1,0:T(8,128)(2,1)S(1)}, bf16[96,1024]{1,0:T(8,128)(2,1)S(1)}, u32[]{:S(2)}, u32[]{:S(2)}) collective-permute-start(bf16[96,1024]{1,0:T(8,128)(2,1)S(1)} %get-tuple-element.81), channel_id=1, source_target_pairs={{0,8},{1,9},{2,10},{3,11},{4,12},{5,13},{6,14},{7,15},{8,0},{9,1},... | collective-permute-start | bytes 589832 | tf_op jit(solution)/shard_map/ppermute | solution.py:96
  27.5 3.4 %collective-permute-start.14 = (bf16[192,1024]{1,0:T(8,128)(2,1)S(1)}, bf16[192,1024]{1,0:T(8,128)(2,1)S(1)}, u32[]{:S(2)}, u32[]{:S(2)}) collective-permute-start(bf16[192,1024]{1,0:T(8,128)(2,1)S(1)} %collective-permute-done.5), channel_id=1, source_target_pairs={{0,2},{1,0},{2,3},{3,1},{4,6},{5,4},{6,7},{7,5},{8,10},{9,8},{10,1... | collective-permute-start | bytes 1179656 | tf_op jit(solution)/shard_map/ppermute | solution.py:96
  31.9 1.5 %collective-permute-start.13 = (bf16[96,1024]{1,0:T(8,128)(2,1)S(1)}, bf16[96,1024]{1,0:T(8,128)(2,1)S(1)}, u32[]{:S(2)}, u32[]{:S(2)}) collective-permute-start(bf16[96,1024]{1,0:T(8,128)(2,1)S(1)} %get-tuple-element.78), channel_id=1, source_target_pairs={{0,16},{1,17},{2,18},{3,19},{4,20},{5,21},{6,22},{7,23},{8,24},{9,... | collective-permute-start | bytes 589832 | tf_op jit(solution)/shard_map/ppermute | solution.py:96
  34.0 3.4 %collective-permute-start.17 = (bf16[192,1024]{1,0:T(8,128)(2,1)S(1)}, bf16[192,1024]{1,0:T(8,128)(2,1)S(1)}, u32[]{:S(2)}, u32[]{:S(2)}) collective-permute-start(bf16[192,1024]{1,0:T(8,128)(2,1)S(1)} %fusion.2), channel_id=1, source_target_pairs={{0,2},{1,0},{2,3},{3,1},{4,6},{5,4},{6,7},{7,5},{8,10},{9,8},{10,1... | collective-permute-start | bytes 1179656 | tf_op jit(solution)/shard_map/ppermute | solution.py:96
  37.3 2.8 %collective-permute-done.14 = bf16[192,1024]{1,0:T(8,128)(2,1)S(1)} collective-permute-done((bf16[192,1024]{1,0:T(8,128)(2,1)S(1)}, bf16[192,1024]{1,0:T(8,128)(2,1)S(1)}, u32[]{:S(2)}, u32[]{:S(2)}) %collective-permute-start.14) | collective-permute-done | bytes 393248 | tf_op jit(solution)/shard_map/ppermute | solution.py:96
  40.3 2.1 %collective-permute-start.15 = (bf16[96,1024]{1,0:T(8,128)(2,1)S(1)}, bf16[96,1024]{1,0:T(8,128)(2,1)S(1)}, u32[]{:S(2)}, u32[]{:S(2)}) collective-permute-start(bf16[96,1024]{1,0:T(8,128)(2,1)S(1)} %get-tuple-element.77), channel_id=1, source_target_pairs={{0,8},{1,9},{2,10},{3,11},{4,12},{5,13},{6,14},{7,15},{8,0},{9,1},... | collective-permute-start | bytes 589832 | tf_op jit(solution)/shard_map/ppermute | solution.py:96
  42.4 2.9 %collective-permute-done.17 = bf16[192,1024]{1,0:T(8,128)(2,1)S(1)} collective-permute-done((bf16[192,1024]{1,0:T(8,128)(2,1)S(1)}, bf16[192,1024]{1,0:T(8,128)(2,1)S(1)}, u32[]{:S(2)}, u32[]{:S(2)}) %collective-permute-start.17) | collective-permute-done | bytes 393248 | tf_op jit(solution)/shard_map/ppermute | solution.py:96
  45.4 3.4 %collective-permute-start.20 = (bf16[192,1024]{1,0:T(8,128)(2,1)S(1)}, bf16[192,1024]{1,0:T(8,128)(2,1)S(1)}, u32[]{:S(2)}, u32[]{:S(2)}) collective-permute-start(bf16[192,1024]{1,0:T(8,128)(2,1)S(1)} %collective-permute-done.17), channel_id=1, source_target_pairs={{0,2},{1,0},{2,3},{3,1},{4,6},{5,4},{6,7},{7,5},{8,10},{9,8},{10,1... | collective-permute-start | bytes 1179656 | tf_op jit(solution)/shard_map/ppermute | solution.py:96
  50.0 4.6 %collective-permute-done.20 = bf16[192,1024]{1,0:T(8,128)(2,1)S(1)} collective-permute-done((bf16[192,1024]{1,0:T(8,128)(2,1)S(1)}, bf16[192,1024]{1,0:T(8,128)(2,1)S(1)}, u32[]{:S(2)}, u32[]{:S(2)}) %collective-permute-start.20) | collective-permute-done | bytes 393248 | tf_op jit(solution)/shard_map/ppermute | solution.py:96
  54.6 3.4 %collective-permute-start.23 = (bf16[192,1024]{1,0:T(8,128)(2,1)S(1)}, bf16[192,1024]{1,0:T(8,128)(2,1)S(1)}, u32[]{:S(2)}, u32[]{:S(2)}) collective-permute-start(bf16[192,1024]{1,0:T(8,128)(2,1)S(1)} %collective-permute-done.20), channel_id=1, source_target_pairs={{0,2},{1,0},{2,3},{3,1},{4,6},{5,4},{6,7},{7,5},{8,10},{9,8},{10,1... | collective-permute-start | bytes 1179656 | tf_op jit(solution)/shard_map/ppermute | solution.py:96
  59.6 3.7 %collective-permute-done.23 = bf16[192,1024]{1,0:T(8,128)(2,1)S(1)} collective-permute-done((bf16[192,1024]{1,0:T(8,128)(2,1)S(1)}, bf16[192,1024]{1,0:T(8,128)(2,1)S(1)}, u32[]{:S(2)}, u32[]{:S(2)}) %collective-permute-start.23) | collective-permute-done | bytes 393248 | tf_op jit(solution)/shard_map/ppermute | solution.py:96
  65.3 1.2 %broadcast_select_fusion.2 = (bf16[96,1024]{1,0:T(8,128)(2,1)}, bf16[96,1024]{1,0:T(8,128)(2,1)}, bf16[768,1024]{1,0:T(8,128)(2,1)S(1)}, bf16[768,1024]{1,0:T(8,128)(2,1)S(1)}) fusion(bf16[96,1024]{1,0:T(8,128)(2,1)S(1)} %collective-permute-done.21, pred[]{:T(512)S(6)} %eq.5, bf16[192,1024]{1,0:T(8,128)(2,1)S(1)} %collective-permute-done.23, ...), kind=kLoop, calls=%fused_computation.30 | loop fusion | flops 786431 | bytes 2555908 | tf_op jit(solution)/shard_map/jit(_where)/select_n | solution.py:136
  66.5 1.4 %collective-permute-start.25 = (bf16[96,1024]{1,0:T(8,128)(2,1)}, bf16[96,1024]{1,0:T(8,128)(2,1)S(1)}, u32[]{:S(2)}, u32[]{:S(2)}) collective-permute-start(bf16[96,1024]{1,0:T(8,128)(2,1)} %get-tuple-element.70), channel_id=1, source_target_pairs={{0,16},{1,17},{2,18},{3,19},{4,20},{5,21},{6,22},{7,23},{8,24},{9,... | collective-permute-start | bytes 589832 | tf_op jit(solution)/shard_map/ppermute | solution.py:96
  68.4 1.0 %constant_dynamic-update-slice_fusion.2 = bf16[576,1024]{1,0:T(8,128)(2,1)S(1)} fusion(bf16[192,1024]{1,0:T(8,128)(2,1)} %copy-done.11), kind=kLoop, calls=%fused_computation.40 | loop fusion | bytes 786432
  69.5 1.0 %constant_dynamic-update-slice_fusion.1 = bf16[576,1024]{1,0:T(8,128)(2,1)S(1)} fusion(bf16[576,1024]{1,0:T(8,128)(2,1)S(1)} %constant_dynamic-update-slice_fusion.2, bf16[192,1024]{1,0:T(8,128)(2,1)} %copy-done.12), kind=kLoop, calls=%fused_computation.39 | loop fusion | bytes 786432
  70.8 3.5 %shard_map.50.refs_4_ = f32[2048,1024]{1,0:T(8,128)} custom-call(s32[1]{0:T(128)} %bitcast.refs_0_, bf16[768,1024]{1,0:T(8,128)(2,1)S(1)} %get-tuple-element.88.refs_1_, bf16[192,1024]{1,0:T(8,128)(2,1)S(1)} %copy-done, bf16[576,1024]{1,0:T(8,128)(2,1)S(1)} %constant_dynamic-update-slice_fusion.refs_3_), custom_call_target="tpu_custom_call" | custom-call | flops 1610612736 | bytes 7340032 | tf_op jit(solution)/shard_map/pallas_call | solution.py:45
  77.2 4.5 %shard_map.51 = f32[2048,1024]{1,0:T(8,128)} custom-call(s32[1]{0:T(128)S(6)} %sub.7.refs_0_, bf16[768,1024]{1,0:T(8,128)(2,1)} %collective-permute-done.26.refs_1_, bf16[192,1024]{1,0:T(8,128)(2,1)S(1)} %copy-done, bf16[576,1024]{1,0:T(8,128)(2,1)S(1)} %constant_dynamic-update-slice_fusion.refs_3_, ...), custom_call_target="tpu_custom_call", output_to_operand_aliasing={{}: (4, {})} | custom-call | flops 1610612736 | bytes 7340032 | tf_op jit(solution)/shard_map/pallas_call | solution.py:45
  82.8 3.5 %shard_map.52.refs_3_ = f32[2048,1024]{1,0:T(8,128)} custom-call(s32[1]{0:T(128)} %bitcast.refs_0_, bf16[768,1024]{1,0:T(8,128)(2,1)S(1)} %select_dynamic-update-slice_fusion.refs_1_, bf16[768,1024]{1,0:T(8,128)(2,1)S(1)} %pad_maximum_fusion.refs_2_), custom_call_target="tpu_custom_call" | custom-call | flops 1610612736 | bytes 7340032 | tf_op jit(solution)/shard_map/pallas_call | solution.py:45
  86.3 3.5 %shard_map.53 = f32[2048,1024]{1,0:T(8,128)} custom-call(s32[1]{0:T(128)S(6)} %sub.7.refs_0_, bf16[768,1024]{1,0:T(8,128)(2,1)S(1)} %collective-permute-done.29.refs_1_, bf16[768,1024]{1,0:T(8,128)(2,1)S(1)} %pad_maximum_fusion.refs_2_, f32[2048,1024]{1,0:T(8,128)} %shard_map.52.refs_3_), custom_call_target="tpu_custom_call", output_to_operand_aliasing={{}: (3, {})} | custom-call | flops 1610612736 | bytes 7340032 | tf_op jit(solution)/shard_map/pallas_call | solution.py:45
  (114 shorter events, 13.6 us)
Async XLA Ops:
  0.6 14.1 %collective-permute-start.2 = (bf16[192,1024]{1,0:T(8,128)(2,1)}, bf16[192,1024]{1,0:T(8,128)(2,1)S(1)}, u32[]{:S(2)}, u32[]{:S(2)}) collective-permute-start(bf16[192,1024]{1,0:T(8,128)(2,1)} %refs_2_.3), channel_id=1, source_target_pairs={{0,2},{1,0},{2,3},{3,1},{4,6},{5,4},{6,7},{7,5},{8,10},{9,8},{10,1... | collective-permute-start | bytes 1179656 | tf_op jit(solution)/shard_map/ppermute | solution.py:96
  5.8 7.4 %collective-permute-start.1 = (bf16[96,1024]{1,0:T(8,128)(2,1)S(1)}, bf16[96,1024]{1,0:T(8,128)(2,1)S(1)}, u32[]{:S(2)}, u32[]{:S(2)}) collective-permute-start(bf16[96,1024]{1,0:T(8,128)(2,1)S(1)} %get-tuple-element.84), channel_id=1, source_target_pairs={{0,16},{1,17},{2,18},{3,19},{4,20},{5,21},{6,22},{7,23},{8,24},{9,... | collective-permute-start | bytes 589832 | tf_op jit(solution)/shard_map/ppermute | solution.py:96
  7.4 7.3 %collective-permute-start = (bf16[96,1024]{1,0:T(8,128)(2,1)S(1)}, bf16[96,1024]{1,0:T(8,128)(2,1)S(1)}, u32[]{:S(2)}, u32[]{:S(2)}) collective-permute-start(bf16[96,1024]{1,0:T(8,128)(2,1)S(1)} %get-tuple-element.85), channel_id=1, source_target_pairs={{0,8},{1,9},{2,10},{3,11},{4,12},{5,13},{6,14},{7,15},{8,0},{9,1},... | collective-permute-start | bytes 589832 | tf_op jit(solution)/shard_map/ppermute | solution.py:96
  10.0 1.2 %collective-permute-start.8 = (f32[192,1]{0,1:T(1,128)S(1)}, f32[192,1]{0,1:T(1,128)S(1)}, u32[]{:S(2)}, u32[]{:S(2)}) collective-permute-start(f32[192,1]{0,1:T(1,128)S(1)} %bitcast.5), channel_id=1, source_target_pairs={{0,4},{1,5},{2,6},{3,7},{4,0},{5,1},{6,2},{7,3},{8,12},{9,13},{10,... | collective-permute-start | bytes 2312 | tf_op jit(solution)/shard_map/ppermute | solution.py:96
  11.2 7.1 %collective-permute-start.11 = (f32[192,1]{0,1:T(1,128)S(1)}, f32[192,1]{0,1:T(1,128)S(1)}, u32[]{:S(2)}, u32[]{:S(2)}) collective-permute-start(f32[192,1]{0,1:T(1,128)S(1)} %add.24), channel_id=1, source_target_pairs={{0,24},{1,25},{2,26},{3,27},{4,28},{5,29},{6,30},{7,31},{8,16},{9,... | collective-permute-start | bytes 2312 | tf_op jit(solution)/shard_map/ppermute | solution.py:96
  11.7 8.1 %collective-permute-start.10 = (f32[192,1]{0,1:T(1,128)S(1)}, f32[192,1]{0,1:T(1,128)S(1)}, u32[]{:S(2)}, u32[]{:S(2)}) collective-permute-start(f32[192,1]{0,1:T(1,128)S(1)} %add.24), channel_id=1, source_target_pairs={{0,16},{1,17},{2,18},{3,19},{4,20},{5,21},{6,22},{7,23},{8,24},{9,... | collective-permute-start | bytes 2312 | tf_op jit(solution)/shard_map/ppermute | solution.py:96
  13.2 6.6 %collective-permute-start.9 = (f32[192,1]{0,1:T(1,128)S(1)}, f32[192,1]{0,1:T(1,128)S(1)}, u32[]{:S(2)}, u32[]{:S(2)}) collective-permute-start(f32[192,1]{0,1:T(1,128)S(1)} %add.24), channel_id=1, source_target_pairs={{0,8},{1,9},{2,10},{3,11},{4,12},{5,13},{6,14},{7,15},{8,0},{9,1},... | collective-permute-start | bytes 2312 | tf_op jit(solution)/shard_map/ppermute | solution.py:96
  14.7 50.0 %copy-start.11 = (bf16[192,1024]{1,0:T(8,128)(2,1)}, bf16[192,1024]{1,0:T(8,128)(2,1)S(1)}, u32[]{:S(2)}) copy-start(bf16[192,1024]{1,0:T(8,128)(2,1)S(1)} %collective-permute-done.2) | copy-start | bytes 1179652
  14.7 10.4 %collective-permute-start.5 = (bf16[192,1024]{1,0:T(8,128)(2,1)S(1)}, bf16[192,1024]{1,0:T(8,128)(2,1)S(1)}, u32[]{:S(2)}, u32[]{:S(2)}) collective-permute-start(bf16[192,1024]{1,0:T(8,128)(2,1)S(1)} %collective-permute-done.2), channel_id=1, source_target_pairs={{0,2},{1,0},{2,3},{3,1},{4,6},{5,4},{6,7},{7,5},{8,10},{9,8},{10,1... | collective-permute-start | bytes 1179656 | tf_op jit(solution)/shard_map/ppermute | solution.py:96
  16.7 5.7 %collective-permute-start.4 = (bf16[96,1024]{1,0:T(8,128)(2,1)S(1)}, bf16[96,1024]{1,0:T(8,128)(2,1)S(1)}, u32[]{:S(2)}, u32[]{:S(2)}) collective-permute-start(bf16[96,1024]{1,0:T(8,128)(2,1)S(1)} %get-tuple-element.82), channel_id=1, source_target_pairs={{0,16},{1,17},{2,18},{3,19},{4,20},{5,21},{6,22},{7,23},{8,24},{9,... | collective-permute-start | bytes 589832 | tf_op jit(solution)/shard_map/ppermute | solution.py:96
  18.3 5.7 %collective-permute-start.3 = (bf16[96,1024]{1,0:T(8,128)(2,1)S(1)}, bf16[96,1024]{1,0:T(8,128)(2,1)S(1)}, u32[]{:S(2)}, u32[]{:S(2)}) collective-permute-start(bf16[96,1024]{1,0:T(8,128)(2,1)S(1)} %get-tuple-element.83), channel_id=1, source_target_pairs={{0,8},{1,9},{2,10},{3,11},{4,12},{5,13},{6,14},{7,15},{8,0},{9,1},... | collective-permute-start | bytes 589832 | tf_op jit(solution)/shard_map/ppermute | solution.py:96
  25.1 39.8 %copy-start.12 = (bf16[192,1024]{1,0:T(8,128)(2,1)}, bf16[192,1024]{1,0:T(8,128)(2,1)S(1)}, u32[]{:S(2)}) copy-start(bf16[192,1024]{1,0:T(8,128)(2,1)S(1)} %collective-permute-done.5) | copy-start | bytes 1179652
  25.2 5.7 %collective-permute-start.7 = (bf16[96,1024]{1,0:T(8,128)(2,1)S(1)}, bf16[96,1024]{1,0:T(8,128)(2,1)S(1)}, u32[]{:S(2)}, u32[]{:S(2)}) collective-permute-start(bf16[96,1024]{1,0:T(8,128)(2,1)S(1)} %get-tuple-element.80), channel_id=1, source_target_pairs={{0,16},{1,17},{2,18},{3,19},{4,20},{5,21},{6,22},{7,23},{8,24},{9,... | collective-permute-start | bytes 589832 | tf_op jit(solution)/shard_map/ppermute | solution.py:96
  25.8 5.7 %collective-permute-start.6 = (bf16[96,1024]{1,0:T(8,128)(2,1)S(1)}, bf16[96,1024]{1,0:T(8,128)(2,1)S(1)}, u32[]{:S(2)}, u32[]{:S(2)}) collective-permute-start(bf16[96,1024]{1,0:T(8,128)(2,1)S(1)} %get-tuple-element.81), channel_id=1, source_target_pairs={{0,8},{1,9},{2,10},{3,11},{4,12},{5,13},{6,14},{7,15},{8,0},{9,1},... | collective-permute-start | bytes 589832 | tf_op jit(solution)/shard_map/ppermute | solution.py:96
  27.5 12.7 %collective-permute-start.14 = (bf16[192,1024]{1,0:T(8,128)(2,1)S(1)}, bf16[192,1024]{1,0:T(8,128)(2,1)S(1)}, u32[]{:S(2)}, u32[]{:S(2)}) collective-permute-start(bf16[192,1024]{1,0:T(8,128)(2,1)S(1)} %collective-permute-done.5), channel_id=1, source_target_pairs={{0,2},{1,0},{2,3},{3,1},{4,6},{5,4},{6,7},{7,5},{8,10},{9,8},{10,1... | collective-permute-start | bytes 1179656 | tf_op jit(solution)/shard_map/ppermute | solution.py:96
  31.9 8.3 %collective-permute-start.13 = (bf16[96,1024]{1,0:T(8,128)(2,1)S(1)}, bf16[96,1024]{1,0:T(8,128)(2,1)S(1)}, u32[]{:S(2)}, u32[]{:S(2)}) collective-permute-start(bf16[96,1024]{1,0:T(8,128)(2,1)S(1)} %get-tuple-element.78), channel_id=1, source_target_pairs={{0,16},{1,17},{2,18},{3,19},{4,20},{5,21},{6,22},{7,23},{8,24},{9,... | collective-permute-start | bytes 589832 | tf_op jit(solution)/shard_map/ppermute | solution.py:96
  33.4 6.8 %collective-permute-start.12 = (bf16[96,1024]{1,0:T(8,128)(2,1)S(1)}, bf16[96,1024]{1,0:T(8,128)(2,1)S(1)}, u32[]{:S(2)}, u32[]{:S(2)}) collective-permute-start(bf16[96,1024]{1,0:T(8,128)(2,1)S(1)} %get-tuple-element.79), channel_id=1, source_target_pairs={{0,8},{1,9},{2,10},{3,11},{4,12},{5,13},{6,14},{7,15},{8,0},{9,1},... | collective-permute-start | bytes 589832 | tf_op jit(solution)/shard_map/ppermute | solution.py:96
  34.0 11.4 %collective-permute-start.17 = (bf16[192,1024]{1,0:T(8,128)(2,1)S(1)}, bf16[192,1024]{1,0:T(8,128)(2,1)S(1)}, u32[]{:S(2)}, u32[]{:S(2)}) collective-permute-start(bf16[192,1024]{1,0:T(8,128)(2,1)S(1)} %fusion.2), channel_id=1, source_target_pairs={{0,2},{1,0},{2,3},{3,1},{4,6},{5,4},{6,7},{7,5},{8,10},{9,8},{10,1... | collective-permute-start | bytes 1179656 | tf_op jit(solution)/shard_map/ppermute | solution.py:96
  40.2 8.5 %collective-permute-start.16 = (bf16[96,1024]{1,0:T(8,128)(2,1)S(1)}, bf16[96,1024]{1,0:T(8,128)(2,1)S(1)}, u32[]{:S(2)}, u32[]{:S(2)}) collective-permute-start(bf16[96,1024]{1,0:T(8,128)(2,1)S(1)} %get-tuple-element.76), channel_id=1, source_target_pairs={{0,16},{1,17},{2,18},{3,19},{4,20},{5,21},{6,22},{7,23},{8,24},{9,... | collective-permute-start | bytes 589832 | tf_op jit(solution)/shard_map/ppermute | solution.py:96
  40.3 8.4 %collective-permute-start.15 = (bf16[96,1024]{1,0:T(8,128)(2,1)S(1)}, bf16[96,1024]{1,0:T(8,128)(2,1)S(1)}, u32[]{:S(2)}, u32[]{:S(2)}) collective-permute-start(bf16[96,1024]{1,0:T(8,128)(2,1)S(1)} %get-tuple-element.77), channel_id=1, source_target_pairs={{0,8},{1,9},{2,10},{3,11},{4,12},{5,13},{6,14},{7,15},{8,0},{9,1},... | collective-permute-start | bytes 589832 | tf_op jit(solution)/shard_map/ppermute | solution.py:96
  45.4 9.3 %collective-permute-start.20 = (bf16[192,1024]{1,0:T(8,128)(2,1)S(1)}, bf16[192,1024]{1,0:T(8,128)(2,1)S(1)}, u32[]{:S(2)}, u32[]{:S(2)}) collective-permute-start(bf16[192,1024]{1,0:T(8,128)(2,1)S(1)} %collective-permute-done.17), channel_id=1, source_target_pairs={{0,2},{1,0},{2,3},{3,1},{4,6},{5,4},{6,7},{7,5},{8,10},{9,8},{10,1... | collective-permute-start | bytes 1179656 | tf_op jit(solution)/shard_map/ppermute | solution.py:96
  48.8 9.2 %collective-permute-start.19 = (bf16[96,1024]{1,0:T(8,128)(2,1)S(1)}, bf16[96,1024]{1,0:T(8,128)(2,1)S(1)}, u32[]{:S(2)}, u32[]{:S(2)}) collective-permute-start(bf16[96,1024]{1,0:T(8,128)(2,1)S(1)} %get-tuple-element.74), channel_id=1, source_target_pairs={{0,16},{1,17},{2,18},{3,19},{4,20},{5,21},{6,22},{7,23},{8,24},{9,... | collective-permute-start | bytes 589832 | tf_op jit(solution)/shard_map/ppermute | solution.py:96
  49.4 8.7 %collective-permute-start.18 = (bf16[96,1024]{1,0:T(8,128)(2,1)S(1)}, bf16[96,1024]{1,0:T(8,128)(2,1)S(1)}, u32[]{:S(2)}, u32[]{:S(2)}) collective-permute-start(bf16[96,1024]{1,0:T(8,128)(2,1)S(1)} %get-tuple-element.75), channel_id=1, source_target_pairs={{0,8},{1,9},{2,10},{3,11},{4,12},{5,13},{6,14},{7,15},{8,0},{9,1},... | collective-permute-start | bytes 589832 | tf_op jit(solution)/shard_map/ppermute | solution.py:96
  54.6 8.7 %collective-permute-start.23 = (bf16[192,1024]{1,0:T(8,128)(2,1)S(1)}, bf16[192,1024]{1,0:T(8,128)(2,1)S(1)}, u32[]{:S(2)}, u32[]{:S(2)}) collective-permute-start(bf16[192,1024]{1,0:T(8,128)(2,1)S(1)} %collective-permute-done.20), channel_id=1, source_target_pairs={{0,2},{1,0},{2,3},{3,1},{4,6},{5,4},{6,7},{7,5},{8,10},{9,8},{10,1... | collective-permute-start | bytes 1179656 | tf_op jit(solution)/shard_map/ppermute | solution.py:96
  58.1 5.7 %collective-permute-start.22 = (bf16[96,1024]{1,0:T(8,128)(2,1)S(1)}, bf16[96,1024]{1,0:T(8,128)(2,1)S(1)}, u32[]{:S(2)}, u32[]{:S(2)}) collective-permute-start(bf16[96,1024]{1,0:T(8,128)(2,1)S(1)} %get-tuple-element.72), channel_id=1, source_target_pairs={{0,16},{1,17},{2,18},{3,19},{4,20},{5,21},{6,22},{7,23},{8,24},{9,... | collective-permute-start | bytes 589832 | tf_op jit(solution)/shard_map/ppermute | solution.py:96
  58.9 5.7 %collective-permute-start.21 = (bf16[96,1024]{1,0:T(8,128)(2,1)S(1)}, bf16[96,1024]{1,0:T(8,128)(2,1)S(1)}, u32[]{:S(2)}, u32[]{:S(2)}) collective-permute-start(bf16[96,1024]{1,0:T(8,128)(2,1)S(1)} %get-tuple-element.73), channel_id=1, source_target_pairs={{0,8},{1,9},{2,10},{3,11},{4,12},{5,13},{6,14},{7,15},{8,0},{9,1},... | collective-permute-start | bytes 589832 | tf_op jit(solution)/shard_map/ppermute | solution.py:96
  66.5 8.6 %collective-permute-start.26 = (bf16[768,1024]{1,0:T(8,128)(2,1)S(1)}, bf16[768,1024]{1,0:T(8,128)(2,1)}, u32[]{:S(2)}, u32[]{:S(2)}) collective-permute-start(bf16[768,1024]{1,0:T(8,128)(2,1)S(1)} %get-tuple-element.88.refs_1_), channel_id=1, source_target_pairs={{0,4},{1,5},{2,6},{3,7},{4,0},{5,1},{6,2},{7,3},{8,12},{9,13},{10,... | collective-permute-start | bytes 4718600 | tf_op jit(solution)/shard_map/ppermute | solution.py:96
  66.5 7.7 %collective-permute-start.25 = (bf16[96,1024]{1,0:T(8,128)(2,1)}, bf16[96,1024]{1,0:T(8,128)(2,1)S(1)}, u32[]{:S(2)}, u32[]{:S(2)}) collective-permute-start(bf16[96,1024]{1,0:T(8,128)(2,1)} %get-tuple-element.70), channel_id=1, source_target_pairs={{0,16},{1,17},{2,18},{3,19},{4,20},{5,21},{6,22},{7,23},{8,24},{9,... | collective-permute-start | bytes 589832 | tf_op jit(solution)/shard_map/ppermute | solution.py:96
  67.9 7.2 %collective-permute-start.24 = (bf16[96,1024]{1,0:T(8,128)(2,1)}, bf16[96,1024]{1,0:T(8,128)(2,1)S(1)}, u32[]{:S(2)}, u32[]{:S(2)}) collective-permute-start(bf16[96,1024]{1,0:T(8,128)(2,1)} %get-tuple-element.71), channel_id=1, source_target_pairs={{0,8},{1,9},{2,10},{3,11},{4,12},{5,13},{6,14},{7,15},{8,0},{9,1},... | collective-permute-start | bytes 589832 | tf_op jit(solution)/shard_map/ppermute | solution.py:96
  75.6 6.3 %collective-permute-start.28 = (bf16[96,1024]{1,0:T(8,128)(2,1)S(1)}, bf16[96,1024]{1,0:T(8,128)(2,1)S(1)}, u32[]{:S(2)}, u32[]{:S(2)}) collective-permute-start(bf16[96,1024]{1,0:T(8,128)(2,1)S(1)} %get-tuple-element.66), channel_id=1, source_target_pairs={{0,16},{1,17},{2,18},{3,19},{4,20},{5,21},{6,22},{7,23},{8,24},{9,... | collective-permute-start | bytes 589832 | tf_op jit(solution)/shard_map/ppermute | solution.py:96
  76.4 5.9 %collective-permute-start.27 = (bf16[96,1024]{1,0:T(8,128)(2,1)S(1)}, bf16[96,1024]{1,0:T(8,128)(2,1)S(1)}, u32[]{:S(2)}, u32[]{:S(2)}) collective-permute-start(bf16[96,1024]{1,0:T(8,128)(2,1)S(1)} %get-tuple-element.67), channel_id=1, source_target_pairs={{0,8},{1,9},{2,10},{3,11},{4,12},{5,13},{6,14},{7,15},{8,0},{9,1},... | collective-permute-start | bytes 589832 | tf_op jit(solution)/shard_map/ppermute | solution.py:96
  82.7 3.6 %collective-permute-start.29 = (bf16[768,1024]{1,0:T(8,128)(2,1)S(1)}, bf16[768,1024]{1,0:T(8,128)(2,1)S(1)}, u32[]{:S(2)}, u32[]{:S(2)}) collective-permute-start(bf16[768,1024]{1,0:T(8,128)(2,1)S(1)} %select_dynamic-update-slice_fusion.refs_1_), channel_id=1, source_target_pairs={{0,4},{1,5},{2,6},{3,7},{4,0},{5,1},{6,2},{7,3},{8,12},{9,13},{10,... | collective-permute-start | bytes 4718600 | tf_op jit(solution)/shard_map/ppermute | solution.py:96
  (24 other events, 239.3 us)

commit v6 on v5

--- a/solution.py
+++ b/solution.py
@@ -20,32 +20,40 @@
     )
 
 
-ROWS = 512
-
-
-def gram_rows_kernel(scale, count, _place, left, *refs):
+TILES = (8, 4, 4)
+
+
+def gram_rows_kernel(scale, count, place, left, *refs):
+    out, tiles, sems = refs[-3:]
     column = jnp.concatenate([ref[...] for ref in refs[:count]], axis=0)
-    refs[-1][...] = scale * lax.dot_general(
-        left[...], column, (((0,), (0,)), ((), ())), preferred_element_type=jnp.float32
-    )
+    rows = left.shape[1]
+    base = pl.multiple_of(place[0] * rows, rows)
+    copies, start = [], 0
+    for part, size in enumerate(TILES):
+        size = size * rows // 16
+        tiles[pl.ds(start, size)] = scale * lax.dot_general(
+            left[:, pl.ds(start, size)], column, (((0,), (0,)), ((), ())), preferred_element_type=jnp.float32
+        )
+        copies.append(
+            pltpu.make_async_copy(tiles.at[pl.ds(start, size)], out.at[pl.ds(base + start, size)], sems.at[part])
+        )
+        copies[-1].start()
+        start += size
+    for copy in copies:
+        copy.wait()
 
 
 def gram_rows(left, chunks, place, scale, rows_all, into=None):
     depth, rows = left.shape
-    steps = rows // ROWS
     columns = chunks[0].shape[1]
-    grid = pltpu.PrefetchScalarGridSpec(
-        num_scalar_prefetch=1,
-        grid=(steps,),
-        in_specs=[pl.BlockSpec((depth, ROWS), lambda i, place: (0, i))]
-        + [pl.BlockSpec(chunk.shape, lambda i, place: (0, 0)) for chunk in chunks]
-        + ([] if into is None else [pl.BlockSpec(memory_space=pl.ANY)]),
-        out_specs=pl.BlockSpec((ROWS, columns), lambda i, place: (place[0] * steps + i, 0)),
-    )
     return pl.pallas_call(
         lambda *refs: gram_rows_kernel(scale, len(chunks), *refs),
         out_shape=jax.ShapeDtypeStruct((rows_all, columns), jnp.float32),
-        grid_spec=grid,
+        in_specs=[pl.BlockSpec(memory_space=pltpu.SMEM)]
+        + [pl.BlockSpec(memory_space=pltpu.VMEM)] * (1 + len(chunks))
+        + ([] if into is None else [pl.BlockSpec(memory_space=pl.ANY)]),
+        out_specs=pl.BlockSpec(memory_space=pl.ANY),
+        scratch_shapes=[pltpu.VMEM((rows, columns), jnp.float32), pltpu.SemaphoreType.DMA((len(TILES),))],
         input_output_aliases={} if into is None else {2 + len(chunks): 0},
         compiler_params=pltpu.CompilerParams(vmem_limit_bytes=32 * 1024 * 1024),
         cost_estimate=pl.CostEstimate(

time: 90.4 us -> 89.6 us (level)
  Pallas kernels: 15 us -> 13.6 us
    pallas_call x4, Pallas kernels: 15 us -> 13.6 us  [gram_rows(): pl.pallas_call(lambda *refs: gram_rows_kernel(scale, len(chunks), *refs),...]
  transfers between devices with their start and end apart: 30 -> 30, of which waited for: 14 -> 16; matrix products, arithmetic and copies ran while one was open for 7% -> 7% of each run, Pallas kernels for 13% -> 12%
where the time goes in v6:
time: 89.6 us; the launch traced here: 89.3 us
  starting transfers between devices  41.9 us (47%)
  waiting for transfers between devices  23.9 us (27%)
  Pallas kernels  13.6 us (15%)
  other arithmetic  5.47 us (6%)
  local copies, waits for them, and re-layouts  3.23 us (4%)
  between operations  1.14 us (1%)
    ppermute x30, starting transfers between devices, swap(): return lax.ppermute(x, AXES, pairs)  41.9 us
    ppermute x30, waiting for transfers between devices, swap(): return lax.ppermute(x, AXES, pairs)  23.9 us
    pallas_call x4, Pallas kernels, gram_rows(): pl.pallas_call(lambda *refs: gram_rows_kernel(scale, len(chunks), *refs),...  13.6 us
    unnamed x54, local copies, waits for them, and re-layouts  2.15 us
    select_n x8, other arithmetic, send(): high = jnp.where(root, high, back[0])  1.92 us
  transfers between devices with their start and end apart: 30, of which 16 were waited for; matrix products, arithmetic and copies ran while one was open for 7% of the time, Pallas kernels for 12%

profile of v6, /device:TPU:0, one launch (start us, length us, event | category | flops | bytes accessed | tf_op | source)
XLA Modules:
  0.0 89.3 jit_solution(15164281773379597051)
XLA Ops:
  0.6 4.1 %collective-permute-start.2 = (bf16[192,1024]{1,0:T(8,128)(2,1)}, bf16[192,1024]{1,0:T(8,128)(2,1)S(1)}, u32[]{:S(2)}, u32[]{:S(2)}) collective-permute-start(bf16[192,1024]{1,0:T(8,128)(2,1)} %refs_2_.3), channel_id=1, source_target_pairs={{0,2},{1,0},{2,3},{3,1},{4,6},{5,4},{6,7},{7,5},{8,10},{9,8},{10,1... | collective-permute-start | bytes 1179656 | tf_op jit(solution)/shard_map/ppermute | solution.py:104
  4.7 1.0 %fusion.3 = (bf16[96,1024]{1,0:T(8,128)(2,1)S(1)}, bf16[96,1024]{1,0:T(8,128)(2,1)S(1)}) fusion(bf16[192,1024]{1,0:T(8,128)(2,1)} %refs_2_.3), kind=kLoop, calls=%fused_computation.42 | loop fusion | bytes 786432 | tf_op jit(solution)/shard_map/slice | solution.py:141
  5.8 1.6 %collective-permute-start.1 = (bf16[96,1024]{1,0:T(8,128)(2,1)S(1)}, bf16[96,1024]{1,0:T(8,128)(2,1)S(1)}, u32[]{:S(2)}, u32[]{:S(2)}) collective-permute-start(bf16[96,1024]{1,0:T(8,128)(2,1)S(1)} %get-tuple-element.84), channel_id=1, source_target_pairs={{0,16},{1,17},{2,18},{3,19},{4,20},{5,21},{6,22},{7,23},{8,24},{9,... | collective-permute-start | bytes 589832 | tf_op jit(solution)/shard_map/ppermute | solution.py:104
  7.4 1.5 %collective-permute-start = (bf16[96,1024]{1,0:T(8,128)(2,1)S(1)}, bf16[96,1024]{1,0:T(8,128)(2,1)S(1)}, u32[]{:S(2)}, u32[]{:S(2)}) collective-permute-start(bf16[96,1024]{1,0:T(8,128)(2,1)S(1)} %get-tuple-element.85), channel_id=1, source_target_pairs={{0,8},{1,9},{2,10},{3,11},{4,12},{5,13},{6,14},{7,15},{8,0},{9,1},... | collective-permute-start | bytes 589832 | tf_op jit(solution)/shard_map/ppermute | solution.py:104
  8.9 1.2 %fusion = f32[192]{0:T(256)S(1)} fusion(bf16[192,1024]{1,0:T(8,128)(2,1)} %param.3), kind=kLoop, calls=%fused_computation.3 | loop fusion | flops 589632 | bytes 393984 | tf_op jit(solution)/shard_map/reduce_sum | solution.py:76
  11.7 1.5 %collective-permute-start.10 = (f32[192,1]{0,1:T(1,128)S(1)}, f32[192,1]{0,1:T(1,128)S(1)}, u32[]{:S(2)}, u32[]{:S(2)}) collective-permute-start(f32[192,1]{0,1:T(1,128)S(1)} %add.24), channel_id=1, source_target_pairs={{0,16},{1,17},{2,18},{3,19},{4,20},{5,21},{6,22},{7,23},{8,24},{9,... | collective-permute-start | bytes 2312 | tf_op jit(solution)/shard_map/ppermute | solution.py:104
  13.2 1.5 %collective-permute-start.9 = (f32[192,1]{0,1:T(1,128)S(1)}, f32[192,1]{0,1:T(1,128)S(1)}, u32[]{:S(2)}, u32[]{:S(2)}) collective-permute-start(f32[192,1]{0,1:T(1,128)S(1)} %add.24), channel_id=1, source_target_pairs={{0,8},{1,9},{2,10},{3,11},{4,12},{5,13},{6,14},{7,15},{8,0},{9,1},... | collective-permute-start | bytes 2312 | tf_op jit(solution)/shard_map/ppermute | solution.py:104
  14.7 2.0 %collective-permute-start.5 = (bf16[192,1024]{1,0:T(8,128)(2,1)S(1)}, bf16[192,1024]{1,0:T(8,128)(2,1)S(1)}, u32[]{:S(2)}, u32[]{:S(2)}) collective-permute-start(bf16[192,1024]{1,0:T(8,128)(2,1)S(1)} %collective-permute-done.2), channel_id=1, source_target_pairs={{0,2},{1,0},{2,3},{3,1},{4,6},{5,4},{6,7},{7,5},{8,10},{9,8},{10,1... | collective-permute-start | bytes 1179656 | tf_op jit(solution)/shard_map/ppermute | solution.py:104
  16.7 1.6 %collective-permute-start.4 = (bf16[96,1024]{1,0:T(8,128)(2,1)S(1)}, bf16[96,1024]{1,0:T(8,128)(2,1)S(1)}, u32[]{:S(2)}, u32[]{:S(2)}) collective-permute-start(bf16[96,1024]{1,0:T(8,128)(2,1)S(1)} %get-tuple-element.82), channel_id=1, source_target_pairs={{0,16},{1,17},{2,18},{3,19},{4,20},{5,21},{6,22},{7,23},{8,24},{9,... | collective-permute-start | bytes 589832 | tf_op jit(solution)/shard_map/ppermute | solution.py:104
  18.3 1.5 %collective-permute-start.3 = (bf16[96,1024]{1,0:T(8,128)(2,1)S(1)}, bf16[96,1024]{1,0:T(8,128)(2,1)S(1)}, u32[]{:S(2)}, u32[]{:S(2)}) collective-permute-start(bf16[96,1024]{1,0:T(8,128)(2,1)S(1)} %get-tuple-element.83), channel_id=1, source_target_pairs={{0,8},{1,9},{2,10},{3,11},{4,12},{5,13},{6,14},{7,15},{8,0},{9,1},... | collective-permute-start | bytes 589832 | tf_op jit(solution)/shard_map/ppermute | solution.py:104
  19.8 2.6 %collective-permute-done.4 = bf16[96,1024]{1,0:T(8,128)(2,1)S(1)} collective-permute-done((bf16[96,1024]{1,0:T(8,128)(2,1)S(1)}, bf16[96,1024]{1,0:T(8,128)(2,1)S(1)}, u32[]{:S(2)}, u32[]{:S(2)}) %collective-permute-start.4) | collective-permute-done | bytes 196640 | tf_op jit(solution)/shard_map/ppermute | solution.py:104
  22.5 1.5 %collective-permute-done.3 = bf16[96,1024]{1,0:T(8,128)(2,1)S(1)} collective-permute-done((bf16[96,1024]{1,0:T(8,128)(2,1)S(1)}, bf16[96,1024]{1,0:T(8,128)(2,1)S(1)}, u32[]{:S(2)}, u32[]{:S(2)}) %collective-permute-start.3) | collective-permute-done | bytes 196640 | tf_op jit(solution)/shard_map/ppermute | solution.py:104
  24.0 1.2 %collective-permute-done.5 = bf16[192,1024]{1,0:T(8,128)(2,1)S(1)} collective-permute-done((bf16[192,1024]{1,0:T(8,128)(2,1)S(1)}, bf16[192,1024]{1,0:T(8,128)(2,1)S(1)}, u32[]{:S(2)}, u32[]{:S(2)}) %collective-permute-start.5) | collective-permute-done | bytes 393248 | tf_op jit(solution)/shard_map/ppermute | solution.py:104
  25.8 1.5 %collective-permute-start.6 = (bf16[96,1024]{1,0:T(8,128)(2,1)S(1)}, bf16[96,1024]{1,0:T(8,128)(2,1)S(1)}, u32[]{:S(2)}, u32[]{:S(2)}) collective-permute-start(bf16[96,1024]{1,0:T(8,128)(2,1)S(1)} %get-tuple-element.81), channel_id=1, source_target_pairs={{0,8},{1,9},{2,10},{3,11},{4,12},{5,13},{6,14},{7,15},{8,0},{9,1},... | collective-permute-start | bytes 589832 | tf_op jit(solution)/shard_map/ppermute | solution.py:104
  27.5 3.4 %collective-permute-start.14 = (bf16[192,1024]{1,0:T(8,128)(2,1)S(1)}, bf16[192,1024]{1,0:T(8,128)(2,1)S(1)}, u32[]{:S(2)}, u32[]{:S(2)}) collective-permute-start(bf16[192,1024]{1,0:T(8,128)(2,1)S(1)} %collective-permute-done.5), channel_id=1, source_target_pairs={{0,2},{1,0},{2,3},{3,1},{4,6},{5,4},{6,7},{7,5},{8,10},{9,8},{10,1... | collective-permute-start | bytes 1179656 | tf_op jit(solution)/shard_map/ppermute | solution.py:104
  31.9 1.5 %collective-permute-start.13 = (bf16[96,1024]{1,0:T(8,128)(2,1)S(1)}, bf16[96,1024]{1,0:T(8,128)(2,1)S(1)}, u32[]{:S(2)}, u32[]{:S(2)}) collective-permute-start(bf16[96,1024]{1,0:T(8,128)(2,1)S(1)} %get-tuple-element.78), channel_id=1, source_target_pairs={{0,16},{1,17},{2,18},{3,19},{4,20},{5,21},{6,22},{7,23},{8,24},{9,... | collective-permute-start | bytes 589832 | tf_op jit(solution)/shard_map/ppermute | solution.py:104
  34.0 3.4 %collective-permute-start.17 = (bf16[192,1024]{1,0:T(8,128)(2,1)S(1)}, bf16[192,1024]{1,0:T(8,128)(2,1)S(1)}, u32[]{:S(2)}, u32[]{:S(2)}) collective-permute-start(bf16[192,1024]{1,0:T(8,128)(2,1)S(1)} %fusion.2), channel_id=1, source_target_pairs={{0,2},{1,0},{2,3},{3,1},{4,6},{5,4},{6,7},{7,5},{8,10},{9,8},{10,1... | collective-permute-start | bytes 1179656 | tf_op jit(solution)/shard_map/ppermute | solution.py:104
  37.3 2.8 %collective-permute-done.14 = bf16[192,1024]{1,0:T(8,128)(2,1)S(1)} collective-permute-done((bf16[192,1024]{1,0:T(8,128)(2,1)S(1)}, bf16[192,1024]{1,0:T(8,128)(2,1)S(1)}, u32[]{:S(2)}, u32[]{:S(2)}) %collective-permute-start.14) | collective-permute-done | bytes 393248 | tf_op jit(solution)/shard_map/ppermute | solution.py:104
  40.3 2.1 %collective-permute-start.15 = (bf16[96,1024]{1,0:T(8,128)(2,1)S(1)}, bf16[96,1024]{1,0:T(8,128)(2,1)S(1)}, u32[]{:S(2)}, u32[]{:S(2)}) collective-permute-start(bf16[96,1024]{1,0:T(8,128)(2,1)S(1)} %get-tuple-element.77), channel_id=1, source_target_pairs={{0,8},{1,9},{2,10},{3,11},{4,12},{5,13},{6,14},{7,15},{8,0},{9,1},... | collective-permute-start | bytes 589832 | tf_op jit(solution)/shard_map/ppermute | solution.py:104
  42.4 2.9 %collective-permute-done.17 = bf16[192,1024]{1,0:T(8,128)(2,1)S(1)} collective-permute-done((bf16[192,1024]{1,0:T(8,128)(2,1)S(1)}, bf16[192,1024]{1,0:T(8,128)(2,1)S(1)}, u32[]{:S(2)}, u32[]{:S(2)}) %collective-permute-start.17) | collective-permute-done | bytes 393248 | tf_op jit(solution)/shard_map/ppermute | solution.py:104
  45.4 3.4 %collective-permute-start.20 = (bf16[192,1024]{1,0:T(8,128)(2,1)S(1)}, bf16[192,1024]{1,0:T(8,128)(2,1)S(1)}, u32[]{:S(2)}, u32[]{:S(2)}) collective-permute-start(bf16[192,1024]{1,0:T(8,128)(2,1)S(1)} %collective-permute-done.17), channel_id=1, source_target_pairs={{0,2},{1,0},{2,3},{3,1},{4,6},{5,4},{6,7},{7,5},{8,10},{9,8},{10,1... | collective-permute-start | bytes 1179656 | tf_op jit(solution)/shard_map/ppermute | solution.py:104
  50.0 4.6 %collective-permute-done.20 = bf16[192,1024]{1,0:T(8,128)(2,1)S(1)} collective-permute-done((bf16[192,1024]{1,0:T(8,128)(2,1)S(1)}, bf16[192,1024]{1,0:T(8,128)(2,1)S(1)}, u32[]{:S(2)}, u32[]{:S(2)}) %collective-permute-start.20) | collective-permute-done | bytes 393248 | tf_op jit(solution)/shard_map/ppermute | solution.py:104
  54.6 3.4 %collective-permute-start.23 = (bf16[192,1024]{1,0:T(8,128)(2,1)S(1)}, bf16[192,1024]{1,0:T(8,128)(2,1)S(1)}, u32[]{:S(2)}, u32[]{:S(2)}) collective-permute-start(bf16[192,1024]{1,0:T(8,128)(2,1)S(1)} %collective-permute-done.20), channel_id=1, source_target_pairs={{0,2},{1,0},{2,3},{3,1},{4,6},{5,4},{6,7},{7,5},{8,10},{9,8},{10,1... | collective-permute-start | bytes 1179656 | tf_op jit(solution)/shard_map/ppermute | solution.py:104
  59.6 3.7 %collective-permute-done.23 = bf16[192,1024]{1,0:T(8,128)(2,1)S(1)} collective-permute-done((bf16[192,1024]{1,0:T(8,128)(2,1)S(1)}, bf16[192,1024]{1,0:T(8,128)(2,1)S(1)}, u32[]{:S(2)}, u32[]{:S(2)}) %collective-permute-start.23) | collective-permute-done | bytes 393248 | tf_op jit(solution)/shard_map/ppermute | solution.py:104
  65.3 1.2 %broadcast_select_fusion.2 = (bf16[96,1024]{1,0:T(8,128)(2,1)}, bf16[96,1024]{1,0:T(8,128)(2,1)}, bf16[768,1024]{1,0:T(8,128)(2,1)S(1)}, bf16[768,1024]{1,0:T(8,128)(2,1)S(1)}) fusion(bf16[96,1024]{1,0:T(8,128)(2,1)S(1)} %collective-permute-done.21, pred[]{:T(512)S(6)} %eq.5, bf16[192,1024]{1,0:T(8,128)(2,1)S(1)} %collective-permute-done.23, ...), kind=kLoop, calls=%fused_computation.30 | loop fusion | flops 786431 | bytes 2555908 | tf_op jit(solution)/shard_map/jit(_where)/select_n | solution.py:144
  66.5 1.4 %collective-permute-start.25 = (bf16[96,1024]{1,0:T(8,128)(2,1)}, bf16[96,1024]{1,0:T(8,128)(2,1)S(1)}, u32[]{:S(2)}, u32[]{:S(2)}) collective-permute-start(bf16[96,1024]{1,0:T(8,128)(2,1)} %get-tuple-element.70), channel_id=1, source_target_pairs={{0,16},{1,17},{2,18},{3,19},{4,20},{5,21},{6,22},{7,23},{8,24},{9,... | collective-permute-start | bytes 589832 | tf_op jit(solution)/shard_map/ppermute | solution.py:104
  69.5 1.0 %constant_dynamic-update-slice_fusion.1 = bf16[576,1024]{1,0:T(8,128)(2,1)S(1)} fusion(bf16[576,1024]{1,0:T(8,128)(2,1)S(1)} %constant_dynamic-update-slice_fusion.2, bf16[192,1024]{1,0:T(8,128)(2,1)} %copy-done.12), kind=kLoop, calls=%fused_computation.39 | loop fusion | bytes 786432
  70.8 3.1 %shard_map.50.refs_4_ = f32[2048,1024]{1,0:T(8,128)} custom-call(s32[1]{0:T(128)} %bitcast.refs_0_, bf16[768,1024]{1,0:T(8,128)(2,1)S(1)} %get-tuple-element.88.refs_1_, bf16[192,1024]{1,0:T(8,128)(2,1)S(1)} %copy-done, bf16[576,1024]{1,0:T(8,128)(2,1)S(1)} %constant_dynamic-update-slice_fusion.refs_3_), custom_call_target="tpu_custom_call" | custom-call | flops 1610612736 | bytes 7340032 | tf_op jit(solution)/shard_map/pallas_call | solution.py:49
  74.1 1.0 %collective-permute-done.24 = bf16[96,1024]{1,0:T(8,128)(2,1)S(1)} collective-permute-done((bf16[96,1024]{1,0:T(8,128)(2,1)}, bf16[96,1024]{1,0:T(8,128)(2,1)S(1)}, u32[]{:S(2)}, u32[]{:S(2)}) %collective-permute-start.24) | collective-permute-done | bytes 196640 | tf_op jit(solution)/shard_map/ppermute | solution.py:104
  77.2 4.5 %shard_map.51 = f32[2048,1024]{1,0:T(8,128)} custom-call(s32[1]{0:T(128)S(6)} %sub.7.refs_0_, bf16[768,1024]{1,0:T(8,128)(2,1)} %collective-permute-done.26.refs_1_, bf16[192,1024]{1,0:T(8,128)(2,1)S(1)} %copy-done, bf16[576,1024]{1,0:T(8,128)(2,1)S(1)} %constant_dynamic-update-slice_fusion.refs_3_, ...), custom_call_target="tpu_custom_call", output_to_operand_aliasing={{}: (4, {})} | custom-call | flops 1610612736 | bytes 7340032 | tf_op jit(solution)/shard_map/pallas_call | solution.py:49
  82.8 3.0 %shard_map.52.refs_3_ = f32[2048,1024]{1,0:T(8,128)} custom-call(s32[1]{0:T(128)} %bitcast.refs_0_, bf16[768,1024]{1,0:T(8,128)(2,1)S(1)} %select_dynamic-update-slice_fusion.refs_1_, bf16[768,1024]{1,0:T(8,128)(2,1)S(1)} %pad_maximum_fusion.refs_2_), custom_call_target="tpu_custom_call" | custom-call | flops 1610612736 | bytes 7340032 | tf_op jit(solution)/shard_map/pallas_call | solution.py:49
  86.2 3.0 %shard_map.53 = f32[2048,1024]{1,0:T(8,128)} custom-call(s32[1]{0:T(128)S(6)} %sub.7.refs_0_, bf16[768,1024]{1,0:T(8,128)(2,1)S(1)} %collective-permute-done.29.refs_1_, bf16[768,1024]{1,0:T(8,128)(2,1)S(1)} %pad_maximum_fusion.refs_2_, f32[2048,1024]{1,0:T(8,128)} %shard_map.52.refs_3_), custom_call_target="tpu_custom_call", output_to_operand_aliasing={{}: (3, {})} | custom-call | flops 1610612736 | bytes 7340032 | tf_op jit(solution)/shard_map/pallas_call | solution.py:49
  (114 shorter events, 14.4 us)
Async XLA Ops:
  0.6 14.1 %collective-permute-start.2 = (bf16[192,1024]{1,0:T(8,128)(2,1)}, bf16[192,1024]{1,0:T(8,128)(2,1)S(1)}, u32[]{:S(2)}, u32[]{:S(2)}) collective-permute-start(bf16[192,1024]{1,0:T(8,128)(2,1)} %refs_2_.3), channel_id=1, source_target_pairs={{0,2},{1,0},{2,3},{3,1},{4,6},{5,4},{6,7},{7,5},{8,10},{9,8},{10,1... | collective-permute-start | bytes 1179656 | tf_op jit(solution)/shard_map/ppermute | solution.py:104
  5.8 7.4 %collective-permute-start.1 = (bf16[96,1024]{1,0:T(8,128)(2,1)S(1)}, bf16[96,1024]{1,0:T(8,128)(2,1)S(1)}, u32[]{:S(2)}, u32[]{:S(2)}) collective-permute-start(bf16[96,1024]{1,0:T(8,128)(2,1)S(1)} %get-tuple-element.84), channel_id=1, source_target_pairs={{0,16},{1,17},{2,18},{3,19},{4,20},{5,21},{6,22},{7,23},{8,24},{9,... | collective-permute-start | bytes 589832 | tf_op jit(solution)/shard_map/ppermute | solution.py:104
  7.4 7.3 %collective-permute-start = (bf16[96,1024]{1,0:T(8,128)(2,1)S(1)}, bf16[96,1024]{1,0:T(8,128)(2,1)S(1)}, u32[]{:S(2)}, u32[]{:S(2)}) collective-permute-start(bf16[96,1024]{1,0:T(8,128)(2,1)S(1)} %get-tuple-element.85), channel_id=1, source_target_pairs={{0,8},{1,9},{2,10},{3,11},{4,12},{5,13},{6,14},{7,15},{8,0},{9,1},... | collective-permute-start | bytes 589832 | tf_op jit(solution)/shard_map/ppermute | solution.py:104
  10.0 1.2 %collective-permute-start.8 = (f32[192,1]{0,1:T(1,128)S(1)}, f32[192,1]{0,1:T(1,128)S(1)}, u32[]{:S(2)}, u32[]{:S(2)}) collective-permute-start(f32[192,1]{0,1:T(1,128)S(1)} %bitcast.5), channel_id=1, source_target_pairs={{0,4},{1,5},{2,6},{3,7},{4,0},{5,1},{6,2},{7,3},{8,12},{9,13},{10,... | collective-permute-start | bytes 2312 | tf_op jit(solution)/shard_map/ppermute | solution.py:104
  11.2 7.1 %collective-permute-start.11 = (f32[192,1]{0,1:T(1,128)S(1)}, f32[192,1]{0,1:T(1,128)S(1)}, u32[]{:S(2)}, u32[]{:S(2)}) collective-permute-start(f32[192,1]{0,1:T(1,128)S(1)} %add.24), channel_id=1, source_target_pairs={{0,24},{1,25},{2,26},{3,27},{4,28},{5,29},{6,30},{7,31},{8,16},{9,... | collective-permute-start | bytes 2312 | tf_op jit(solution)/shard_map/ppermute | solution.py:104
  11.7 8.1 %collective-permute-start.10 = (f32[192,1]{0,1:T(1,128)S(1)}, f32[192,1]{0,1:T(1,128)S(1)}, u32[]{:S(2)}, u32[]{:S(2)}) collective-permute-start(f32[192,1]{0,1:T(1,128)S(1)} %add.24), channel_id=1, source_target_pairs={{0,16},{1,17},{2,18},{3,19},{4,20},{5,21},{6,22},{7,23},{8,24},{9,... | collective-permute-start | bytes 2312 | tf_op jit(solution)/shard_map/ppermute | solution.py:104
  13.2 6.6 %collective-permute-start.9 = (f32[192,1]{0,1:T(1,128)S(1)}, f32[192,1]{0,1:T(1,128)S(1)}, u32[]{:S(2)}, u32[]{:S(2)}) collective-permute-start(f32[192,1]{0,1:T(1,128)S(1)} %add.24), channel_id=1, source_target_pairs={{0,8},{1,9},{2,10},{3,11},{4,12},{5,13},{6,14},{7,15},{8,0},{9,1},... | collective-permute-start | bytes 2312 | tf_op jit(solution)/shard_map/ppermute | solution.py:104
  14.7 50.0 %copy-start.11 = (bf16[192,1024]{1,0:T(8,128)(2,1)}, bf16[192,1024]{1,0:T(8,128)(2,1)S(1)}, u32[]{:S(2)}) copy-start(bf16[192,1024]{1,0:T(8,128)(2,1)S(1)} %collective-permute-done.2) | copy-start | bytes 1179652
  14.7 10.4 %collective-permute-start.5 = (bf16[192,1024]{1,0:T(8,128)(2,1)S(1)}, bf16[192,1024]{1,0:T(8,128)(2,1)S(1)}, u32[]{:S(2)}, u32[]{:S(2)}) collective-permute-start(bf16[192,1024]{1,0:T(8,128)(2,1)S(1)} %collective-permute-done.2), channel_id=1, source_target_pairs={{0,2},{1,0},{2,3},{3,1},{4,6},{5,4},{6,7},{7,5},{8,10},{9,8},{10,1... | collective-permute-start | bytes 1179656 | tf_op jit(solution)/shard_map/ppermute | solution.py:104
  16.7 5.7 %collective-permute-start.4 = (bf16[96,1024]{1,0:T(8,128)(2,1)S(1)}, bf16[96,1024]{1,0:T(8,128)(2,1)S(1)}, u32[]{:S(2)}, u32[]{:S(2)}) collective-permute-start(bf16[96,1024]{1,0:T(8,128)(2,1)S(1)} %get-tuple-element.82), channel_id=1, source_target_pairs={{0,16},{1,17},{2,18},{3,19},{4,20},{5,21},{6,22},{7,23},{8,24},{9,... | collective-permute-start | bytes 589832 | tf_op jit(solution)/shard_map/ppermute | solution.py:104
  18.3 5.7 %collective-permute-start.3 = (bf16[96,1024]{1,0:T(8,128)(2,1)S(1)}, bf16[96,1024]{1,0:T(8,128)(2,1)S(1)}, u32[]{:S(2)}, u32[]{:S(2)}) collective-permute-start(bf16[96,1024]{1,0:T(8,128)(2,1)S(1)} %get-tuple-element.83), channel_id=1, source_target_pairs={{0,8},{1,9},{2,10},{3,11},{4,12},{5,13},{6,14},{7,15},{8,0},{9,1},... | collective-permute-start | bytes 589832 | tf_op jit(solution)/shard_map/ppermute | solution.py:104
  25.1 39.8 %copy-start.12 = (bf16[192,1024]{1,0:T(8,128)(2,1)}, bf16[192,1024]{1,0:T(8,128)(2,1)S(1)}, u32[]{:S(2)}) copy-start(bf16[192,1024]{1,0:T(8,128)(2,1)S(1)} %collective-permute-done.5) | copy-start | bytes 1179652
  25.2 5.7 %collective-permute-start.7 = (bf16[96,1024]{1,0:T(8,128)(2,1)S(1)}, bf16[96,1024]{1,0:T(8,128)(2,1)S(1)}, u32[]{:S(2)}, u32[]{:S(2)}) collective-permute-start(bf16[96,1024]{1,0:T(8,128)(2,1)S(1)} %get-tuple-element.80), channel_id=1, source_target_pairs={{0,16},{1,17},{2,18},{3,19},{4,20},{5,21},{6,22},{7,23},{8,24},{9,... | collective-permute-start | bytes 589832 | tf_op jit(solution)/shard_map/ppermute | solution.py:104
  25.8 5.7 %collective-permute-start.6 = (bf16[96,1024]{1,0:T(8,128)(2,1)S(1)}, bf16[96,1024]{1,0:T(8,128)(2,1)S(1)}, u32[]{:S(2)}, u32[]{:S(2)}) collective-permute-start(bf16[96,1024]{1,0:T(8,128)(2,1)S(1)} %get-tuple-element.81), channel_id=1, source_target_pairs={{0,8},{1,9},{2,10},{3,11},{4,12},{5,13},{6,14},{7,15},{8,0},{9,1},... | collective-permute-start | bytes 589832 | tf_op jit(solution)/shard_map/ppermute | solution.py:104
  27.5 12.7 %collective-permute-start.14 = (bf16[192,1024]{1,0:T(8,128)(2,1)S(1)}, bf16[192,1024]{1,0:T(8,128)(2,1)S(1)}, u32[]{:S(2)}, u32[]{:S(2)}) collective-permute-start(bf16[192,1024]{1,0:T(8,128)(2,1)S(1)} %collective-permute-done.5), channel_id=1, source_target_pairs={{0,2},{1,0},{2,3},{3,1},{4,6},{5,4},{6,7},{7,5},{8,10},{9,8},{10,1... | collective-permute-start | bytes 1179656 | tf_op jit(solution)/shard_map/ppermute | solution.py:104
  31.9 8.3 %collective-permute-start.13 = (bf16[96,1024]{1,0:T(8,128)(2,1)S(1)}, bf16[96,1024]{1,0:T(8,128)(2,1)S(1)}, u32[]{:S(2)}, u32[]{:S(2)}) collective-permute-start(bf16[96,1024]{1,0:T(8,128)(2,1)S(1)} %get-tuple-element.78), channel_id=1, source_target_pairs={{0,16},{1,17},{2,18},{3,19},{4,20},{5,21},{6,22},{7,23},{8,24},{9,... | collective-permute-start | bytes 589832 | tf_op jit(solution)/shard_map/ppermute | solution.py:104
  33.4 6.8 %collective-permute-start.12 = (bf16[96,1024]{1,0:T(8,128)(2,1)S(1)}, bf16[96,1024]{1,0:T(8,128)(2,1)S(1)}, u32[]{:S(2)}, u32[]{:S(2)}) collective-permute-start(bf16[96,1024]{1,0:T(8,128)(2,1)S(1)} %get-tuple-element.79), channel_id=1, source_target_pairs={{0,8},{1,9},{2,10},{3,11},{4,12},{5,13},{6,14},{7,15},{8,0},{9,1},... | collective-permute-start | bytes 589832 | tf_op jit(solution)/shard_map/ppermute | solution.py:104
  34.0 11.4 %collective-permute-start.17 = (bf16[192,1024]{1,0:T(8,128)(2,1)S(1)}, bf16[192,1024]{1,0:T(8,128)(2,1)S(1)}, u32[]{:S(2)}, u32[]{:S(2)}) collective-permute-start(bf16[192,1024]{1,0:T(8,128)(2,1)S(1)} %fusion.2), channel_id=1, source_target_pairs={{0,2},{1,0},{2,3},{3,1},{4,6},{5,4},{6,7},{7,5},{8,10},{9,8},{10,1... | collective-permute-start | bytes 1179656 | tf_op jit(solution)/shard_map/ppermute | solution.py:104
  40.2 8.5 %collective-permute-start.16 = (bf16[96,1024]{1,0:T(8,128)(2,1)S(1)}, bf16[96,1024]{1,0:T(8,128)(2,1)S(1)}, u32[]{:S(2)}, u32[]{:S(2)}) collective-permute-start(bf16[96,1024]{1,0:T(8,128)(2,1)S(1)} %get-tuple-element.76), channel_id=1, source_target_pairs={{0,16},{1,17},{2,18},{3,19},{4,20},{5,21},{6,22},{7,23},{8,24},{9,... | collective-permute-start | bytes 589832 | tf_op jit(solution)/shard_map/ppermute | solution.py:104
  40.3 8.4 %collective-permute-start.15 = (bf16[96,1024]{1,0:T(8,128)(2,1)S(1)}, bf16[96,1024]{1,0:T(8,128)(2,1)S(1)}, u32[]{:S(2)}, u32[]{:S(2)}) collective-permute-start(bf16[96,1024]{1,0:T(8,128)(2,1)S(1)} %get-tuple-element.77), channel_id=1, source_target_pairs={{0,8},{1,9},{2,10},{3,11},{4,12},{5,13},{6,14},{7,15},{8,0},{9,1},... | collective-permute-start | bytes 589832 | tf_op jit(solution)/shard_map/ppermute | solution.py:104
  45.4 9.3 %collective-permute-start.20 = (bf16[192,1024]{1,0:T(8,128)(2,1)S(1)}, bf16[192,1024]{1,0:T(8,128)(2,1)S(1)}, u32[]{:S(2)}, u32[]{:S(2)}) collective-permute-start(bf16[192,1024]{1,0:T(8,128)(2,1)S(1)} %collective-permute-done.17), channel_id=1, source_target_pairs={{0,2},{1,0},{2,3},{3,1},{4,6},{5,4},{6,7},{7,5},{8,10},{9,8},{10,1... | collective-permute-start | bytes 1179656 | tf_op jit(solution)/shard_map/ppermute | solution.py:104
  48.8 9.2 %collective-permute-start.19 = (bf16[96,1024]{1,0:T(8,128)(2,1)S(1)}, bf16[96,1024]{1,0:T(8,128)(2,1)S(1)}, u32[]{:S(2)}, u32[]{:S(2)}) collective-permute-start(bf16[96,1024]{1,0:T(8,128)(2,1)S(1)} %get-tuple-element.74), channel_id=1, source_target_pairs={{0,16},{1,17},{2,18},{3,19},{4,20},{5,21},{6,22},{7,23},{8,24},{9,... | collective-permute-start | bytes 589832 | tf_op jit(solution)/shard_map/ppermute | solution.py:104
  49.4 8.7 %collective-permute-start.18 = (bf16[96,1024]{1,0:T(8,128)(2,1)S(1)}, bf16[96,1024]{1,0:T(8,128)(2,1)S(1)}, u32[]{:S(2)}, u32[]{:S(2)}) collective-permute-start(bf16[96,1024]{1,0:T(8,128)(2,1)S(1)} %get-tuple-element.75), channel_id=1, source_target_pairs={{0,8},{1,9},{2,10},{3,11},{4,12},{5,13},{6,14},{7,15},{8,0},{9,1},... | collective-permute-start | bytes 589832 | tf_op jit(solution)/shard_map/ppermute | solution.py:104
  54.6 8.7 %collective-permute-start.23 = (bf16[192,1024]{1,0:T(8,128)(2,1)S(1)}, bf16[192,1024]{1,0:T(8,128)(2,1)S(1)}, u32[]{:S(2)}, u32[]{:S(2)}) collective-permute-start(bf16[192,1024]{1,0:T(8,128)(2,1)S(1)} %collective-permute-done.20), channel_id=1, source_target_pairs={{0,2},{1,0},{2,3},{3,1},{4,6},{5,4},{6,7},{7,5},{8,10},{9,8},{10,1... | collective-permute-start | bytes 1179656 | tf_op jit(solution)/shard_map/ppermute | solution.py:104
  58.1 5.7 %collective-permute-start.22 = (bf16[96,1024]{1,0:T(8,128)(2,1)S(1)}, bf16[96,1024]{1,0:T(8,128)(2,1)S(1)}, u32[]{:S(2)}, u32[]{:S(2)}) collective-permute-start(bf16[96,1024]{1,0:T(8,128)(2,1)S(1)} %get-tuple-element.72), channel_id=1, source_target_pairs={{0,16},{1,17},{2,18},{3,19},{4,20},{5,21},{6,22},{7,23},{8,24},{9,... | collective-permute-start | bytes 589832 | tf_op jit(solution)/shard_map/ppermute | solution.py:104
  58.9 5.7 %collective-permute-start.21 = (bf16[96,1024]{1,0:T(8,128)(2,1)S(1)}, bf16[96,1024]{1,0:T(8,128)(2,1)S(1)}, u32[]{:S(2)}, u32[]{:S(2)}) collective-permute-start(bf16[96,1024]{1,0:T(8,128)(2,1)S(1)} %get-tuple-element.73), channel_id=1, source_target_pairs={{0,8},{1,9},{2,10},{3,11},{4,12},{5,13},{6,14},{7,15},{8,0},{9,1},... | collective-permute-start | bytes 589832 | tf_op jit(solution)/shard_map/ppermute | solution.py:104
  66.5 8.6 %collective-permute-start.26 = (bf16[768,1024]{1,0:T(8,128)(2,1)S(1)}, bf16[768,1024]{1,0:T(8,128)(2,1)}, u32[]{:S(2)}, u32[]{:S(2)}) collective-permute-start(bf16[768,1024]{1,0:T(8,128)(2,1)S(1)} %get-tuple-element.88.refs_1_), channel_id=1, source_target_pairs={{0,4},{1,5},{2,6},{3,7},{4,0},{5,1},{6,2},{7,3},{8,12},{9,13},{10,... | collective-permute-start | bytes 4718600 | tf_op jit(solution)/shard_map/ppermute | solution.py:104
  66.5 7.6 %collective-permute-start.25 = (bf16[96,1024]{1,0:T(8,128)(2,1)}, bf16[96,1024]{1,0:T(8,128)(2,1)S(1)}, u32[]{:S(2)}, u32[]{:S(2)}) collective-permute-start(bf16[96,1024]{1,0:T(8,128)(2,1)} %get-tuple-element.70), channel_id=1, source_target_pairs={{0,16},{1,17},{2,18},{3,19},{4,20},{5,21},{6,22},{7,23},{8,24},{9,... | collective-permute-start | bytes 589832 | tf_op jit(solution)/shard_map/ppermute | solution.py:104
  67.9 7.2 %collective-permute-start.24 = (bf16[96,1024]{1,0:T(8,128)(2,1)}, bf16[96,1024]{1,0:T(8,128)(2,1)S(1)}, u32[]{:S(2)}, u32[]{:S(2)}) collective-permute-start(bf16[96,1024]{1,0:T(8,128)(2,1)} %get-tuple-element.71), channel_id=1, source_target_pairs={{0,8},{1,9},{2,10},{3,11},{4,12},{5,13},{6,14},{7,15},{8,0},{9,1},... | collective-permute-start | bytes 589832 | tf_op jit(solution)/shard_map/ppermute | solution.py:104
  75.6 6.3 %collective-permute-start.28 = (bf16[96,1024]{1,0:T(8,128)(2,1)S(1)}, bf16[96,1024]{1,0:T(8,128)(2,1)S(1)}, u32[]{:S(2)}, u32[]{:S(2)}) collective-permute-start(bf16[96,1024]{1,0:T(8,128)(2,1)S(1)} %get-tuple-element.66), channel_id=1, source_target_pairs={{0,16},{1,17},{2,18},{3,19},{4,20},{5,21},{6,22},{7,23},{8,24},{9,... | collective-permute-start | bytes 589832 | tf_op jit(solution)/shard_map/ppermute | solution.py:104
  76.4 5.9 %collective-permute-start.27 = (bf16[96,1024]{1,0:T(8,128)(2,1)S(1)}, bf16[96,1024]{1,0:T(8,128)(2,1)S(1)}, u32[]{:S(2)}, u32[]{:S(2)}) collective-permute-start(bf16[96,1024]{1,0:T(8,128)(2,1)S(1)} %get-tuple-element.67), channel_id=1, source_target_pairs={{0,8},{1,9},{2,10},{3,11},{4,12},{5,13},{6,14},{7,15},{8,0},{9,1},... | collective-permute-start | bytes 589832 | tf_op jit(solution)/shard_map/ppermute | solution.py:104
  82.7 3.5 %collective-permute-start.29 = (bf16[768,1024]{1,0:T(8,128)(2,1)S(1)}, bf16[768,1024]{1,0:T(8,128)(2,1)S(1)}, u32[]{:S(2)}, u32[]{:S(2)}) collective-permute-start(bf16[768,1024]{1,0:T(8,128)(2,1)S(1)} %select_dynamic-update-slice_fusion.refs_1_), channel_id=1, source_target_pairs={{0,4},{1,5},{2,6},{3,7},{4,0},{5,1},{6,2},{7,3},{8,12},{9,13},{10,... | collective-permute-start | bytes 4718600 | tf_op jit(solution)/shard_map/ppermute | solution.py:104
  (24 other events, 239.7 us)
